TPU v7x, 32 devices: a whole 2x2x4 slice. The times are simulated.
32 devices in a mesh: rows: 8 (over z, y), quant: 4 (over x, core).
Axes of the slice: x: 2, y: 2, z: 4, core: 2. Of those that a mesh axis runs over, the one named last changes fastest.
Arguments:
- observed_inputs: bfloat16 [32768, 376], P(('rows', 'quant')), may hold values from -6 to 6
- chosen_controls: bfloat16 [32768, 17], P(('rows', 'quant')), may hold values from -0.94921875 to 0.94921875
- present_gauss_draw: float32 [32768, 17], P(('rows', 'quant')), may hold values from -5 to 5
- successor_observations: bfloat16 [32768, 376], P('rows'), may hold values from -6 to 6
- successor_gauss_draw: float32 [32768, 17], P('rows'), may hold values from -5 to 5
- payoffs: float32 [32768], P('rows'), may hold values from -4 to 4
- terminal_indicator: int32 [32768], P('rows'), may hold values 0 or 1
- merged_support_order: int32 [32768, 125], P('rows'), may hold values from 0 to 124, each once within a row
- entry_layer_cast: bfloat16 [393, 2560], replicated, may hold values from -0.3125 to 0.3125
- inner_layer_cast: bfloat16 [512, 2560], replicated, may hold values from -0.25 to 0.25
- critic_inner_offsets: float32 [2, 2560], replicated, may hold values from -1.5 to 1.5
- readout_matrix_cast: bfloat16 [512, 128], P(None, 'quant'), may hold values from -0.25 to 0.25
- lagged_entry_layer: bfloat16 [393, 2560], replicated, may hold values from -0.3125 to 0.3125
- lagged_inner_layer: bfloat16 [512, 2560], replicated, may hold values from -0.25 to 0.25
- lagged_inner_offsets: float32 [2, 2560], replicated, may hold values from -1.5 to 1.5
- lagged_readout: bfloat16 [512, 128], P(None, 'quant'), may hold values from -0.25 to 0.25
- lagged_readout_offsets: float32 [128], replicated, may hold values from -1.5 to 1.5
- pilot_weights_cast: bfloat16 [666, 256], replicated, may hold values from -0.375 to 0.375
- update_counter: int32 [1], replicated, may hold values from 2 to 20
- entry_layer_main: float32 [393, 2560], P(None, ('rows', 'quant')), may hold values from -0.3125 to 0.3125
- entry_layer_moment_one: float32 [393, 2560], P(None, ('rows', 'quant')), may hold values from -2.3841858e-06 to 2.3841858e-06
- entry_layer_moment_two: float32 [393, 2560], P(None, ('rows', 'quant')), may hold values from 2.2e-15 to 9e-15
- inner_layer_main: float32 [512, 2560], P(None, ('rows', 'quant')), may hold values from -0.25 to 0.25
- inner_layer_moment_one: float32 [512, 2560], P(None, ('rows', 'quant')), may hold values from -7.6293945e-06 to 7.6293945e-06
- inner_layer_moment_two: float32 [512, 2560], P(None, ('rows', 'quant')), may hold values from 2e-14 to 8e-14
- offset_vector_main: float32 [2, 2560], P(None, ('rows', 'quant')), may hold values from -1.5 to 1.5
- offset_moment_one: float32 [2, 2560], P(None, ('rows', 'quant')), may hold values from -1.5258789e-05 to 1.5258789e-05
- offset_moment_two: float32 [2, 2560], P(None, ('rows', 'quant')), may hold values from 8e-14 to 3.2e-13
- readout_matrix_main: float32 [512, 128], P('rows', 'quant'), may hold values from -0.25 to 0.25
- readout_moment_one: float32 [512, 128], P('rows', 'quant'), may hold values from -0.00061035156 to 0.00061035156
- readout_moment_two: float32 [512, 128], P('rows', 'quant'), may hold values from 1.6e-10 to 6.4e-10
- pilot_weights_main: float32 [666, 256], replicated, may hold values from -0.375 to 0.375
- pilot_moment_one: float32 [666, 256], replicated, may hold values from -0.0078125 to 0.0078125
- pilot_moment_two: float32 [666, 256], replicated, may hold values from 2.5e-08 to 1e-07
- vector_params_main: float32 [674], replicated, may hold values from -1.5 to 1.5
- vector_moment_one: float32 [674], replicated, may hold values from -1 to 1, as said below
- vector_moment_two: float32 [674], replicated, may hold values from 0 to 1, as said below
- heat_logarithm_main: float32 [1], replicated, may hold values from -4 to -3
- heat_moment_one: float32 [1], replicated, may hold values from 1.5 to 5
- heat_moment_two: float32 [1], replicated, may hold values from 1 to 4
Outputs:
- objective_scalar: float32 [], replicated
- in_new: float32 [393, 2560], P(None, ('rows', 'quant'))
- in_first_new: float32 [393, 2560], P(None, ('rows', 'quant'))
- in_second_new: float32 [393, 2560], P(None, ('rows', 'quant'))
- mid_new: float32 [512, 2560], P(None, ('rows', 'quant'))
- mid_first_new: float32 [512, 2560], P(None, ('rows', 'quant'))
- mid_second_new: float32 [512, 2560], P(None, ('rows', 'quant'))
- bias_new: float32 [2, 2560], P(None, ('rows', 'quant'))
- bias_first_new: float32 [2, 2560], P(None, ('rows', 'quant'))
- bias_second_new: float32 [2, 2560], P(None, ('rows', 'quant'))
- head_new: float32 [512, 128], P('rows', 'quant')
- head_first_new: float32 [512, 128], P('rows', 'quant')
- head_second_new: float32 [512, 128], P('rows', 'quant')
- actor_new: float32 [666, 256], replicated
- actor_first_new: float32 [666, 256], replicated
- actor_second_new: float32 [666, 256], replicated
- small_new: float32 [674], replicated
- small_first_new: float32 [674], replicated
- small_second_new: float32 [674], replicated
- alpha_new: float32 [1], replicated
- alpha_first_new: float32 [1], replicated
- alpha_second_new: float32 [1], replicated
Inputs may be any that keep to these rules, and one draw needn't show every extreme that they name: `vector_moment_one`: entries of both signs. `vector_moment_two`: positive entries.
All inputs are finite; a program needn't handle non-finite values. No bound on the sum of `terminal_indicator` on one device may be relied on, other than what follows from the above.
Results may differ from a plain program's by a relative error of at most 0.017.
Values may be sent and summed in bfloat16 or wider, within the bound.
No kernel may reach another device: no remote copies, remote signals or barrier semaphores. Data moves between devices by JAX's collectives and lax.ppermute only.
A program may use at most 512 MiB of HBM per device.

v0:
```python
import functools
import math

import jax
import jax.numpy as jnp
import ml_dtypes
import numpy as np
from jax import lax
from jax.experimental import pallas as pl
from jax.experimental.pallas import tpu as pltpu
from jax.sharding import PartitionSpec as P

OBS_DIM = 376
ACT_DIM = 17
HIDDEN_SIZE = 512
ACTOR_HIDDEN = 256
CRITICS = 5
QUANTS = 25
SLOT = 32
PADDED = 128
MERGED_SUPPORTS = 125
KEPT_ATOMS = 115
INPUTS = 393
FEATURES = 2560
SMALL_VEC = 674
LANES = 1024
EXTRA = 128
TILE = 512
MiB = 1024 * 1024

DISCOUNT = 0.99
BETA_FIRST = 0.9
BETA_SECOND = 0.999
EPSILON = 1e-08
WEIGHT_DECAY = 0.01
RATE_MATRIX = 0.05
RATE_VECTOR = 0.3
STEP_SIZE_SCALE = 0.5
LOG_TWO = math.log(2.0)
HALF_LOG_CIRCLE = 0.5 * math.log(2.0 * math.pi)
AXES = ("rows", "quant")
BF = jnp.bfloat16
F32 = jnp.float32
WHOLE = pl.BlockSpec(memory_space=pltpu.VMEM)
SCALAR = pl.BlockSpec(memory_space=pltpu.SMEM)
UNREAD = pl.BlockSpec(memory_space=pl.ANY)


def dot_nn(left, right):
    return jnp.dot(left, right, preferred_element_type=F32)


def dot_tn(left, right):
    return lax.dot_general(left, right, (((0,), (0,)), ((), ())), preferred_element_type=F32)


def dot_nt(left, right):
    return lax.dot_general(left, right, (((1,), (1,)), ((), ())), preferred_element_type=F32)


def params(limit=32, steps=0):
    semantics = ("arbitrary",) * steps if steps else None
    return pltpu.CompilerParams(vmem_limit_bytes=limit * MiB, dimension_semantics=semantics)


def cost(flops, moved):
    return pl.CostEstimate(flops=int(flops), bytes_accessed=int(moved), transcendentals=0)


def column(row):
    return jnp.transpose(jnp.broadcast_to(row, (8, row.shape[1])))[:, :1]


def fill_inputs(tall, inputs, obs, act):
    rows = obs.shape[1]
    body = OBS_DIM // 16 * 16
    inputs[:body] = obs[:body]
    tall[:8] = obs[body:OBS_DIM].astype(F32)
    tall[8 : 8 + ACT_DIM] = act.astype(F32)
    tall[8 + ACT_DIM : 32] = jnp.zeros((24 - ACT_DIM, rows), F32)
    tall[8 + ACT_DIM : 11 + ACT_DIM] = jnp.ones((3, rows), F32)
    inputs[body : body + 32] = tall[...].astype(BF)
    inputs[body + 32 :] = jnp.zeros((HIDDEN_SIZE - body - 32, rows), BF)


def actor_layers(inputs, draw, actor, small, out_scratch):
    s_one = column(small[:, :ACTOR_HIDDEN])
    s_two = column(small[:, ACTOR_HIDDEN : 2 * ACTOR_HIDDEN])
    s_three = column(small[:, 2 * ACTOR_HIDDEN : 2 * ACTOR_HIDDEN + PADDED])[: 2 * ACT_DIM]
    g_one = jnp.maximum(dot_tn(actor[:OBS_DIM], inputs) + s_one, 0.0).astype(BF)
    g_two = jnp.maximum(dot_tn(actor[OBS_DIM : OBS_DIM + ACTOR_HIDDEN], g_one) + s_two, 0.0).astype(BF)
    out_scratch[: 2 * ACT_DIM] = dot_nn(actor[OBS_DIM + ACTOR_HIDDEN :], g_two) + s_three
    mean = out_scratch[:ACT_DIM]
    log_std = out_scratch[ACT_DIM : 2 * ACT_DIM]
    scaled = jnp.exp(log_std) * draw
    pre = mean + scaled
    act = jnp.tanh(pre)
    soft = jnp.maximum(-2.0 * pre, 0.0) + jnp.log(1.0 + jnp.exp(-2.0 * jnp.abs(pre)))
    logp = jnp.sum(
        -0.5 * draw * draw - log_std - HALF_LOG_CIRCLE - 2.0 * (LOG_TWO - pre - soft),
        axis=0,
        keepdims=True,
    )
    return g_one, g_two, scaled, act, logp


def heads_kernel(me, own, got_one, got_two, got_three, small, lag_bias, out, bias_out, stage, col):
    quarter = own.shape[0]
    for k, got in enumerate((own, got_one, got_two, got_three)):
        first = pl.multiple_of((me[0] ^ k) * quarter, quarter)
        stage[pl.ds(first, quarter)] = got[...].astype(F32)
    keep = lax.broadcasted_iota(jnp.int32, (SLOT, 1), 0) < QUANTS
    bias = small[:, SMALL_VEC - PADDED :]
    both = jnp.concatenate([bias, lag_bias[...], jnp.zeros((6, PADDED), F32)], 0)
    col[:PADDED] = jnp.transpose(both)
    for e in range(CRITICS):
        rows = pl.ds(e * QUANTS, SLOT)
        out[e] = jnp.where(keep, stage[rows], 0.0).astype(BF)
        columns = jnp.where(keep, col[rows], 0.0)
        for net in range(2):
            bias_out[net, e] = jnp.broadcast_to(columns[:, net : net + 1], (SLOT, PADDED))


def heads(me, own, got, small, lag_bias):
    return pl.pallas_call(
        heads_kernel,
        in_specs=[SCALAR] + [WHOLE] * 6,
        out_specs=[WHOLE, WHOLE],
        out_shape=[
            jax.ShapeDtypeStruct((CRITICS, SLOT, 2 * HIDDEN_SIZE), BF),
            jax.ShapeDtypeStruct((2, CRITICS, SLOT, PADDED), F32),
        ],
        scratch_shapes=[pltpu.VMEM((136, 2 * HIDDEN_SIZE), F32), pltpu.VMEM((136, 8), F32)],
        compiler_params=params(),
        cost_estimate=cost(3e10, 1e6),
        name="heads",
    )(me, own, *got, small, lag_bias)


def fill_first(tall, filled, first, bias):
    body = INPUTS // 16 * 16
    high = bias.astype(BF).astype(F32)
    middle = (bias - high).astype(BF).astype(F32)
    filled[:body] = first[:body]
    tall[: INPUTS - body] = first[body:].astype(F32)
    tall[INPUTS - body : 32] = jnp.zeros((32 - INPUTS + body, HIDDEN_SIZE), F32)
    tall[INPUTS - body : INPUTS - body + 1] = high
    tall[INPUTS - body + 1 : INPUTS - body + 2] = middle
    tall[INPUTS - body + 2 : INPUTS - body + 3] = bias - high - middle
    filled[body : body + 32] = tall[...].astype(BF)
    filled[body + 32 :] = jnp.zeros((HIDDEN_SIZE - body - 32, HIDDEN_SIZE), BF)


def tiles(rows):
    width = min(rows, TILE)
    return [pl.ds(i * width, width) for i in range(rows // width)]


def critic_lanes(e):
    return pl.ds(pl.multiple_of(e * HIDDEN_SIZE, HIDDEN_SIZE), HIDDEN_SIZE)


def target_kernel(
    index, heat, inputs, logp, payoffs, done, order_in, first, second, bias, head, head_bias, after,
    lagged, keep, filled, tall_w, slots, packed, order, sems,
):
    rows = inputs.shape[1]
    mine = pl.ds(pl.multiple_of(index[0] * rows, PADDED), rows)
    copy = pltpu.make_async_copy(order_in.at[mine], order, sems.at[0])
    copy.start()
    def one_critic(e, carry):
        lanes = critic_lanes(e)
        fill_first(tall_w, filled, first[:, lanes], bias[:1, lanes])
        b_two = column(bias[1:2, lanes])
        w_two = second[:, lanes]
        for part in tiles(rows):
            h_one = jnp.maximum(dot_tn(filled[...], inputs[:, part]), 0.0).astype(BF)
            h_two = jnp.maximum(dot_tn(w_two, h_one) + b_two, 0.0).astype(BF)
            value = dot_nn(head[e, :, HIDDEN_SIZE:], h_two) + head_bias[1, e, :, :1]
            slots[pl.ds(pl.multiple_of(e * SLOT, SLOT), SLOT), part] = value
        return carry

    lax.fori_loop(0, CRITICS, one_critic, 0)
    for e in range(CRITICS):
        packed[e * QUANTS : e * QUANTS + SLOT] = slots[e * SLOT : (e + 1) * SLOT]
    copy.wait()
    for i in range(rows // PADDED):
        part = pl.ds(i * PADDED, PADDED)
        kept = (order[part] < KEPT_ATOMS).astype(F32)
        kept = jnp.concatenate([kept, jnp.zeros((PADDED, PADDED - MERGED_SUPPORTS), F32)], 1)
        keep[:, part] = jnp.transpose(kept).astype(BF)
    decay = DISCOUNT * (1.0 - done[:, mine].astype(F32))
    temperature = jnp.exp(jnp.full((1, 1), heat[0], F32))
    lagged[...] = payoffs[:, mine] + decay * (packed[:PADDED] - temperature * logp[...])


def target_pass(index, heat, inputs, logp, payoffs, done, order, first, second, bias, head, head_bias, after):
    rows = inputs.shape[1]
    return pl.pallas_call(
        target_kernel,
        in_specs=[SCALAR] * 2 + [WHOLE] * 4 + [pl.BlockSpec(memory_space=pltpu.HBM)] + [WHOLE] * 5 + [UNREAD],
        out_specs=[WHOLE] * 2,
        out_shape=[jax.ShapeDtypeStruct((PADDED, rows), F32), jax.ShapeDtypeStruct((PADDED, rows), BF)],
        scratch_shapes=[
            pltpu.VMEM((HIDDEN_SIZE, HIDDEN_SIZE), BF),
            pltpu.VMEM((32, HIDDEN_SIZE), F32),
            pltpu.VMEM((CRITICS * SLOT, rows), F32),
            pltpu.VMEM((136, rows), F32),
            pltpu.VMEM((rows, MERGED_SUPPORTS), jnp.int32),
            pltpu.SemaphoreType.DMA((1,)),
        ],
        compiler_params=params(24),
        cost_estimate=cost(7e9, 7e6),
        name="target_pass",
    )(index, heat, inputs, logp, payoffs, done, order, first, second, bias, head, head_bias, after)


HALF = 336


def two_terms(value):
    high = value.astype(BF).astype(F32)
    both = jnp.concatenate([high, value - high], 1)
    return jnp.concatenate([both, jnp.zeros((8, 2 * PADDED), F32)], 0).astype(BF)


def pilot_kernel(
    level, share, me, index, heat, obs, next_in, noise, noise_next_in, chosen, actor, small,
    first, second, bias, head, head_bias,
    own_out, send_out, x_now, x_target, logp_next,
    inputs, filled, tall_x, tall_w, dact, total, out_scratch, grad_out, small_out, next_obs, noise_next, sems,
):
    rows = obs.shape[1]
    mine = pl.ds(pl.multiple_of(index[0] * rows, PADDED), rows)
    copies = [
        pltpu.make_async_copy(next_in.at[:, mine], next_obs, sems.at[0]),
        pltpu.make_async_copy(noise_next_in.at[:, mine], noise_next, sems.at[1]),
    ]
    for copy in copies:
        copy.start()
    g_one, g_two, scaled, act, logp = actor_layers(obs[...], noise[...], actor, small, out_scratch)
    fill_inputs(tall_x, inputs, obs, act.astype(BF))
    fill_inputs(tall_x, x_now, obs, chosen[...])
    for copy in copies:
        copy.wait()
    _, _, _, next_act, next_logp = actor_layers(next_obs[...], noise_next[...], actor, small, out_scratch)
    fill_inputs(tall_x, x_target, next_obs, next_act.astype(BF))
    logp_next[...] = next_logp

    dact[...] = jnp.zeros(dact.shape, F32)
    total[...] = jnp.zeros(total.shape, F32)

    def one_critic(e, tail):
        lanes = critic_lanes(e)
        fill_first(tall_w, filled, first[:, lanes], bias[:1, lanes])
        b_two = column(bias[1:2, lanes])
        head_sum = jnp.sum(head[e, :, :HIDDEN_SIZE].astype(F32), axis=0, keepdims=True)
        weight = column(head_sum)
        push = column(head_sum * level)
        w_two = second[:, lanes]
        for part in tiles(rows):
            h_one = jnp.maximum(dot_tn(filled[...], inputs[:, part]), 0.0).astype(BF)
            h_two = jnp.maximum(dot_tn(w_two, h_one) + b_two, 0.0)
            weighted = h_two * weight
            total[:, part] += jnp.sum(weighted.reshape(-1, 8, weighted.shape[1]), axis=0)
            dz_two = jnp.where(h_two > 0, push, 0.0).astype(BF)
            grad = dot_nn(w_two, dz_two)
            dz_one = jnp.where(h_one > 0, grad, 0.0).astype(BF)
            dact[:, part] += dot_nn(first[OBS_DIM // 16 * 16 :, lanes], dz_one)
        return tail + head_bias[0, e, :, :1]

    tail = lax.fori_loop(0, CRITICS, one_critic, jnp.zeros((SLOT, 1), F32))
    temperature_share = jnp.exp(jnp.full((1, 1), heat[0], F32)) * share
    skip = OBS_DIM % 16
    action_grad = dact[skip : skip + ACT_DIM]
    pre = action_grad * (1.0 - act * act) + 2.0 * temperature_share * act
    out_scratch[:ACT_DIM] = pre
    out_scratch[ACT_DIM : 2 * ACT_DIM] = pre * scaled - temperature_share
    dout = out_scratch[: 2 * ACT_DIM].astype(BF)
    a_two = actor[OBS_DIM : OBS_DIM + ACTOR_HIDDEN]
    a_three = actor[OBS_DIM + ACTOR_HIDDEN :]
    dz_two = jnp.where(g_two > 0, dot_tn(a_three, dout), 0.0).astype(BF)
    dz_one = jnp.where(g_one > 0, dot_nn(a_two, dz_two), 0.0).astype(BF)
    grad_out[OBS_DIM + ACTOR_HIDDEN : OBS_DIM + ACTOR_HIDDEN + 2 * ACT_DIM] = dot_nt(dout, g_two)
    grad_out[OBS_DIM + ACTOR_HIDDEN + 2 * ACT_DIM :] = jnp.zeros((6, ACTOR_HIDDEN), F32)
    grad_out[OBS_DIM : OBS_DIM + ACTOR_HIDDEN] = dot_nt(g_one, dz_two)
    grad_out[:OBS_DIM] = dot_nt(obs[...], dz_one)
    ones = jnp.ones((16, rows), BF)
    small_out[...] = jnp.zeros(small_out.shape, F32)
    sum_one = dot_nt(ones, dz_one)[:1]
    sum_two = dot_nt(ones, dz_two)[:1]
    small_out[0:1] = sum_one[:, :PADDED]
    small_out[1:2] = sum_one[:, PADDED:]
    small_out[2:3] = sum_two[:, :PADDED]
    small_out[3:4] = sum_two[:, PADDED:]
    small_out[4:5, : 2 * ACT_DIM] = dot_nt(ones, dout)[:1]
    pilot_total = jnp.sum(total[...]) + rows * jnp.sum(tail)
    small_out[5:6] = jnp.broadcast_to(pilot_total, (1, PADDED))
    small_out[6:7] = jnp.broadcast_to(jnp.sum(logp), (1, PADDED))
    packed = two_terms(small_out[...])
    side = me[0] & 1
    for out, which in ((own_out, side), (send_out, 1 - side)):
        out[:HALF] = grad_out[pl.ds(pl.multiple_of(which * HALF, 16), HALF)].astype(BF)
        out[HALF:] = packed


def pilot_pass(
    level, share, me, index, heat, obs, next_obs, noise, noise_next, chosen, actor, small,
    first, second, bias, head, head_bias,
):
    rows = obs.shape[1]
    far = pl.BlockSpec(memory_space=pltpu.HBM)
    filled = jax.ShapeDtypeStruct((HIDDEN_SIZE, rows), BF)
    return pl.pallas_call(
        functools.partial(pilot_kernel, level, share),
        in_specs=[SCALAR] * 3 + [WHOLE, far, WHOLE, far] + [WHOLE] * 8,
        out_specs=[WHOLE] * 5,
        out_shape=[jax.ShapeDtypeStruct((HALF + 16, ACTOR_HIDDEN), BF)] * 2
        + [filled, filled, jax.ShapeDtypeStruct((1, rows), F32)],
        scratch_shapes=[
            pltpu.VMEM((HIDDEN_SIZE, rows), BF),
            pltpu.VMEM((HIDDEN_SIZE, HIDDEN_SIZE), BF),
            pltpu.VMEM((32, rows), F32),
            pltpu.VMEM((32, HIDDEN_SIZE), F32),
            pltpu.VMEM((INPUTS - OBS_DIM // 16 * 16, rows), F32),
            pltpu.VMEM((8, rows), F32),
            pltpu.VMEM((40, rows), F32),
            pltpu.VMEM((2 * HALF, ACTOR_HIDDEN), F32),
            pltpu.VMEM((8, PADDED), F32),
            pltpu.VMEM((OBS_DIM, rows), BF),
            pltpu.VMEM((ACT_DIM, rows), F32),
            pltpu.SemaphoreType.DMA((2,)),
        ],
        compiler_params=params(24),
        cost_estimate=cost(14e9, 9e6),
        name="pilot_pass",
    )(me, index, heat, obs, next_obs, noise, noise_next, chosen, actor, small, first, second, bias, head, head_bias)


def pair_terms(q_ref, lagged, keep, parts, rows):
    def group(i, carry):
        part = pl.ds(pl.multiple_of(i * PADDED, PADDED), PADDED)
        q = q_ref[:, part]
        shift = jnp.sum(q, axis=0, keepdims=True) * (1.0 / QUANTS)
        y = (lagged[:, part] - shift).astype(BF).reshape(8, 16, PADDED)
        upper = keep[:, part].reshape(8, 16, PADDED)
        lower = -upper
        q_ref[:, part] = q - shift
        for j in range(QUANTS):
            level = jnp.broadcast_to(q_ref[j : j + 1, part], (16, PADDED)).astype(BF)
            d = y - level[None]
            c = jnp.minimum(jnp.maximum(d, lower), upper)
            half = c * jnp.asarray(0.5, BF)
            g = half + jnp.abs(c) * jnp.asarray((j + 0.5) / QUANTS - 0.5, BF)
            h = g * (d - half)
            g = g[:4] + g[4:]
            g = g[:2] + g[2:]
            parts[j * 16 : j * 16 + 16, part] = g[0] + g[1]
            h = h[:4] + h[4:]
            h = h[:2] + h[2:]
            parts[(QUANTS + j) * 16 : (QUANTS + j) * 16 + 16, part] = h[0] + h[1]
        return carry

    lax.fori_loop(0, rows // PADDED, group, 0)
    shape = (48, 2 * QUANTS * 16)
    row = lax.broadcasted_iota(jnp.int32, shape, 0)
    owner = jnp.minimum(lax.broadcasted_iota(jnp.int32, shape, 1) // 16, SLOT)
    owner = jnp.where(owner >= QUANTS, SLOT, owner)
    return dot_nn((row == owner).astype(F32).astype(BF), parts[...])


PARITY = 18


def granules(e):
    mine = range(32 * e, 32 * e + 32)
    return [[g for g in mine if g // CRITICS % 2 == parity] for parity in range(2)]


def granule_places(chunk):
    places = np.zeros(CRITICS * 32, np.int32)
    for i, e in enumerate(chunk):
        for way in granules(e):
            for t, g in enumerate(way):
                places[g] = i * PARITY + t
    return places


SENT = (6, 6, 6, 4)


def store_piece(outs, t, value):
    for out in outs:
        if t < out.shape[0]:
            out[t] = value
            return
        t -= out.shape[0]


def critic_kernel(
    e, waits, rows_scale, split, me, inputs, lagged, keep, first, second, bias, head, head_bias, *refs,
):
    last = e == CRITICS - 1
    refs = refs[waits:]
    if e:
        before, refs = refs[:3], refs[3:]
    outs, scratch = refs[:-9], refs[-9:]
    filled, tall_w, h_one, h_two, q, parts, grads, packed, extra = scratch
    rows = inputs.shape[1]
    lanes = slice(e * HIDDEN_SIZE, (e + 1) * HIDDEN_SIZE)
    second = second.at[:, lanes]
    head = head.at[e : e + 1, :, :HIDDEN_SIZE]
    head_bias = head_bias.at[:1, e : e + 1]
    fill_first(tall_w, filled, first[:, lanes], bias[:1, lanes])
    b_two = column(bias[1:2, lanes])
    for part in tiles(rows):
        one = jnp.maximum(dot_tn(filled[...], inputs[:, part]), 0.0).astype(BF)
        h_one[:, part] = one
        two = jnp.maximum(dot_tn(second[...], one) + b_two, 0.0).astype(BF)
        h_two[:, part] = two
        q[:, part] = dot_nn(head[0], two) + head_bias[0, 0, :, :1]
    terms = pair_terms(q, lagged, keep, parts, rows)
    low = (terms[:SLOT] * -rows_scale).astype(BF)
    loss = terms[SLOT : SLOT + 1]
    head_grad = dot_nt(low, h_two[...])
    count = jnp.ones((8, rows), BF)
    bias_grad = dot_nt(count, low)[:1]
    sums = jnp.zeros((HIDDEN_SIZE, PADDED), F32)
    for part in tiles(rows):
        two = h_two[:, part]
        dz_two = jnp.where(two > 0, dot_tn(head[0], low[:, part.start : part.start + part.size]), 0.0)
        for i in range(part.size // PADDED):
            sums = sums + dz_two[:, i * PADDED : (i + 1) * PADDED]
        dz_two = dz_two.astype(BF)
        h_two[:, part] = dz_two
        one = h_one[:, part]
        h_one[:, part] = jnp.where(one > 0, dot_nn(second[...], dz_two), 0.0).astype(BF)
        second_part = dot_nt(dz_two, one)
        second_grad = second_grad + second_part if part.start else second_part
    grads[:, :, :HIDDEN_SIZE] = second_grad.astype(BF).reshape(-1, 16, HIDDEN_SIZE)
    first_grad = dot_nt(h_one[...], inputs[...])
    grads[:, :, HIDDEN_SIZE : LANES - PADDED] = (
        first_grad[:, : HIDDEN_SIZE - PADDED].astype(BF).reshape(-1, 16, HIDDEN_SIZE - PADDED)
    )
    lane = lax.broadcasted_iota(jnp.int32, (HIDDEN_SIZE, PADDED), 1)
    tail = jnp.where(
        lane == INPUTS + 1 - HIDDEN_SIZE + PADDED,
        jnp.sum(sums, axis=1, keepdims=True),
        first_grad[:, HIDDEN_SIZE - PADDED :],
    )
    grads[:, :, LANES - PADDED : LANES] = tail.astype(BF).reshape(-1, 16, PADDED)
    direct = split[0] > 0
    rest = outs[1 + (len(SENT) if last else 1) :] if direct else outs[1:]
    if not last:
        all_heads, all_bias, all_loss = rest
        if e:
            all_heads[...] = before[0][...]
            all_bias[...] = before[1][...]
            all_loss[...] = before[2][...] + loss
        else:
            all_heads[...] = jnp.zeros(all_heads.shape, F32)
            all_bias[...] = jnp.zeros(all_bias.shape, F32)
            all_loss[...] = loss
        all_heads[e * SLOT : (e + 1) * SLOT] = head_grad
        all_bias[e : e + 1, :SLOT] = bias_grad
    else:
        n_rows, n_quant = split
        for i in range(CRITICS):
            packed[i * QUANTS : i * QUANTS + SLOT] = (
                before[0][i * SLOT : (i + 1) * SLOT] if i < e else head_grad
            )
        bias_row = jnp.zeros((1, PADDED), F32)
        lane = lax.broadcasted_iota(jnp.int32, (1, PADDED), 1)
        spare = jnp.zeros((1, PADDED - SLOT), F32)
        for i in range(CRITICS):
            piece = before[1][i : i + 1] if i < e else jnp.concatenate([bias_grad, spare], 1)
            piece = pltpu.roll(jnp.broadcast_to(piece, (8, PADDED)), i * QUANTS, 1)[:1]
            inside = (lane >= i * QUANTS) & (lane < (i + 1) * QUANTS)
            bias_row = jnp.where(inside, piece, bias_row)
        value = jnp.sum(before[2][...] + loss, axis=1, keepdims=True) * rows_scale
        value = jnp.broadcast_to(value, (1, PADDED))
        if direct:
            width = HIDDEN_SIZE // n_rows
            high = PADDED // n_quant
            lane = lax.broadcasted_iota(jnp.int32, (16, PADDED), 1)
            halves = [bias_row, pltpu.roll(jnp.broadcast_to(bias_row, (8, PADDED)), 64, 1)[:1], value]
            common = jnp.concatenate(halves + [jnp.zeros((13, PADDED), F32)], 0)
            for j in range(8):
                y, c = j // 4, j % 4
                for z in range(n_rows // 2):
                    r = 2 * z + y
                    block = packed[c * high : (c + 1) * high, r // 2 * PADDED : (r // 2 + 1) * PADDED]
                    if r % 2 == 0:
                        block = pltpu.roll(block, width, 1)
                    base = 2 * z * PADDED
                    extra[j, :, base : base + PADDED] = jnp.where(lane < 64, common, block[:16]).astype(BF)
                    extra[j, :, base + PADDED : base + 2 * PADDED] = block[16:].astype(BF)
        else:
            rest[0][...] = packed[:PADDED]
            rest[1][...] = jnp.concatenate([bias_row, value, jnp.zeros((6, PADDED), F32)], 0)
    if not direct:
        outs[0][...] = grads[...]
        return
    sent, kept = outs[: len(SENT) if last else 1], outs[len(SENT) if last else 1]
    side = me[0] & 1
    ways = granules(e)
    for t in range(max(map(len, ways))):
        pair = [way[min(t, len(way) - 1)] - e * 32 for way in ways]
        kept[t] = grads[jnp.where(side == 0, pair[0], pair[1])]
        store_piece(sent, t, grads[jnp.where(side == 0, pair[1], pair[0])])
    if last:
        for i in range(4):
            kept[PARITY + i] = extra[2 * i + side]
            store_piece(sent, PARITY + i, extra[2 * i + 1 - side])


def critic_pass(e, rows_scale, split, me, inputs, lagged, keep, first, second, bias, head, head_bias, after, before):
    rows = inputs.shape[1]
    last = e == CRITICS - 1
    if split[0]:
        block = lambda count: jax.ShapeDtypeStruct((count, 16, LANES), BF)
        sent = SENT if last else (PARITY,)
        out_shape = [block(count) for count in sent] + [block(sum(sent))]
    else:
        out_shape = [jax.ShapeDtypeStruct((HIDDEN_SIZE // 16, 16, LANES), BF)]
    if not last:
        out_shape += [
            jax.ShapeDtypeStruct((CRITICS * SLOT, HIDDEN_SIZE), F32),
            jax.ShapeDtypeStruct((8, PADDED), F32),
            jax.ShapeDtypeStruct((1, rows), F32),
        ]
    elif not split[0]:
        out_shape += [
            jax.ShapeDtypeStruct((PADDED, HIDDEN_SIZE), F32),
            jax.ShapeDtypeStruct((8, PADDED), F32),
        ]
    return pl.pallas_call(
        functools.partial(critic_kernel, e, len(after), rows_scale, split),
        in_specs=[SCALAR] + [WHOLE] * 8 + [UNREAD] * len(after) + [WHOLE] * len(before),
        out_specs=[WHOLE] * len(out_shape),
        out_shape=out_shape,
        scratch_shapes=[
            pltpu.VMEM((HIDDEN_SIZE, HIDDEN_SIZE), BF),
            pltpu.VMEM((32, HIDDEN_SIZE), F32),
            pltpu.VMEM((HIDDEN_SIZE, rows), BF),
            pltpu.VMEM((HIDDEN_SIZE, rows), BF),
            pltpu.VMEM((SLOT, rows), F32),
            pltpu.VMEM((2 * QUANTS * 16, rows), BF),
            pltpu.VMEM((HIDDEN_SIZE // 16, 16, LANES), BF),
            pltpu.VMEM((136, HIDDEN_SIZE), F32),
            pltpu.VMEM((8, 16, LANES), BF),
        ],
        compiler_params=params(24),
        cost_estimate=cost(7e9, 4e6),
        name="critic_pass",
    )(me, inputs, lagged, keep, first, second, bias, head, head_bias, *after, *before)


def add_kernel(a, b, out):
    out[:HALF] = (a[:HALF].astype(F32) + b[:HALF].astype(F32)).astype(BF)
    pair = [r[HALF:].astype(F32) for r in (a, b)]
    pair = [p[:8, :PADDED] + p[:8, PADDED:] for p in pair]
    out[HALF:] = two_terms(pair[0] + pair[1])


def add_actor(a, b):
    return pl.pallas_call(
        add_kernel,
        in_specs=[WHOLE, WHOLE],
        out_specs=WHOLE,
        out_shape=jax.ShapeDtypeStruct(a.shape, BF),
        compiler_params=params(),
        cost_estimate=cost(1e5, 6e5),
        name="add_actor",
    )(a, b)


def core_kernel(chunk, depth, waits, me, places, *refs):
    count = len(chunk)
    refs = refs[waits:]
    kept, got, outs, sums = refs[:count], refs[count:-3], refs[-3:-1], refs[-1]
    size = count * PARITY
    first = 0
    for piece in got:
        i, inside = min(first // PARITY, count - 1), first - min(first // PARITY, count - 1) * PARITY
        own = kept[i][inside : inside + piece.shape[0]]
        sums[first : first + piece.shape[0]] = (own.astype(F32) + piece[...].astype(F32)).astype(BF)
        first += piece.shape[0]
    z_first = chunk[-1] // 3 * depth
    side = me[0] & 1
    for k in range(4):
        flip = (0, 4 - 2 * side, 2 + 2 * side, 6)[k]
        j = (me[0] & 7) ^ flip
        out = outs[k // 2]
        for z in range(depth):
            owner = (z_first + z) * 8 + j
            for i in range(CRITICS):
                out[k % 2, z * CRITICS + i] = sums[places[owner * CRITICS + i]]
        if chunk[-1] == CRITICS - 1:
            out[k % 2, depth * CRITICS] = sums[size + j // 2]


def add_core(chunk, depth, me, kept, got, after=()):
    tail = kept[-1].shape[0] - PARITY
    count = depth * CRITICS + (1 if tail else 0)
    return pl.pallas_call(
        functools.partial(core_kernel, chunk, depth, len(after)),
        in_specs=[SCALAR, SCALAR] + [UNREAD] * len(after) + [WHOLE] * (len(kept) + len(got)),
        out_specs=[WHOLE] * 2,
        out_shape=[jax.ShapeDtypeStruct((2, count, 16, LANES), BF)] * 2,
        scratch_shapes=[pltpu.VMEM((len(kept) * PARITY + tail, 16, LANES), BF)],
        compiler_params=params(),
        cost_estimate=cost(1e6, 8e6),
        name="add_core",
    )(me, jnp.asarray(granule_places(chunk)), *after, *kept, *got)


def tree(values):
    while len(values) > 1:
        values = [a + b for a, b in zip(values[::2], values[1::2])]
    return values[0]


def half_kernel(kept, got, own, send):
    for k, out in enumerate((own, send)):
        out[...] = (kept[k].astype(F32) + got[k].astype(F32)).astype(BF)


def add_half(kept, got, after=()):
    waits = len(after)
    return pl.pallas_call(
        lambda *refs: half_kernel(*refs[waits:]),
        in_specs=[UNREAD] * waits + [WHOLE] * 2,
        out_specs=[WHOLE] * 2,
        out_shape=[jax.ShapeDtypeStruct(kept.shape[1:], BF)] * 2,
        compiler_params=params(8),
        cost_estimate=cost(1e5, 1e5),
        name="add_half",
    )(*after, kept, got)


def line_kernel(me, early, early_got, late, late_got, *refs):
    outs, sums = refs[:-1], refs[-1]
    count = early.shape[0]
    sums[:count] = (early[...].astype(F32) + early_got[...].astype(F32)).astype(BF)
    total = late[...].astype(F32) + late_got[...].astype(F32)
    sums[count:] = total[:count].astype(BF)
    extra = total[count]
    lane = lax.broadcasted_iota(jnp.int32, (16, PADDED), 1)
    for z in range(len(outs)):
        first = extra[:, 2 * z * PADDED : (2 * z + 1) * PADDED]
        second = extra[:, (2 * z + 1) * PADDED : (2 * z + 2) * PADDED]
        for i, value in enumerate((first, second, pltpu.roll(first, 64, 1))):
            old = sums[z * CRITICS + i, :, LANES - PADDED :].astype(F32)
            sums[z * CRITICS + i, :, LANES - PADDED :] = jnp.where(lane < 64, old, value).astype(BF)
    for k, out in enumerate(outs):
        first = ((me[0] // 8) ^ k) * CRITICS
        for i in range(CRITICS):
            out[i] = sums[first + i]


def add_line(me, early, late, depth, after=()):
    waits = len(after)
    return pl.pallas_call(
        lambda *refs: line_kernel(*refs[waits:]),
        in_specs=[UNREAD] * waits + [SCALAR] + [WHOLE] * 4,
        out_specs=[WHOLE] * depth,
        out_shape=[jax.ShapeDtypeStruct((CRITICS, 16, LANES), BF)] * depth,
        scratch_shapes=[pltpu.VMEM((2 * early[0].shape[0], 16, LANES), BF)],
        compiler_params=params(),
        cost_estimate=cost(1e6, 6e6),
        name="add_line",
    )(*after, me, *early, *late)


def adamw(weight, first, second, grad, rate, factors, outs):
    first_new = BETA_FIRST * first[...] + (1.0 - BETA_FIRST) * grad
    second_new = BETA_SECOND * second[...] + (1.0 - BETA_SECOND) * grad * grad
    old = weight[...]
    step = (first_new * factors[0]) / (jnp.sqrt(second_new * factors[1]) + EPSILON)
    outs[0][...] = old - rate * (step + WEIGHT_DECAY * old)
    outs[1][...] = first_new
    outs[2][...] = second_new


def row_kernel(*refs):
    total = tree([r[2, :, LANES - PADDED :].astype(F32) for r in refs[:-1]])
    total = pltpu.roll(total, 64, 1)
    row = jnp.concatenate([total[:1, :64], total[1:2, :64]], 1)
    refs[-1][...] = jnp.concatenate([row, jnp.broadcast_to(total[2:3, :1], (7, PADDED))], 0)


def sum_row(blocks):
    return pl.pallas_call(
        row_kernel,
        in_specs=[WHOLE] * len(blocks),
        out_specs=WHOLE,
        out_shape=jax.ShapeDtypeStruct((8, PADDED), F32),
        compiler_params=params(8),
        cost_estimate=cost(1e5, 1e5),
        name="sum_row",
    )(*blocks)


def update_kernel(count, direct, factors, *refs):
    blocks, refs = refs[:count], refs[count:]
    if direct:
        total = tree([b[...].astype(F32) for b in blocks]).reshape(-1, LANES)
        head_grad = pltpu.roll(total[:SLOT, LANES - PADDED :], 64, 1)[:, :64]
    else:
        total = blocks[0][...]
        head_grad, refs = refs[0][...], refs[1:]
    state, outs = refs[:12], refs[12:]
    adamw(*state[0:3], total[:, HIDDEN_SIZE : HIDDEN_SIZE + INPUTS], RATE_MATRIX, factors, outs[0:3])
    adamw(*state[3:6], total[:, :HIDDEN_SIZE], RATE_MATRIX, factors, outs[3:6])
    edge = INPUTS - HIDDEN_SIZE + PADDED
    bias_grad = jnp.transpose(total[:, LANES - PADDED :])[edge : edge + 2]
    adamw(*state[6:9], bias_grad, RATE_VECTOR, factors, outs[6:9])
    adamw(*state[9:12], head_grad, RATE_MATRIX, factors, outs[9:12])


def update(factors, blocks, others, state):
    shapes = [jax.ShapeDtypeStruct(a.shape, F32) for a in state]
    count = len(blocks)
    return pl.pallas_call(
        functools.partial(update_kernel, count, not others),
        in_specs=[SCALAR] + [WHOLE] * (count + len(others) + len(state)),
        out_specs=[WHOLE] * len(shapes),
        out_shape=shapes,
        compiler_params=params(),
        cost_estimate=cost(2e6, 6e6),
        name="update",
    )(factors, *blocks, *others, *state)


def actor_update_kernel(me, factors, own, peer, *refs):
    state, outs, grad = refs[:3], refs[3:7], refs[7]
    side = me[0] & 1
    grad[pl.ds(pl.multiple_of(side * HALF, 16), HALF)] = own[:HALF].astype(F32)
    grad[pl.ds(pl.multiple_of((1 - side) * HALF, 16), HALF)] = peer[:HALF].astype(F32)
    adamw(*state, grad[: state[0].shape[0]], RATE_MATRIX, factors, outs[:3])
    pair = own[HALF:].astype(F32)
    outs[3][...] = pair[:8, :PADDED] + pair[:8, PADDED:]


def actor_update(me, factors, own, peer, state):
    shapes = [jax.ShapeDtypeStruct(a.shape, F32) for a in state] + [jax.ShapeDtypeStruct((8, PADDED), F32)]
    return pl.pallas_call(
        actor_update_kernel,
        in_specs=[SCALAR, SCALAR] + [WHOLE] * (2 + len(state)),
        out_specs=[WHOLE] * len(shapes),
        out_shape=shapes,
        scratch_shapes=[pltpu.VMEM((2 * HALF, ACTOR_HIDDEN), F32)],
        compiler_params=params(),
        cost_estimate=cost(2e6, 5e6),
        name="actor_update",
    )(me, factors, own, peer, *state)


def small_update_kernel(samples, me, factors, row_own, row_peer, small_sums, *refs):
    state, outs, vector = refs[:6], refs[6:13], refs[13]
    row = jnp.where((me[0] & 1) == 0, row_own[...], row_peer[...])
    for i in range(4):
        vector[i * PADDED : (i + 1) * PADDED] = small_sums[i]
    wide = jnp.concatenate([row, jnp.zeros((8, PADDED), F32)], 1)
    wide = pltpu.roll(wide, 2 * ACT_DIM, 1)
    wide = wide + jnp.concatenate([small_sums[4:5], jnp.zeros((1, PADDED), F32)], 1)
    vector[4 * PADDED :] = wide[0]
    adamw(*state[:3], vector[:SMALL_VEC], RATE_VECTOR, factors, outs[1:4])
    heat = state[3][...]
    logp_sum = small_sums[6:7, :1]
    shortfall = (ACT_DIM * samples - logp_sum) / samples
    adamw(*state[3:6], shortfall, STEP_SIZE_SCALE, factors, outs[4:7])
    actor_loss = (jnp.exp(heat) * logp_sum - small_sums[5:6, :1] / MERGED_SUPPORTS) / samples
    outs[0][...] = row[1:2, :1] + actor_loss + heat * shortfall


def small_update(samples, me, factors, row, row_peer, small_sums, state):
    shapes = [jax.ShapeDtypeStruct((1, 1), F32)] + [jax.ShapeDtypeStruct(a.shape, F32) for a in state]
    return pl.pallas_call(
        functools.partial(small_update_kernel, samples),
        in_specs=[SCALAR, SCALAR] + [WHOLE] * (3 + len(state)),
        out_specs=[WHOLE] * len(shapes),
        out_shape=shapes,
        scratch_shapes=[pltpu.VMEM((6 * PADDED,), F32)],
        compiler_params=params(8),
        cost_estimate=cost(1e6, 1e5),
        name="small_update",
    )(me, factors, row, row_peer, small_sums, *state)


def exchange(value, flip):
    count = lax.axis_size("rows") * lax.axis_size("quant")
    return lax.ppermute(value, AXES, [(i, i ^ flip) for i in range(count)])


def exchange_sides(value, even, odd):
    count = lax.axis_size("rows") * lax.axis_size("quant")
    return lax.ppermute(value, AXES, [(i, i ^ (odd if i % 2 else even)) for i in range(count)])


def all_sum(value):
    total = lax.axis_size("rows") * lax.axis_size("quant")
    flip = 1
    while flip < total:
        value = value + exchange(value, flip)
        flip *= 2
    return value


def scatter_sum(pieces):
    total = pieces.shape[0]
    flip = total // 2
    while flip:
        low = pieces.astype(BF)
        pieces = low[:flip].astype(F32) + exchange(low[flip:], flip).astype(F32)
        flip //= 2
    return pieces[0]


def local(
    obs, chosen, noise_now, next_obs, noise_next, payoffs, done, order,
    w_one, w_two, biases, head_part, t_one, t_two, t_biases, t_head_part, t_head_bias,
    actor, counter,
    in_w, in_m, in_v, mid_w, mid_m, mid_v, bias_w, bias_m, bias_v, head_w, head_m, head_v,
    actor_w, actor_m, actor_v, small_w, small_m, small_v, heat, heat_m, heat_v,
):
    n_rows, n_quant = lax.axis_size("rows"), lax.axis_size("quant")
    devices = n_rows * n_quant
    rows = obs.shape[0]
    samples = rows * devices
    index = lax.axis_index("quant").reshape(1)
    device = lax.axis_index("rows") * n_quant + lax.axis_index("quant")
    me = device.reshape(1)
    direct = n_rows == 8 and n_quant == 4
    small_row = small_w.reshape(1, -1)
    tally = counter.astype(F32)
    factors = jnp.concatenate(
        [1.0 / (1.0 - jnp.power(BETA_FIRST, tally)), 1.0 / (1.0 - jnp.power(BETA_SECOND, tally))]
    )

    own_head = jnp.concatenate([head_part.T, t_head_part.T], 1)
    got = [
        lax.ppermute(own_head, "quant", [(i, i ^ k) for i in range(n_quant)]) for k in (1, 2, 3)
    ]
    head, head_bias = heads(index, own_head, got, small_row, t_head_bias.reshape(1, -1))

    level = float(np.asarray(-1.0 / (MERGED_SUPPORTS * samples), ml_dtypes.bfloat16))
    own, send, x_now, x_target, logp = pilot_pass(
        level, 1.0 / samples, me, index, heat, obs.T, next_obs.T, noise_now.T, noise_next.T, chosen.T,
        actor, small_row, w_one, w_two, biases, head, head_bias,
    )
    lagged, keep = target_pass(
        index, heat, x_target, logp, payoffs.reshape(1, -1), done.reshape(1, -1), order,
        t_one, t_two, t_biases, head, head_bias, own,
    )
    own = add_actor(own, exchange(send, 1))
    flips = [1 << i for i in range(1, devices.bit_length() - 1)]
    scale = 1.0 / (samples * MERGED_SUPPORTS * KEPT_ATOMS)
    split = (n_rows, n_quant) if direct else (0, 0)
    kept, got, before, early = [], [], (), None
    for e in range(CRITICS):
        after = [own] if e < 4 else []
        if direct and e == CRITICS - 1:
            early = add_core((0, 1, 2), 2, me, kept[:3], got[:3])
            early = [early[0], exchange_sides(early[1], 2, 4)]
            after = [early[0]]
        outs = critic_pass(
            e, scale, split, me, x_now, lagged, keep, w_one, w_two, biases, head, head_bias, after, before
        )
        if direct:
            count = len(SENT) if e == CRITICS - 1 else 1
            got.extend(exchange(piece, 1) for piece in outs[:count])
            outs = outs[count:]
        kept.append(outs[0])
        before = outs[1:]
        for flip in flips[e : e + 1] if e < CRITICS - 1 else flips[e:]:
            own = add_actor(own, exchange(own, flip))
    peer = exchange(own, 1)
    *actor_new, small_sums = actor_update(me, factors, own, peer, (actor_w, actor_m, actor_v))

    if direct:
        early = add_half(*early)
        late = add_core((2, 3, 4), 2, me, kept[2:], got[2:], (early[0],))
        early = [early[0], exchange_sides(early[1], 4, 2)]
        late = add_half(late[0], exchange_sides(late[1], 2, 4), (own, early[1]))
        late = [late[0], exchange_sides(late[1], 4, 2)]
        blocks = add_line(me, early, late, n_rows // 2, (small_sums,))
        blocks = [blocks[0]] + [exchange(blocks[k], 8 * k) for k in range(1, len(blocks))]
        others = []
        row = sum_row(blocks)
        row_peer = exchange(row, 1)
    else:
        grads = jnp.stack(kept).reshape(devices, -1, LANES)
        order_of = device ^ jnp.arange(devices)
        blocks = [scatter_sum(jnp.take(grads, order_of, axis=0))]
        head_grad = before[0].reshape(n_quant, PADDED // n_quant, n_rows, HIDDEN_SIZE // n_rows)
        head_grad = head_grad.transpose(2, 0, 1, 3).reshape((devices,) + (PADDED // n_quant, -1))
        head_grad = scatter_sum(jnp.take(head_grad, order_of, axis=0))
        others = [head_grad]
        row = row_peer = all_sum(before[1])
    state = (
        in_w.T, in_m.T, in_v.T, mid_w.T, mid_m.T, mid_v.T, bias_w, bias_m, bias_v, head_w.T, head_m.T, head_v.T,
    )
    new = update(factors, blocks, others, state)
    state = (
        small_w, small_m, small_v,
        heat.reshape(1, 1), heat_m.reshape(1, 1), heat_v.reshape(1, 1),
    )
    objective, *last = small_update(samples, me, factors, row, row_peer, small_sums, state)
    return (
        objective.reshape(()),
        *(a.T for a in new[:6]),
        *new[6:9],
        *(a.T for a in new[9:]),
        *actor_new,
        *last[:3],
        *(a.reshape(-1) for a in last[3:]),
    )


def solution(mesh):
    both, row, none = P(AXES), P("rows"), P()
    column_of, shard = P(None, "quant"), P(None, AXES)
    placed = (
        (both,) * 3 + (row,) * 5 + (none,) * 3 + (column_of,) + (none,) * 3 + (column_of,) + (none,) * 3
        + (shard,) * 9 + (P("rows", "quant"),) * 3 + (none,) * 9
    )
    return jax.shard_map(
        local,
        mesh=mesh,
        in_specs=placed,
        out_specs=(none,) + (shard,) * 9 + (P("rows", "quant"),) * 3 + (none,) * 9,
        check_vma=False,
    )
```

profile of v0, /device:TPU:17, one launch (start us, length us, event | category | flops | bytes accessed | tf_op | source)
XLA Modules:
  0.0 134.1 jit_solution(16932586409842071519)
XLA Ops:
  0.7 0.8 pad_maximum_fusion.own
  1.4 1.8 %collective-permute-start.2 = (bf16[32,1024]{1,0:T(8,128)(2,1)S(1)}, bf16[32,1024]{1,0:T(8,128)(2,1)S(1)}, u32[]{:S(2)}, u32[]{:S(2)}) collective-permute-start(bf16[32,1024]{1,0:T(8,128)(2,1)S(1)} %pad_maximum_fusion.own), channel_id=1, source_target_pairs={{0,3},{1,2},{2,1},{3,0},{4,7},{5,6},{6,5},{7,4},{8,11},{9,10},{10,... | collective-permute-start | bytes 196616 | tf_op jit(solution)/shard_map/ppermute | solution.py:844
  3.2 0.3 collective-permute-start.1
  3.5 0.2 collective-permute-start
  4.3 0.7 reshape.85.small
  5.0 1.1 collective-permute-done.2.got_three
  6.1 1.3 collective-permute-done.1.got_two
  7.4 0.7 copy-done.35
  8.1 0.4 heads.1
  8.5 1.4 %copy-done.20 = bf16[4096,376]{0,1:T(8,128)(2,1)S(1)} copy-done((bf16[4096,376]{0,1:T(8,128)(2,1)S(1)}, bf16[4096,376]{0,1:T(8,128)(2,1)}, u32[]{:S(2)}) %copy-start.20) | copy-done | bytes 3080216
  9.9 0.8 copy-done.22
  10.7 0.6 copy-done.25
  11.3 0.1 copy-done.26
  11.4 0.1 copy-done.27
  11.5 0.1 copy-done.28
  11.6 0.0 copy-done.29
  11.7 16.5 %pilot_pass.1 = (bf16[352,256]{1,0:T(8,128)(2,1)S(1)}, bf16[352,256]{1,0:T(8,128)(2,1)S(1)}, bf16[512,1024]{1,0:T(8,128)(2,1)S(1)}, bf16[512,1024]{1,0:T(8,128)(2,1)S(1)}, f32[1,1024]{1,0:T(1,128)S(1)}) custom-call(s32[1]{0:T(128)} %bitcast.me.refs_1_, s32[1]{0:T(128)} %bitcast.1.me.index, f32[1]{0:T(128)} %copy.65.heat, bf16[376,1024]{1,0:T(8,128)(2,1)S(1)} %bitcast.50, ...), custom_call_target="tpu_custom_call" | custom-call | flops 14000000000 | bytes 9000000 | tf_op jit(solution)/shard_map/pilot_pass/pallas_call | solution.py:314
  28.2 0.6 collective-permute-start.3
  28.9 9.4 %target_pass.1 = (f32[128,1024]{1,0:T(8,128)S(1)}, bf16[128,1024]{1,0:T(8,128)(2,1)S(1)}) custom-call(s32[1]{0:T(128)} %bitcast.1.me.index, f32[1]{0:T(128)} %copy.65.heat, bf16[512,1024]{1,0:T(8,128)(2,1)S(1)} %get-tuple-element.97.inputs, f32[1,1024]{1,0:T(1,128)S(1)} %get-tuple-element.98.logp, f32[1,4096]{1,0:T(1,128)S(1)} %bitcast.54, ...), custom_call_target="tpu_custom_call" | custom-call | flops 7000000000 | bytes 7000000 | tf_op jit(solution)/shard_map/target_pass/pallas_call | solution.py:199
  38.4 1.3 collective-permute-start.4
  39.7 7.6 %critic_pass.5 = (bf16[18,16,1024]{2,1,0:T(8,128)(2,1)S(1)}, bf16[18,16,1024]{2,1,0:T(8,128)(2,1)S(1)}, f32[160,512]{1,0:T(8,128)S(1)}, f32[8,128]{1,0:T(8,128)S(1)}, f32[1,1024]{1,0:T(1,128)S(1)}) custom-call(s32[1]{0:T(128)} %bitcast.me.refs_1_, bf16[512,1024]{1,0:T(8,128)(2,1)S(1)} %get-tuple-element.96.inputs, f32[128,1024]{1,0:T(8,128)S(1)} %get-tuple-element.99.lagged, ...), custom_call_target="tpu_custom_call" | custom-call | flops 7000000000 | bytes 4000000 | tf_op jit(solution)/shard_map/critic_pass/pallas_call | solution.py:537
  47.3 0.4 collective-permute-start.9
  47.8 1.3 collective-permute-start.5
  49.1 7.7 %critic_pass.6 = (bf16[18,16,1024]{2,1,0:T(8,128)(2,1)S(1)}, bf16[18,16,1024]{2,1,0:T(8,128)(2,1)S(1)}, f32[160,512]{1,0:T(8,128)S(1)}, f32[8,128]{1,0:T(8,128)S(1)}, f32[1,1024]{1,0:T(1,128)S(1)}) custom-call(s32[1]{0:T(128)} %bitcast.me.refs_1_, bf16[512,1024]{1,0:T(8,128)(2,1)S(1)} %get-tuple-element.96.inputs, f32[128,1024]{1,0:T(8,128)S(1)} %get-tuple-element.99.lagged, ...), custom_call_target="tpu_custom_call" | custom-call | flops 7000000000 | bytes 4000000 | tf_op jit(solution)/shard_map/critic_pass/pallas_call | solution.py:537
  56.8 0.5 collective-permute-start.10
  57.4 1.4 %collective-permute-start.6 = (bf16[352,256]{1,0:T(8,128)(2,1)S(1)}, bf16[352,256]{1,0:T(8,128)(2,1)S(1)}, u32[]{:S(2)}, u32[]{:S(2)}) collective-permute-start(bf16[352,256]{1,0:T(8,128)(2,1)S(1)} %add_actor.7.a.refs_0_), channel_id=1, source_target_pairs={{0,8},{1,9},{2,10},{3,11},{4,12},{5,13},{6,14},{7,15},{8,0},{9,1},... | collective-permute-start | bytes 540680 | tf_op jit(solution)/shard_map/ppermute | solution.py:794
  58.7 7.6 %critic_pass.7 = (bf16[18,16,1024]{2,1,0:T(8,128)(2,1)S(1)}, bf16[18,16,1024]{2,1,0:T(8,128)(2,1)S(1)}, f32[160,512]{1,0:T(8,128)S(1)}, f32[8,128]{1,0:T(8,128)S(1)}, f32[1,1024]{1,0:T(1,128)S(1)}) custom-call(s32[1]{0:T(128)} %bitcast.me.refs_1_, bf16[512,1024]{1,0:T(8,128)(2,1)S(1)} %get-tuple-element.96.inputs, f32[128,1024]{1,0:T(8,128)S(1)} %get-tuple-element.99.lagged, ...), custom_call_target="tpu_custom_call" | custom-call | flops 7000000000 | bytes 4000000 | tf_op jit(solution)/shard_map/critic_pass/pallas_call | solution.py:537
  66.4 0.4 collective-permute-start.11
  66.8 7.6 %critic_pass.8 = (bf16[18,16,1024]{2,1,0:T(8,128)(2,1)S(1)}, bf16[18,16,1024]{2,1,0:T(8,128)(2,1)S(1)}, f32[160,512]{1,0:T(8,128)S(1)}, f32[8,128]{1,0:T(8,128)S(1)}, f32[1,1024]{1,0:T(1,128)S(1)}) custom-call(s32[1]{0:T(128)} %bitcast.me.refs_1_, bf16[512,1024]{1,0:T(8,128)(2,1)S(1)} %get-tuple-element.96.inputs, f32[128,1024]{1,0:T(8,128)S(1)} %get-tuple-element.99.lagged, ...), custom_call_target="tpu_custom_call" | custom-call | flops 7000000000 | bytes 4000000 | tf_op jit(solution)/shard_map/critic_pass/pallas_call | solution.py:537
  74.5 0.2 collective-permute-start.14
  74.7 1.5 %add_core.2 = (bf16[2,10,16,1024]{3,2,1,0:T(8,128)(2,1)S(1)}, bf16[2,10,16,1024]{3,2,1,0:T(8,128)(2,1)S(1)}) custom-call(s32[1]{0:T(128)} %bitcast.me.refs_1_, s32[160]{0:T(256)S(1)} %copy-done.16, bf16[18,16,1024]{2,1,0:T(8,128)(2,1)S(1)} %get-tuple-element.101.refs_0_, bf16[18,16,1024]{2,1,0:T(8,128)(2,1)S(1)} %get-tuple-element.105.refs_1_, ...), custom_call_target="tpu_custom_call" | custom-call | flops 1000000 | bytes 8000000 | tf_op jit(solution)/shard_map/add_core/pallas_call | solution.py:606
  76.3 0.3 collective-permute-start.12
  76.5 7.9 %critic_pass.9 = (bf16[6,16,1024]{2,1,0:T(8,128)(2,1)S(1)}, bf16[6,16,1024]{2,1,0:T(8,128)(2,1)S(1)}, bf16[6,16,1024]{2,1,0:T(8,128)(2,1)S(1)}, bf16[4,16,1024]{...) custom-call(s32[1]{0:T(128)} %bitcast.me.refs_1_, bf16[512,1024]{1,0:T(8,128)(2,1)S(1)} %get-tuple-element.96.inputs, ...), custom_call_target="tpu_custom_call" | custom-call | flops 7000000000 | bytes 4000000 | tf_op jit(solution)/shard_map/critic_pass/pallas_call | solution.py:537
  84.4 0.6 collective-permute-start.15
  85.1 0.1 collective-permute-start.16
  85.1 0.4 collective-permute-start.17
  85.6 0.5 collective-permute-done.12.refs_1_
  86.0 1.2 collective-permute-start.18
  87.2 0.2 add_half.2
  87.4 0.8 collective-permute-done.18.refs_9_
  88.3 1.5 %add_core.3 = (bf16[2,11,16,1024]{3,2,1,0:T(8,128)(2,1)S(1)}, bf16[2,11,16,1024]{3,2,1,0:T(8,128)(2,1)S(1)}) custom-call(s32[1]{0:T(128)} %bitcast.me.refs_1_, s32[160]{0:T(256)S(1)} %copy-done.15, bf16[10,16,1024]{2,1,0:T(8,128)(2,1)S(1)} %get-tuple-element.115.refs_0_.refs_2_, bf16[18,16,1024]{2,1,0:T(8,128)(2,1)S(1)} %get-tuple-element.109.refs_2_.refs_1_, ...), custom_call_target="tpu_custom_call" | custom-call | flops 1000000 | bytes 8000000 | tf_op jit(solution)/shard_map/add_core/pallas_call | solution.py:606
  89.8 0.3 collective-permute-start.19
  90.1 0.2 collective-permute-start.13
  90.3 0.1 collective-permute-start.7
  90.3 8.0 %collective-permute-done.7.b = bf16[352,256]{1,0:T(8,128)(2,1)S(1)} collective-permute-done((bf16[352,256]{1,0:T(8,128)(2,1)S(1)}, bf16[352,256]{1,0:T(8,128)(2,1)S(1)}, u32[]{:S(2)}, u32[]{:S(2)}) %collective-permute-start.7) | collective-permute-done | bytes 180256 | tf_op jit(solution)/shard_map/ppermute | solution.py:794
  98.3 0.9 collective-permute-done.13.refs_1_.refs_3_
  99.2 4.6 %collective-permute-done.19.refs_3_ = bf16[2,11,16,1024]{3,2,1,0:T(8,128)(2,1)S(1)} collective-permute-done((bf16[2,11,16,1024]{3,2,1,0:T(8,128)(2,1)S(1)}, bf16[2,11,16,1024]{3,2,1,0:T(8,128)(2,1)S(1)}, u32[]{:S(2)}, u32[]{:S(2)}) %collective-permute-start.19) | collective-permute-done | bytes 720928 | tf_op jit(solution)/shard_map/ppermute | solution.py:799
  103.8 0.2 add_half.3
  104.1 0.2 collective-permute-start.20
  104.4 1.5 %collective-permute-start.8 = (bf16[352,256]{1,0:T(8,128)(2,1)S(1)}, bf16[352,256]{1,0:T(8,128)(2,1)S(1)}, u32[]{:S(2)}, u32[]{:S(2)}) collective-permute-start(bf16[352,256]{1,0:T(8,128)(2,1)S(1)} %add_actor.9.own.refs_0_), channel_id=1, source_target_pairs={{0,1},{1,0},{2,3},{3,2},{4,5},{5,4},{6,7},{7,6},{8,9},{9,8},{10,11... | collective-permute-start | bytes 540680 | tf_op jit(solution)/shard_map/ppermute | solution.py:794
  106.7 0.1 pad_maximum_fusion.1.factors
  106.8 0.2 collective-permute-done.8.peer
  107.0 2.4 %actor_update.1 = (f32[666,256]{1,0:T(8,128)}, f32[666,256]{1,0:T(8,128)}, f32[666,256]{1,0:T(8,128)}, f32[8,128]{1,0:T(8,128)S(1)}) custom-call(s32[1]{0:T(128)} %bitcast.me.refs_1_, f32[2]{0:T(128)S(1)} %pad_maximum_fusion.1.factors, bf16[352,256]{1,0:T(8,128)(2,1)S(1)} %add_actor.9.own.refs_0_, bf16[352,256]{1,0:T(8,128)(2,1)S(1)} %collective-permute-done.8.peer, ...), custom_call_target="tpu_custom_call" | custom-call | flops 2000000 | bytes 5000000 | tf_op jit(solution)/shard_map/actor_update/pallas_call | solution.py:748
  109.3 1.4 %collective-permute-done.20.refs_5_ = bf16[11,16,1024]{2,1,0:T(8,128)(2,1)S(1)} collective-permute-done((bf16[11,16,1024]{2,1,0:T(8,128)(2,1)S(1)}, bf16[11,16,1024]{2,1,0:T(8,128)(2,1)S(1)}, u32[]{:S(2)}, u32[]{:S(2)}) %collective-permute-start.20) | collective-permute-done | bytes 360480 | tf_op jit(solution)/shard_map/ppermute | solution.py:799
  110.8 0.4 add_line.1
  111.1 0.2 collective-permute-start.21
  111.4 2.4 %collective-permute-start.23 = (bf16[5,16,1024]{2,1,0:T(8,128)(2,1)S(1)}, bf16[5,16,1024]{2,1,0:T(8,128)(2,1)S(1)}, u32[]{:S(2)}, u32[]{:S(2)}) collective-permute-start(bf16[5,16,1024]{2,1,0:T(8,128)(2,1)S(1)} %get-tuple-element.137), channel_id=1, source_target_pairs={{0,24},{1,25},{2,26},{3,27},{4,28},{5,29},{6,30},{7,31},{8,16},{9,... | collective-permute-start | bytes 491528 | tf_op jit(solution)/shard_map/ppermute | solution.py:794
  113.8 1.5 %collective-permute-done.21.refs_1_ = bf16[5,16,1024]{2,1,0:T(8,128)(2,1)S(1)} collective-permute-done((bf16[5,16,1024]{2,1,0:T(8,128)(2,1)S(1)}, bf16[5,16,1024]{2,1,0:T(8,128)(2,1)S(1)}, u32[]{:S(2)}, u32[]{:S(2)}) %collective-permute-start.21) | collective-permute-done | bytes 163872 | tf_op jit(solution)/shard_map/ppermute | solution.py:794
  115.4 3.0 %collective-permute-done.22.refs_2_ = bf16[5,16,1024]{2,1,0:T(8,128)(2,1)S(1)} collective-permute-done((bf16[5,16,1024]{2,1,0:T(8,128)(2,1)S(1)}, bf16[5,16,1024]{2,1,0:T(8,128)(2,1)S(1)}, u32[]{:S(2)}, u32[]{:S(2)}) %collective-permute-start.22) | collective-permute-done | bytes 163872 | tf_op jit(solution)/shard_map/ppermute | solution.py:794
  118.4 9.5 %collective-permute-done.23.refs_3_ = bf16[5,16,1024]{2,1,0:T(8,128)(2,1)S(1)} collective-permute-done((bf16[5,16,1024]{2,1,0:T(8,128)(2,1)S(1)}, bf16[5,16,1024]{2,1,0:T(8,128)(2,1)S(1)}, u32[]{:S(2)}, u32[]{:S(2)}) %collective-permute-start.23) | collective-permute-done | bytes 163872 | tf_op jit(solution)/shard_map/ppermute | solution.py:794
  127.9 0.1 sum_row.1.row_own
  128.0 1.6 %collective-permute-start.24 = (f32[8,128]{1,0:T(8,128)S(1)}, f32[8,128]{1,0:T(8,128)S(1)}, u32[]{:S(2)}, u32[]{:S(2)}) collective-permute-start(f32[8,128]{1,0:T(8,128)S(1)} %sum_row.1.row_own), channel_id=1, source_target_pairs={{0,1},{1,0},{2,3},{3,2},{4,5},{5,4},{6,7},{7,6},{8,9},{9,8},{10,11... | collective-permute-start | bytes 12296 | tf_op jit(solution)/shard_map/ppermute | solution.py:794
  131.0 1.8 %update.1 = (f32[80,393]{1,0:T(8,128)}, f32[80,393]{1,0:T(8,128)}, f32[80,393]{1,0:T(8,128)}, f32[80,512]{1,0:T(8,128)}, f32[80,512]{1,0:T(8,128)}, /*index=5*/f...) custom-call(f32[2]{0:T(128)S(1)} %pad_maximum_fusion.1.factors, ...), custom_call_target="tpu_custom_call" | custom-call | flops 2000000 | bytes 6000000 | tf_op jit(solution)/shard_map/update/pallas_call | solution.py:725
  132.8 1.2 small_update.1
  (83 shorter events, 0.5 us)
Async XLA Ops:
  1.4 4.6 %collective-permute-start.2 = (bf16[32,1024]{1,0:T(8,128)(2,1)S(1)}, bf16[32,1024]{1,0:T(8,128)(2,1)S(1)}, u32[]{:S(2)}, u32[]{:S(2)}) collective-permute-start(bf16[32,1024]{1,0:T(8,128)(2,1)S(1)} %pad_maximum_fusion.own), channel_id=1, source_target_pairs={{0,3},{1,2},{2,1},{3,0},{4,7},{5,6},{6,5},{7,4},{8,11},{9,10},{10,... | collective-permute-start | bytes 196616 | tf_op jit(solution)/shard_map/ppermute | solution.py:844
  3.2 4.1 %collective-permute-start.1 = (bf16[32,1024]{1,0:T(8,128)(2,1)S(1)}, bf16[32,1024]{1,0:T(8,128)(2,1)S(1)}, u32[]{:S(2)}, u32[]{:S(2)}) collective-permute-start(bf16[32,1024]{1,0:T(8,128)(2,1)S(1)} %pad_maximum_fusion.own), channel_id=1, source_target_pairs={{0,2},{1,3},{2,0},{3,1},{4,6},{5,7},{6,4},{7,5},{8,10},{9,11},{10,... | collective-permute-start | bytes 196616 | tf_op jit(solution)/shard_map/ppermute | solution.py:844
  3.5 3.9 %collective-permute-start = (bf16[32,1024]{1,0:T(8,128)(2,1)S(1)}, bf16[32,1024]{1,0:T(8,128)(2,1)S(1)}, u32[]{:S(2)}, u32[]{:S(2)}) collective-permute-start(bf16[32,1024]{1,0:T(8,128)(2,1)S(1)} %pad_maximum_fusion.own), channel_id=1, source_target_pairs={{0,1},{1,0},{2,3},{3,2},{4,5},{5,4},{6,7},{7,6},{8,9},{9,8},{10,11... | collective-permute-start | bytes 196616 | tf_op jit(solution)/shard_map/ppermute | solution.py:844
  7.4 0.7 copy-start.35
  8.0 1.9 %copy-start.20 = (bf16[4096,376]{0,1:T(8,128)(2,1)S(1)}, bf16[4096,376]{0,1:T(8,128)(2,1)}, u32[]{:S(2)}) copy-start(bf16[4096,376]{0,1:T(8,128)(2,1)} %param.45) | copy-start | bytes 9240580
  8.0 2.7 %copy-start.22 = (bf16[512,2560]{1,0:T(8,128)(2,1)S(1)}, bf16[512,2560]{1,0:T(8,128)(2,1)}, u32[]{:S(2)}) copy-start(bf16[512,2560]{1,0:T(8,128)(2,1)} %second.13) | copy-start | bytes 7864324
  8.0 3.3 %copy-start.25 = (bf16[393,2560]{1,0:T(8,128)(2,1)S(1)}, bf16[393,2560]{1,0:T(8,128)(2,1)}, u32[]{:S(2)}) copy-start(bf16[393,2560]{1,0:T(8,128)(2,1)} %first.13) | copy-start | bytes 6036484
  8.0 3.4 %copy-start.26 = (bf16[1024,376]{0,1:T(8,128)(2,1)S(1)}, bf16[1024,376]{0,1:T(8,128)(2,1)}, u32[]{:S(2)}) copy-start(bf16[1024,376]{0,1:T(8,128)(2,1)} %param.42) | copy-start | bytes 2310148
  8.0 3.5 %copy-start.27 = (f32[4096,17]{0,1:T(8,128)S(1)}, f32[4096,17]{0,1:T(8,128)}, u32[]{:S(2)}) copy-start(f32[4096,17]{0,1:T(8,128)} %param.46) | copy-start | bytes 835588
  8.0 3.6 %copy-start.28 = (bf16[666,256]{1,0:T(8,128)(2,1)S(1)}, bf16[666,256]{1,0:T(8,128)(2,1)}, u32[]{:S(2)}) copy-start(bf16[666,256]{1,0:T(8,128)(2,1)} %actor.1) | copy-start | bytes 1022980
  8.0 3.6 %copy-start.29 = (f32[1024,17]{0,1:T(8,128)S(1)}, f32[1024,17]{0,1:T(8,128)}, u32[]{:S(2)}) copy-start(f32[1024,17]{0,1:T(8,128)} %param.44) | copy-start | bytes 208900
  8.1 3.6 %copy-start.30 = (bf16[1024,17]{0,1:T(8,128)(2,1)S(1)}, bf16[1024,17]{0,1:T(8,128)(2,1)}, u32[]{:S(2)}) copy-start(bf16[1024,17]{0,1:T(8,128)(2,1)} %param.43) | copy-start | bytes 104452
  8.1 3.6 %copy-start.32 = (f32[2,2560]{1,0:T(2,128)S(1)}, f32[2,2560]{1,0:T(2,128)}, u32[]{:S(2)}) copy-start(f32[2,2560]{1,0:T(2,128)} %bias.13) | copy-start | bytes 61444
  11.6 17.2 %copy-start.21 = (bf16[512,2560]{1,0:T(8,128)(2,1)S(1)}, bf16[512,2560]{1,0:T(8,128)(2,1)}, u32[]{:S(2)}) copy-start(bf16[512,2560]{1,0:T(8,128)(2,1)} %second.8) | copy-start | bytes 7864324
  11.6 17.2 %copy-start.23 = (s32[4096,125]{1,0:T(8,128)S(1)}, s32[4096,125]{1,0:T(8,128)}, u32[]{:S(2)}) copy-start(s32[4096,125]{1,0:T(8,128)} %order_in.1) | copy-start | bytes 6144004
  11.7 17.2 %copy-start.24 = (bf16[393,2560]{1,0:T(8,128)(2,1)S(1)}, bf16[393,2560]{1,0:T(8,128)(2,1)}, u32[]{:S(2)}) copy-start(bf16[393,2560]{1,0:T(8,128)(2,1)} %first.8) | copy-start | bytes 6036484
  11.7 17.2 %copy-start.31 = (f32[2,2560]{1,0:T(2,128)S(1)}, f32[2,2560]{1,0:T(2,128)}, u32[]{:S(2)}) copy-start(f32[2,2560]{1,0:T(2,128)} %bias.8) | copy-start | bytes 61444
  11.7 17.2 %copy-start.33 = (f32[4096]{0:T(1024)S(1)}, f32[4096]{0:T(1024)}, u32[]{:S(2)}) copy-start(f32[4096]{0:T(1024)} %param.47) | copy-start | bytes 49156
  11.7 17.2 %copy-start.34 = (s32[4096]{0:T(1024)S(1)}, s32[4096]{0:T(1024)}, u32[]{:S(2)}) copy-start(s32[4096]{0:T(1024)} %param.48) | copy-start | bytes 49156
  28.2 10.1 %collective-permute-start.3 = (bf16[352,256]{1,0:T(8,128)(2,1)S(1)}, bf16[352,256]{1,0:T(8,128)(2,1)S(1)}, u32[]{:S(2)}, u32[]{:S(2)}) collective-permute-start(bf16[352,256]{1,0:T(8,128)(2,1)S(1)} %get-tuple-element.94), channel_id=1, source_target_pairs={{0,1},{1,0},{2,3},{3,2},{4,5},{5,4},{6,7},{7,6},{8,9},{9,8},{10,11... | collective-permute-start | bytes 540680 | tf_op jit(solution)/shard_map/ppermute | solution.py:794
  38.4 9.3 %collective-permute-start.4 = (bf16[352,256]{1,0:T(8,128)(2,1)S(1)}, bf16[352,256]{1,0:T(8,128)(2,1)S(1)}, u32[]{:S(2)}, u32[]{:S(2)}) collective-permute-start(bf16[352,256]{1,0:T(8,128)(2,1)S(1)} %add_actor.5.a.refs_0_), channel_id=1, source_target_pairs={{0,2},{1,3},{2,0},{3,1},{4,6},{5,7},{6,4},{7,5},{8,10},{9,11},{10,... | collective-permute-start | bytes 540680 | tf_op jit(solution)/shard_map/ppermute | solution.py:794
  47.3 27.4 %collective-permute-start.9 = (bf16[18,16,1024]{2,1,0:T(8,128)(2,1)S(1)}, bf16[18,16,1024]{2,1,0:T(8,128)(2,1)S(1)}, u32[]{:S(2)}, u32[]{:S(2)}) collective-permute-start(bf16[18,16,1024]{2,1,0:T(8,128)(2,1)S(1)} %get-tuple-element.110), channel_id=1, source_target_pairs={{0,1},{1,0},{2,3},{3,2},{4,5},{5,4},{6,7},{7,6},{8,9},{9,8},{10,11... | collective-permute-start | bytes 1769480 | tf_op jit(solution)/shard_map/ppermute | solution.py:794
  47.8 9.5 %collective-permute-start.5 = (bf16[352,256]{1,0:T(8,128)(2,1)S(1)}, bf16[352,256]{1,0:T(8,128)(2,1)S(1)}, u32[]{:S(2)}, u32[]{:S(2)}) collective-permute-start(bf16[352,256]{1,0:T(8,128)(2,1)S(1)} %add_actor.6.a.refs_0_), channel_id=1, source_target_pairs={{0,4},{1,5},{2,6},{3,7},{4,0},{5,1},{6,2},{7,3},{8,12},{9,13},{10,... | collective-permute-start | bytes 540680 | tf_op jit(solution)/shard_map/ppermute | solution.py:794
  56.8 17.9 %collective-permute-start.10 = (bf16[18,16,1024]{2,1,0:T(8,128)(2,1)S(1)}, bf16[18,16,1024]{2,1,0:T(8,128)(2,1)S(1)}, u32[]{:S(2)}, u32[]{:S(2)}) collective-permute-start(bf16[18,16,1024]{2,1,0:T(8,128)(2,1)S(1)} %get-tuple-element.111), channel_id=1, source_target_pairs={{0,1},{1,0},{2,3},{3,2},{4,5},{5,4},{6,7},{7,6},{8,9},{9,8},{10,11... | collective-permute-start | bytes 1769480 | tf_op jit(solution)/shard_map/ppermute | solution.py:794
  57.4 9.4 %collective-permute-start.6 = (bf16[352,256]{1,0:T(8,128)(2,1)S(1)}, bf16[352,256]{1,0:T(8,128)(2,1)S(1)}, u32[]{:S(2)}, u32[]{:S(2)}) collective-permute-start(bf16[352,256]{1,0:T(8,128)(2,1)S(1)} %add_actor.7.a.refs_0_), channel_id=1, source_target_pairs={{0,8},{1,9},{2,10},{3,11},{4,12},{5,13},{6,14},{7,15},{8,0},{9,1},... | collective-permute-start | bytes 540680 | tf_op jit(solution)/shard_map/ppermute | solution.py:794
  66.4 8.4 %collective-permute-start.11 = (bf16[18,16,1024]{2,1,0:T(8,128)(2,1)S(1)}, bf16[18,16,1024]{2,1,0:T(8,128)(2,1)S(1)}, u32[]{:S(2)}, u32[]{:S(2)}) collective-permute-start(bf16[18,16,1024]{2,1,0:T(8,128)(2,1)S(1)} %get-tuple-element.112), channel_id=1, source_target_pairs={{0,1},{1,0},{2,3},{3,2},{4,5},{5,4},{6,7},{7,6},{8,9},{9,8},{10,11... | collective-permute-start | bytes 1769480 | tf_op jit(solution)/shard_map/ppermute | solution.py:794
  66.8 7.9 %copy-start.16 = (s32[160]{0:T(256)S(1)}, s32[160]{0:T(256)}, u32[]{:S(2)}) copy-start(s32[160]{0:T(256)} %constant.21.clone.places) | copy-start | bytes 1924
  74.5 13.8 %collective-permute-start.14 = (bf16[18,16,1024]{2,1,0:T(8,128)(2,1)S(1)}, bf16[18,16,1024]{2,1,0:T(8,128)(2,1)S(1)}, u32[]{:S(2)}, u32[]{:S(2)}) collective-permute-start(bf16[18,16,1024]{2,1,0:T(8,128)(2,1)S(1)} %get-tuple-element.125), channel_id=1, source_target_pairs={{0,1},{1,0},{2,3},{3,2},{4,5},{5,4},{6,7},{7,6},{8,9},{9,8},{10,11... | collective-permute-start | bytes 1769480 | tf_op jit(solution)/shard_map/ppermute | solution.py:794
  76.3 9.8 %collective-permute-start.12 = (bf16[2,10,16,1024]{3,2,1,0:T(8,128)(2,1)S(1)}, bf16[2,10,16,1024]{3,2,1,0:T(8,128)(2,1)S(1)}, u32[]{:S(2)}, u32[]{:S(2)}) collective-permute-start(bf16[2,10,16,1024]{3,2,1,0:T(8,128)(2,1)S(1)} %get-tuple-element.114), channel_id=1, source_target_pairs={{0,2},{1,5},{2,0},{3,7},{4,6},{5,1},{6,4},{7,3},{8,10},{9,13},{10,... | collective-permute-start | bytes 1966088 | tf_op jit(solution)/shard_map/ppermute | solution.py:799
  76.5 11.7 %copy-start.15 = (s32[160]{0:T(256)S(1)}, s32[160]{0:T(256)}, u32[]{:S(2)}) copy-start(s32[160]{0:T(256)} %constant.22.clone.places) | copy-start | bytes 1924
  84.4 3.8 %collective-permute-start.15 = (bf16[6,16,1024]{2,1,0:T(8,128)(2,1)S(1)}, bf16[6,16,1024]{2,1,0:T(8,128)(2,1)S(1)}, u32[]{:S(2)}, u32[]{:S(2)}) collective-permute-start(bf16[6,16,1024]{2,1,0:T(8,128)(2,1)S(1)} %get-tuple-element.126), channel_id=1, source_target_pairs={{0,1},{1,0},{2,3},{3,2},{4,5},{5,4},{6,7},{7,6},{8,9},{9,8},{10,11... | collective-permute-start | bytes 589832 | tf_op jit(solution)/shard_map/ppermute | solution.py:794
  85.1 3.2 %collective-permute-start.16 = (bf16[6,16,1024]{2,1,0:T(8,128)(2,1)S(1)}, bf16[6,16,1024]{2,1,0:T(8,128)(2,1)S(1)}, u32[]{:S(2)}, u32[]{:S(2)}) collective-permute-start(bf16[6,16,1024]{2,1,0:T(8,128)(2,1)S(1)} %get-tuple-element.127), channel_id=1, source_target_pairs={{0,1},{1,0},{2,3},{3,2},{4,5},{5,4},{6,7},{7,6},{8,9},{9,8},{10,11... | collective-permute-start | bytes 589832 | tf_op jit(solution)/shard_map/ppermute | solution.py:794
  85.1 3.1 %collective-permute-start.17 = (bf16[6,16,1024]{2,1,0:T(8,128)(2,1)S(1)}, bf16[6,16,1024]{2,1,0:T(8,128)(2,1)S(1)}, u32[]{:S(2)}, u32[]{:S(2)}) collective-permute-start(bf16[6,16,1024]{2,1,0:T(8,128)(2,1)S(1)} %get-tuple-element.128), channel_id=1, source_target_pairs={{0,1},{1,0},{2,3},{3,2},{4,5},{5,4},{6,7},{7,6},{8,9},{9,8},{10,11... | collective-permute-start | bytes 589832 | tf_op jit(solution)/shard_map/ppermute | solution.py:794
  86.0 2.2 %collective-permute-start.18 = (bf16[4,16,1024]{2,1,0:T(8,128)(2,1)S(1)}, bf16[4,16,1024]{2,1,0:T(8,128)(2,1)S(1)}, u32[]{:S(2)}, u32[]{:S(2)}) collective-permute-start(bf16[4,16,1024]{2,1,0:T(8,128)(2,1)S(1)} %get-tuple-element.129), channel_id=1, source_target_pairs={{0,1},{1,0},{2,3},{3,2},{4,5},{5,4},{6,7},{7,6},{8,9},{9,8},{10,11... | collective-permute-start | bytes 393224 | tf_op jit(solution)/shard_map/ppermute | solution.py:794
  88.3 18.7 %copy-start = (f32[666,256]{1,0:T(8,128)S(1)}, f32[666,256]{1,0:T(8,128)}, u32[]{:S(2)}) copy-start(f32[666,256]{1,0:T(8,128)} %refs_0_.2) | copy-start | bytes 2045956
  88.3 18.7 %copy-start.1 = (f32[666,256]{1,0:T(8,128)S(1)}, f32[666,256]{1,0:T(8,128)}, u32[]{:S(2)}) copy-start(f32[666,256]{1,0:T(8,128)} %refs_1_.2) | copy-start | bytes 2045956
  88.3 18.7 %copy-start.2 = (f32[666,256]{1,0:T(8,128)S(1)}, f32[666,256]{1,0:T(8,128)}, u32[]{:S(2)}) copy-start(f32[666,256]{1,0:T(8,128)} %refs_2_.2) | copy-start | bytes 2045956
  89.8 14.0 %collective-permute-start.19 = (bf16[2,11,16,1024]{3,2,1,0:T(8,128)(2,1)S(1)}, bf16[2,11,16,1024]{3,2,1,0:T(8,128)(2,1)S(1)}, u32[]{:S(2)}, u32[]{:S(2)}) collective-permute-start(bf16[2,11,16,1024]{3,2,1,0:T(8,128)(2,1)S(1)} %get-tuple-element.131), channel_id=1, source_target_pairs={{0,2},{1,5},{2,0},{3,7},{4,6},{5,1},{6,4},{7,3},{8,10},{9,13},{10,... | collective-permute-start | bytes 2162696 | tf_op jit(solution)/shard_map/ppermute | solution.py:799
  90.1 9.2 %collective-permute-start.13 = (bf16[10,16,1024]{2,1,0:T(8,128)(2,1)S(1)}, bf16[10,16,1024]{2,1,0:T(8,128)(2,1)S(1)}, u32[]{:S(2)}, u32[]{:S(2)}) collective-permute-start(bf16[10,16,1024]{2,1,0:T(8,128)(2,1)S(1)} %get-tuple-element.116), channel_id=1, source_target_pairs={{0,4},{1,3},{2,6},{3,1},{4,0},{5,7},{6,2},{7,5},{8,12},{9,11},{10,... | collective-permute-start | bytes 983048 | tf_op jit(solution)/shard_map/ppermute | solution.py:799
  90.3 8.0 %collective-permute-start.7 = (bf16[352,256]{1,0:T(8,128)(2,1)S(1)}, bf16[352,256]{1,0:T(8,128)(2,1)S(1)}, u32[]{:S(2)}, u32[]{:S(2)}) collective-permute-start(bf16[352,256]{1,0:T(8,128)(2,1)S(1)} %add_actor.8.a.refs_0_), channel_id=1, source_target_pairs={{0,16},{1,17},{2,18},{3,19},{4,20},{5,21},{6,22},{7,23},{8,24},{9,... | collective-permute-start | bytes 540680 | tf_op jit(solution)/shard_map/ppermute | solution.py:794
  104.0 26.9 %copy-start.3 = (f32[393,80]{0,1:T(8,128)S(1)}, f32[393,80]{0,1:T(8,128)}, u32[]{:S(2)}) copy-start(f32[393,80]{0,1:T(8,128)} %param.61) | copy-start | bytes 377284
  104.0 26.9 %copy-start.4 = (f32[393,80]{0,1:T(8,128)S(1)}, f32[393,80]{0,1:T(8,128)}, u32[]{:S(2)}) copy-start(f32[393,80]{0,1:T(8,128)} %param.62) | copy-start | bytes 377284
  104.0 26.9 %copy-start.5 = (f32[393,80]{0,1:T(8,128)S(1)}, f32[393,80]{0,1:T(8,128)}, u32[]{:S(2)}) copy-start(f32[393,80]{0,1:T(8,128)} %param.63) | copy-start | bytes 377284
  104.0 26.9 %copy-start.6 = (f32[512,80]{0,1:T(8,128)S(1)}, f32[512,80]{0,1:T(8,128)}, u32[]{:S(2)}) copy-start(f32[512,80]{0,1:T(8,128)} %param.64) | copy-start | bytes 491524
  104.0 26.9 %copy-start.7 = (f32[512,80]{0,1:T(8,128)S(1)}, f32[512,80]{0,1:T(8,128)}, u32[]{:S(2)}) copy-start(f32[512,80]{0,1:T(8,128)} %param.65) | copy-start | bytes 491524
  104.0 26.9 %copy-start.8 = (f32[512,80]{0,1:T(8,128)S(1)}, f32[512,80]{0,1:T(8,128)}, u32[]{:S(2)}) copy-start(f32[512,80]{0,1:T(8,128)} %param.66) | copy-start | bytes 491524
  104.1 26.9 %copy-start.9 = (f32[64,32]{0,1:T(8,128)S(1)}, f32[64,32]{0,1:T(8,128)}, u32[]{:S(2)}) copy-start(f32[64,32]{0,1:T(8,128)} %param.70) | copy-start | bytes 24580
  104.1 26.9 %copy-start.10 = (f32[64,32]{0,1:T(8,128)S(1)}, f32[64,32]{0,1:T(8,128)}, u32[]{:S(2)}) copy-start(f32[64,32]{0,1:T(8,128)} %param.71) | copy-start | bytes 24580
  104.1 26.9 %copy-start.11 = (f32[64,32]{0,1:T(8,128)S(1)}, f32[64,32]{0,1:T(8,128)}, u32[]{:S(2)}) copy-start(f32[64,32]{0,1:T(8,128)} %param.72) | copy-start | bytes 24580
  104.1 26.9 %copy-start.17 = (f32[2,80]{1,0:T(2,128)S(1)}, f32[2,80]{1,0:T(2,128)}, u32[]{:S(2)}) copy-start(f32[2,80]{1,0:T(2,128)} %refs_10_.1) | copy-start | bytes 1924
  104.1 26.9 %copy-start.18 = (f32[2,80]{1,0:T(2,128)S(1)}, f32[2,80]{1,0:T(2,128)}, u32[]{:S(2)}) copy-start(f32[2,80]{1,0:T(2,128)} %refs_11_.1) | copy-start | bytes 1924
  104.1 26.9 %copy-start.19 = (f32[2,80]{1,0:T(2,128)S(1)}, f32[2,80]{1,0:T(2,128)}, u32[]{:S(2)}) copy-start(f32[2,80]{1,0:T(2,128)} %refs_12_.1) | copy-start | bytes 1924
  104.1 6.6 %collective-permute-start.20 = (bf16[11,16,1024]{2,1,0:T(8,128)(2,1)S(1)}, bf16[11,16,1024]{2,1,0:T(8,128)(2,1)S(1)}, u32[]{:S(2)}, u32[]{:S(2)}) collective-permute-start(bf16[11,16,1024]{2,1,0:T(8,128)(2,1)S(1)} %get-tuple-element.133), channel_id=1, source_target_pairs={{0,4},{1,3},{2,6},{3,1},{4,0},{5,7},{6,2},{7,5},{8,12},{9,11},{10,... | collective-permute-start | bytes 1081352 | tf_op jit(solution)/shard_map/ppermute | solution.py:799
  104.4 2.6 %collective-permute-start.8 = (bf16[352,256]{1,0:T(8,128)(2,1)S(1)}, bf16[352,256]{1,0:T(8,128)(2,1)S(1)}, u32[]{:S(2)}, u32[]{:S(2)}) collective-permute-start(bf16[352,256]{1,0:T(8,128)(2,1)S(1)} %add_actor.9.own.refs_0_), channel_id=1, source_target_pairs={{0,1},{1,0},{2,3},{3,2},{4,5},{5,4},{6,7},{7,6},{8,9},{9,8},{10,11... | collective-permute-start | bytes 540680 | tf_op jit(solution)/shard_map/ppermute | solution.py:794
  106.8 26.0 %copy-start.12 = (f32[674]{0:T(1024)S(1)}, f32[674]{0:T(1024)}, u32[]{:S(2)}) copy-start(f32[674]{0:T(1024)} %refs_0_.3) | copy-start | bytes 8092
  106.8 26.0 %copy-start.13 = (f32[674]{0:T(1024)S(1)}, f32[674]{0:T(1024)}, u32[]{:S(2)}) copy-start(f32[674]{0:T(1024)} %refs_1_.3) | copy-start | bytes 8092
  106.8 26.0 %copy-start.14 = (f32[674]{0:T(1024)S(1)}, f32[674]{0:T(1024)}, u32[]{:S(2)}) copy-start(f32[674]{0:T(1024)} %refs_2_.3) | copy-start | bytes 8092
  111.1 4.2 %collective-permute-start.21 = (bf16[5,16,1024]{2,1,0:T(8,128)(2,1)S(1)}, bf16[5,16,1024]{2,1,0:T(8,128)(2,1)S(1)}, u32[]{:S(2)}, u32[]{:S(2)}) collective-permute-start(bf16[5,16,1024]{2,1,0:T(8,128)(2,1)S(1)} %get-tuple-element.135), channel_id=1, source_target_pairs={{0,8},{1,9},{2,10},{3,11},{4,12},{5,13},{6,14},{7,15},{8,0},{9,1},... | collective-permute-start | bytes 491528 | tf_op jit(solution)/shard_map/ppermute | solution.py:794
  111.4 7.0 %collective-permute-start.22 = (bf16[5,16,1024]{2,1,0:T(8,128)(2,1)S(1)}, bf16[5,16,1024]{2,1,0:T(8,128)(2,1)S(1)}, u32[]{:S(2)}, u32[]{:S(2)}) collective-permute-start(bf16[5,16,1024]{2,1,0:T(8,128)(2,1)S(1)} %get-tuple-element.136), channel_id=1, source_target_pairs={{0,16},{1,17},{2,18},{3,19},{4,20},{5,21},{6,22},{7,23},{8,24},{9,... | collective-permute-start | bytes 491528 | tf_op jit(solution)/shard_map/ppermute | solution.py:794
  111.4 16.5 %collective-permute-start.23 = (bf16[5,16,1024]{2,1,0:T(8,128)(2,1)S(1)}, bf16[5,16,1024]{2,1,0:T(8,128)(2,1)S(1)}, u32[]{:S(2)}, u32[]{:S(2)}) collective-permute-start(bf16[5,16,1024]{2,1,0:T(8,128)(2,1)S(1)} %get-tuple-element.137), channel_id=1, source_target_pairs={{0,24},{1,25},{2,26},{3,27},{4,28},{5,29},{6,30},{7,31},{8,16},{9,... | collective-permute-start | bytes 491528 | tf_op jit(solution)/shard_map/ppermute | solution.py:794
  128.0 4.8 %collective-permute-start.24 = (f32[8,128]{1,0:T(8,128)S(1)}, f32[8,128]{1,0:T(8,128)S(1)}, u32[]{:S(2)}, u32[]{:S(2)}) collective-permute-start(f32[8,128]{1,0:T(8,128)S(1)} %sum_row.1.row_own), channel_id=1, source_target_pairs={{0,1},{1,0},{2,3},{3,2},{4,5},{5,4},{6,7},{7,6},{8,9},{9,8},{10,11... | collective-permute-start | bytes 12296 | tf_op jit(solution)/shard_map/ppermute | solution.py:794
where the time goes:
time: 134 us
  Pallas kernels  74.3 us (55%)
  waiting for transfers between devices  32.7 us (24%)
  starting transfers between devices  17.6 us (13%)
  local copies, waits for them, and re-layouts  4.71 us (4%)
  between operations  3.92 us (3%)
    pallas_call x5, Pallas kernels, critic_pass(): pl.pallas_call(functools.partial(critic_kernel, e, len(after), rows_scale...  38.4 us
    ppermute x18, waiting for transfers between devices, exchange(): return lax.ppermute(value, AXES, [(i, i ^ flip) for i in range(count)])  23 us
    pallas_call x1, Pallas kernels, pilot_pass(): pl.pallas_call(functools.partial(pilot_kernel, level, share), in_specs=[S...  16.5 us
    ppermute x18, starting transfers between devices, exchange(): return lax.ppermute(value, AXES, [(i, i ^ flip) for i in range(count)])  14.4 us
    pallas_call x1, Pallas kernels, target_pass(): pl.pallas_call(target_kernel, in_specs=[SCALAR] * 2 + [WHOLE] * 4 + [pl.B...  9.45 us
    ppermute x4, waiting for transfers between devices, exchange_sides(): lax.ppermute(value, AXES, [(i, i ^ (odd if i % 2 else even)) for i in ran...  7.37 us
    unnamed x72, local copies, waits for them, and re-layouts  4.01 us
    pallas_call x2, Pallas kernels, add_core(): pl.pallas_call(functools.partial(core_kernel, chunk, depth, len(after)),...  3.02 us
  transfers between devices with their start and end apart: 25, of which 12 were waited for; matrix products, arithmetic and copies ran while one was open for 1% of the time, Pallas kernels for 40%

commit v1 on v0

--- a/solution.py
+++ b/solution.py
@@ -25,7 +25,8 @@
 SMALL_VEC = 674
 LANES = 1024
 EXTRA = 128
-TILE = 512
+TILE = 1024
+CRITIC_TILE = 512
 MiB = 1024 * 1024
 
 DISCOUNT = 0.99
@@ -104,37 +105,37 @@
     return g_one, g_two, scaled, act, logp
 
 
-def heads_kernel(me, own, got_one, got_two, got_three, small, lag_bias, out, bias_out, stage, col):
+def heads_kernel(me, own, got_one, got_two, got_three, out, stage):
     quarter = own.shape[0]
     for k, got in enumerate((own, got_one, got_two, got_three)):
         first = pl.multiple_of((me[0] ^ k) * quarter, quarter)
         stage[pl.ds(first, quarter)] = got[...].astype(F32)
     keep = lax.broadcasted_iota(jnp.int32, (SLOT, 1), 0) < QUANTS
-    bias = small[:, SMALL_VEC - PADDED :]
-    both = jnp.concatenate([bias, lag_bias[...], jnp.zeros((6, PADDED), F32)], 0)
+    for e in range(CRITICS):
+        out[e] = jnp.where(keep, stage[e * QUANTS : e * QUANTS + SLOT], 0.0).astype(BF)
+
+
+def heads(me, own, got):
+    return pl.pallas_call(
+        heads_kernel,
+        in_specs=[SCALAR] + [WHOLE] * 4,
+        out_specs=WHOLE,
+        out_shape=jax.ShapeDtypeStruct((CRITICS, SLOT, 2 * HIDDEN_SIZE), BF),
+        scratch_shapes=[pltpu.VMEM((136, 2 * HIDDEN_SIZE), F32)],
+        compiler_params=params(4),
+        cost_estimate=cost(3e10, 1e6),
+        name="heads",
+    )(me, own, *got)
+
+
+def fill_biases(small, lag_bias, out, col):
+    keep = lax.broadcasted_iota(jnp.int32, (SLOT, 1), 0) < QUANTS
+    both = jnp.concatenate([small[:, SMALL_VEC - PADDED :], lag_bias[...], jnp.zeros((6, PADDED), F32)], 0)
     col[:PADDED] = jnp.transpose(both)
     for e in range(CRITICS):
-        rows = pl.ds(e * QUANTS, SLOT)
-        out[e] = jnp.where(keep, stage[rows], 0.0).astype(BF)
-        columns = jnp.where(keep, col[rows], 0.0)
+        columns = jnp.where(keep, col[e * QUANTS : e * QUANTS + SLOT], 0.0)
         for net in range(2):
-            bias_out[net, e] = jnp.broadcast_to(columns[:, net : net + 1], (SLOT, PADDED))
-
-
-def heads(me, own, got, small, lag_bias):
-    return pl.pallas_call(
-        heads_kernel,
-        in_specs=[SCALAR] + [WHOLE] * 6,
-        out_specs=[WHOLE, WHOLE],
-        out_shape=[
-            jax.ShapeDtypeStruct((CRITICS, SLOT, 2 * HIDDEN_SIZE), BF),
-            jax.ShapeDtypeStruct((2, CRITICS, SLOT, PADDED), F32),
-        ],
-        scratch_shapes=[pltpu.VMEM((136, 2 * HIDDEN_SIZE), F32), pltpu.VMEM((136, 8), F32)],
-        compiler_params=params(),
-        cost_estimate=cost(3e10, 1e6),
-        name="heads",
-    )(me, own, *got, small, lag_bias)
+            out[net, e] = jnp.broadcast_to(columns[:, net : net + 1], (SLOT, PADDED))
 
 
 def fill_first(tall, filled, first, bias):
@@ -151,8 +152,8 @@
     filled[body + 32 :] = jnp.zeros((HIDDEN_SIZE - body - 32, HIDDEN_SIZE), BF)
 
 
-def tiles(rows):
-    width = min(rows, TILE)
+def tiles(rows, width=TILE):
+    width = min(rows, width)
     return [pl.ds(i * width, width) for i in range(rows // width)]
 
 
@@ -226,26 +227,32 @@
 
 def pilot_kernel(
     level, share, me, index, heat, obs, next_in, noise, noise_next_in, chosen, actor, small,
-    first, second, bias, head, head_bias,
-    own_out, send_out, x_now, x_target, logp_next,
-    inputs, filled, tall_x, tall_w, dact, total, out_scratch, grad_out, small_out, next_obs, noise_next, sems,
+    first_in, second_in, bias, head, lag_bias,
+    own_out, send_out, x_now, x_target, logp_next, head_bias,
+    inputs, filled, tall_x, tall_w, dact, total, out_scratch, grad_out, small_out, next_obs, noise_next, col,
+    first, second, sems,
 ):
     rows = obs.shape[1]
     mine = pl.ds(pl.multiple_of(index[0] * rows, PADDED), rows)
     copies = [
         pltpu.make_async_copy(next_in.at[:, mine], next_obs, sems.at[0]),
         pltpu.make_async_copy(noise_next_in.at[:, mine], noise_next, sems.at[1]),
+        pltpu.make_async_copy(first_in, first, sems.at[2]),
+        pltpu.make_async_copy(second_in, second, sems.at[3]),
     ]
     for copy in copies:
         copy.start()
     g_one, g_two, scaled, act, logp = actor_layers(obs[...], noise[...], actor, small, out_scratch)
     fill_inputs(tall_x, inputs, obs, act.astype(BF))
     fill_inputs(tall_x, x_now, obs, chosen[...])
-    for copy in copies:
+    for copy in copies[:2]:
         copy.wait()
     _, _, _, next_act, next_logp = actor_layers(next_obs[...], noise_next[...], actor, small, out_scratch)
     fill_inputs(tall_x, x_target, next_obs, next_act.astype(BF))
     logp_next[...] = next_logp
+    fill_biases(small, lag_bias, head_bias, col)
+    for copy in copies[2:]:
+        copy.wait()
 
     dact[...] = jnp.zeros(dact.shape, F32)
     total[...] = jnp.zeros(total.shape, F32)
@@ -306,17 +313,18 @@
 
 def pilot_pass(
     level, share, me, index, heat, obs, next_obs, noise, noise_next, chosen, actor, small,
-    first, second, bias, head, head_bias,
+    first, second, bias, head, lag_bias,
 ):
     rows = obs.shape[1]
     far = pl.BlockSpec(memory_space=pltpu.HBM)
     filled = jax.ShapeDtypeStruct((HIDDEN_SIZE, rows), BF)
     return pl.pallas_call(
         functools.partial(pilot_kernel, level, share),
-        in_specs=[SCALAR] * 3 + [WHOLE, far, WHOLE, far] + [WHOLE] * 8,
-        out_specs=[WHOLE] * 5,
+        in_specs=[SCALAR] * 3 + [WHOLE, far, WHOLE, far] + [WHOLE] * 3 + [far] * 2 + [WHOLE] * 3,
+        out_specs=[WHOLE] * 6,
         out_shape=[jax.ShapeDtypeStruct((HALF + 16, ACTOR_HIDDEN), BF)] * 2
-        + [filled, filled, jax.ShapeDtypeStruct((1, rows), F32)],
+        + [filled, filled, jax.ShapeDtypeStruct((1, rows), F32)]
+        + [jax.ShapeDtypeStruct((2, CRITICS, SLOT, PADDED), F32)],
         scratch_shapes=[
             pltpu.VMEM((HIDDEN_SIZE, rows), BF),
             pltpu.VMEM((HIDDEN_SIZE, HIDDEN_SIZE), BF),
@@ -329,12 +337,15 @@
             pltpu.VMEM((8, PADDED), F32),
             pltpu.VMEM((OBS_DIM, rows), BF),
             pltpu.VMEM((ACT_DIM, rows), F32),
-            pltpu.SemaphoreType.DMA((2,)),
+            pltpu.VMEM((136, 8), F32),
+            pltpu.VMEM(first.shape, BF),
+            pltpu.VMEM(second.shape, BF),
+            pltpu.SemaphoreType.DMA((4,)),
         ],
-        compiler_params=params(24),
+        compiler_params=params(48),
         cost_estimate=cost(14e9, 9e6),
         name="pilot_pass",
-    )(me, index, heat, obs, next_obs, noise, noise_next, chosen, actor, small, first, second, bias, head, head_bias)
+    )(me, index, heat, obs, next_obs, noise, noise_next, chosen, actor, small, first, second, bias, head, lag_bias)
 
 
 def pair_terms(q_ref, lagged, keep, parts, rows):
@@ -413,12 +424,12 @@
     head_bias = head_bias.at[:1, e : e + 1]
     fill_first(tall_w, filled, first[:, lanes], bias[:1, lanes])
     b_two = column(bias[1:2, lanes])
-    for part in tiles(rows):
-        one = jnp.maximum(dot_tn(filled[...], inputs[:, part]), 0.0).astype(BF)
-        h_one[:, part] = one
-        two = jnp.maximum(dot_tn(second[...], one) + b_two, 0.0).astype(BF)
-        h_two[:, part] = two
-        q[:, part] = dot_nn(head[0], two) + head_bias[0, 0, :, :1]
+    for part in tiles(rows, CRITIC_TILE):
+        h_one[:, part] = jnp.maximum(dot_tn(filled[...], inputs[:, part]), 0.0).astype(BF)
+    for part in tiles(rows, CRITIC_TILE):
+        h_two[:, part] = jnp.maximum(dot_tn(second[...], h_one[:, part]) + b_two, 0.0).astype(BF)
+    for part in tiles(rows, CRITIC_TILE):
+        q[:, part] = dot_nn(head[0], h_two[:, part]) + head_bias[0, 0, :, :1]
     terms = pair_terms(q, lagged, keep, parts, rows)
     low = (terms[:SLOT] * -rows_scale).astype(BF)
     loss = terms[SLOT : SLOT + 1]
@@ -426,17 +437,16 @@
     count = jnp.ones((8, rows), BF)
     bias_grad = dot_nt(count, low)[:1]
     sums = jnp.zeros((HIDDEN_SIZE, PADDED), F32)
-    for part in tiles(rows):
+    for part in tiles(rows, CRITIC_TILE):
         two = h_two[:, part]
         dz_two = jnp.where(two > 0, dot_tn(head[0], low[:, part.start : part.start + part.size]), 0.0)
         for i in range(part.size // PADDED):
             sums = sums + dz_two[:, i * PADDED : (i + 1) * PADDED]
-        dz_two = dz_two.astype(BF)
-        h_two[:, part] = dz_two
+        h_two[:, part] = dz_two.astype(BF)
+    second_grad = dot_nt(h_two[...], h_one[...])
+    for part in tiles(rows, CRITIC_TILE):
         one = h_one[:, part]
-        h_one[:, part] = jnp.where(one > 0, dot_nn(second[...], dz_two), 0.0).astype(BF)
-        second_part = dot_nt(dz_two, one)
-        second_grad = second_grad + second_part if part.start else second_part
+        h_one[:, part] = jnp.where(one > 0, dot_nn(second[...], h_two[:, part]), 0.0).astype(BF)
     grads[:, :, :HIDDEN_SIZE] = second_grad.astype(BF).reshape(-1, 16, HIDDEN_SIZE)
     first_grad = dot_nt(h_one[...], inputs[...])
     grads[:, :, HIDDEN_SIZE : LANES - PADDED] = (
@@ -843,12 +853,12 @@
     got = [
         lax.ppermute(own_head, "quant", [(i, i ^ k) for i in range(n_quant)]) for k in (1, 2, 3)
     ]
-    head, head_bias = heads(index, own_head, got, small_row, t_head_bias.reshape(1, -1))
+    head = heads(index, own_head, got)
 
     level = float(np.asarray(-1.0 / (MERGED_SUPPORTS * samples), ml_dtypes.bfloat16))
-    own, send, x_now, x_target, logp = pilot_pass(
+    own, send, x_now, x_target, logp, head_bias = pilot_pass(
         level, 1.0 / samples, me, index, heat, obs.T, next_obs.T, noise_now.T, noise_next.T, chosen.T,
-        actor, small_row, w_one, w_two, biases, head, head_bias,
+        actor, small_row, w_one, w_two, biases, head, t_head_bias.reshape(1, -1),
     )
     lagged, keep = target_pass(
         index, heat, x_target, logp, payoffs.reshape(1, -1), done.reshape(1, -1), order,

time: 134 us -> 128 us (0.955)
  Pallas kernels: 74.3 us -> 70.2 us
  local copies, waits for them, and re-layouts: 4.71 us -> 2.06 us
    unnamed x72 -> x70, local copies, waits for them, and re-layouts: 4.01 us -> 1.37 us
    pallas_call x5, Pallas kernels: 38.4 us -> 36.2 us  [critic_pass(): pl.pallas_call(functools.partial(critic_kernel, e, len(after), rows_scale...]
  transfers between devices with their start and end apart: 25 -> 25, of which waited for: 12 -> 12; matrix products, arithmetic and copies ran while one was open for 1% -> 1% of each run, Pallas kernels for 40% -> 39%
where the time goes in v1:
time: 128 us
  Pallas kernels  70.2 us (55%)
  waiting for transfers between devices  33.1 us (26%)
  starting transfers between devices  17.7 us (14%)
  between operations  3.95 us (3%)
  local copies, waits for them, and re-layouts  2.06 us (2%)
    pallas_call x5, Pallas kernels, critic_pass(): pl.pallas_call(functools.partial(critic_kernel, e, len(after), rows_scale...  36.2 us
    ppermute x18, waiting for transfers between devices, exchange(): return lax.ppermute(value, AXES, [(i, i ^ flip) for i in range(count)])  23 us
    pallas_call x1, Pallas kernels, pilot_pass(): pl.pallas_call(functools.partial(pilot_kernel, level, share), in_specs=[S...  16.2 us
    ppermute x18, starting transfers between devices, exchange(): return lax.ppermute(value, AXES, [(i, i ^ flip) for i in range(count)])  14.5 us
    pallas_call x1, Pallas kernels, target_pass(): pl.pallas_call(target_kernel, in_specs=[SCALAR] * 2 + [WHOLE] * 4 + [pl.B...  8.24 us
    ppermute x4, waiting for transfers between devices, exchange_sides(): lax.ppermute(value, AXES, [(i, i ^ (odd if i % 2 else even)) for i in ran...  7.79 us
    pallas_call x2, Pallas kernels, add_core(): pl.pallas_call(functools.partial(core_kernel, chunk, depth, len(after)),...  3.02 us
  transfers between devices with their start and end apart: 25, of which 12 were waited for; matrix products, arithmetic and copies ran while one was open for 1% of the time, Pallas kernels for 39%

profile of v1, /device:TPU:17, one launch (start us, length us, event | category | flops | bytes accessed | tf_op | source)
XLA Modules:
  0.0 127.9 jit_solution(3540195547156622758)
XLA Ops:
  0.7 0.8 pad_maximum_fusion.own
  1.4 1.8 %collective-permute-start.2 = (bf16[32,1024]{1,0:T(8,128)(2,1)S(1)}, bf16[32,1024]{1,0:T(8,128)(2,1)S(1)}, u32[]{:S(2)}, u32[]{:S(2)}) collective-permute-start(bf16[32,1024]{1,0:T(8,128)(2,1)S(1)} %pad_maximum_fusion.own), channel_id=1, source_target_pairs={{0,3},{1,2},{2,1},{3,0},{4,7},{5,6},{6,5},{7,4},{8,11},{9,10},{10,... | collective-permute-start | bytes 196616 | tf_op jit(solution)/shard_map/ppermute | solution.py:854
  3.2 0.3 collective-permute-start.1
  3.5 0.2 collective-permute-start
  4.3 0.7 reshape.85.small
  5.0 1.1 collective-permute-done.2.got_three
  6.1 1.3 collective-permute-done.1.got_two
  7.4 0.0 copy-start.29
  7.4 0.0 copy-start.31
  7.4 0.1 heads.1.head
  7.5 1.0 copy-done.25
  8.5 0.1 copy-done.26
  8.6 0.1 copy-done.27
  8.7 0.0 copy-done.28
  8.8 16.2 %pilot_pass.1 = (bf16[352,256]{1,0:T(8,128)(2,1)S(1)}, bf16[352,256]{1,0:T(8,128)(2,1)S(1)}, bf16[512,1024]{1,0:T(8,128)(2,1)S(1)}, bf16[512,1024]{1,0:T(8,128)(...) custom-call(s32[1]{0:T(128)} %bitcast.me.refs_1_, s32[1]{0:T(128)} %bitcast.1.me.index, f32[1]{0:T(128)} %copy.65.heat, ...), custom_call_target="tpu_custom_call" | custom-call | flops 14000000000 | bytes 9000000 | tf_op jit(solution)/shard_map/pilot_pass/pallas_call | solution.py:321
  25.0 0.6 collective-permute-start.3
  25.7 8.2 %target_pass.1 = (f32[128,1024]{1,0:T(8,128)S(1)}, bf16[128,1024]{1,0:T(8,128)(2,1)S(1)}) custom-call(s32[1]{0:T(128)} %bitcast.1.me.index, f32[1]{0:T(128)} %copy.65.heat, bf16[512,1024]{1,0:T(8,128)(2,1)S(1)} %get-tuple-element.94.inputs, f32[1,1024]{1,0:T(1,128)S(1)} %get-tuple-element.95.logp, f32[1,4096]{1,0:T(1,128)S(1)} %bitcast.53, ...), custom_call_target="tpu_custom_call" | custom-call | flops 7000000000 | bytes 7000000 | tf_op jit(solution)/shard_map/target_pass/pallas_call | solution.py:200
  34.0 1.3 %collective-permute-start.4 = (bf16[352,256]{1,0:T(8,128)(2,1)S(1)}, bf16[352,256]{1,0:T(8,128)(2,1)S(1)}, u32[]{:S(2)}, u32[]{:S(2)}) collective-permute-start(bf16[352,256]{1,0:T(8,128)(2,1)S(1)} %add_actor.5.a.refs_0_), channel_id=1, source_target_pairs={{0,2},{1,3},{2,0},{3,1},{4,6},{5,7},{6,4},{7,5},{8,10},{9,11},{10,... | collective-permute-start | bytes 540680 | tf_op jit(solution)/shard_map/ppermute | solution.py:804
  35.3 7.2 %critic_pass.5 = (bf16[18,16,1024]{2,1,0:T(8,128)(2,1)S(1)}, bf16[18,16,1024]{2,1,0:T(8,128)(2,1)S(1)}, f32[160,512]{1,0:T(8,128)S(1)}, f32[8,128]{1,0:T(8,128)S(1)}, f32[1,1024]{1,0:T(1,128)S(1)}) custom-call(s32[1]{0:T(128)} %bitcast.me.refs_1_, bf16[512,1024]{1,0:T(8,128)(2,1)S(1)} %get-tuple-element.93.inputs, f32[128,1024]{1,0:T(8,128)S(1)} %get-tuple-element.97.lagged, ...), custom_call_target="tpu_custom_call" | custom-call | flops 7000000000 | bytes 4000000 | tf_op jit(solution)/shard_map/critic_pass/pallas_call | solution.py:547
  42.4 0.4 collective-permute-start.9
  42.9 1.3 %collective-permute-start.5 = (bf16[352,256]{1,0:T(8,128)(2,1)S(1)}, bf16[352,256]{1,0:T(8,128)(2,1)S(1)}, u32[]{:S(2)}, u32[]{:S(2)}) collective-permute-start(bf16[352,256]{1,0:T(8,128)(2,1)S(1)} %add_actor.6.a.refs_0_), channel_id=1, source_target_pairs={{0,4},{1,5},{2,6},{3,7},{4,0},{5,1},{6,2},{7,3},{8,12},{9,13},{10,... | collective-permute-start | bytes 540680 | tf_op jit(solution)/shard_map/ppermute | solution.py:804
  44.2 7.3 %critic_pass.6 = (bf16[18,16,1024]{2,1,0:T(8,128)(2,1)S(1)}, bf16[18,16,1024]{2,1,0:T(8,128)(2,1)S(1)}, f32[160,512]{1,0:T(8,128)S(1)}, f32[8,128]{1,0:T(8,128)S(1)}, f32[1,1024]{1,0:T(1,128)S(1)}) custom-call(s32[1]{0:T(128)} %bitcast.me.refs_1_, bf16[512,1024]{1,0:T(8,128)(2,1)S(1)} %get-tuple-element.93.inputs, f32[128,1024]{1,0:T(8,128)S(1)} %get-tuple-element.97.lagged, ...), custom_call_target="tpu_custom_call" | custom-call | flops 7000000000 | bytes 4000000 | tf_op jit(solution)/shard_map/critic_pass/pallas_call | solution.py:547
  51.5 0.5 collective-permute-start.10
  52.0 1.4 %collective-permute-start.6 = (bf16[352,256]{1,0:T(8,128)(2,1)S(1)}, bf16[352,256]{1,0:T(8,128)(2,1)S(1)}, u32[]{:S(2)}, u32[]{:S(2)}) collective-permute-start(bf16[352,256]{1,0:T(8,128)(2,1)S(1)} %add_actor.7.a.refs_0_), channel_id=1, source_target_pairs={{0,8},{1,9},{2,10},{3,11},{4,12},{5,13},{6,14},{7,15},{8,0},{9,1},... | collective-permute-start | bytes 540680 | tf_op jit(solution)/shard_map/ppermute | solution.py:804
  53.4 7.1 %critic_pass.7 = (bf16[18,16,1024]{2,1,0:T(8,128)(2,1)S(1)}, bf16[18,16,1024]{2,1,0:T(8,128)(2,1)S(1)}, f32[160,512]{1,0:T(8,128)S(1)}, f32[8,128]{1,0:T(8,128)S(1)}, f32[1,1024]{1,0:T(1,128)S(1)}) custom-call(s32[1]{0:T(128)} %bitcast.me.refs_1_, bf16[512,1024]{1,0:T(8,128)(2,1)S(1)} %get-tuple-element.93.inputs, f32[128,1024]{1,0:T(8,128)S(1)} %get-tuple-element.97.lagged, ...), custom_call_target="tpu_custom_call" | custom-call | flops 7000000000 | bytes 4000000 | tf_op jit(solution)/shard_map/critic_pass/pallas_call | solution.py:547
  60.6 0.4 collective-permute-start.11
  61.1 0.0 copy-start.16
  61.1 7.2 %critic_pass.8 = (bf16[18,16,1024]{2,1,0:T(8,128)(2,1)S(1)}, bf16[18,16,1024]{2,1,0:T(8,128)(2,1)S(1)}, f32[160,512]{1,0:T(8,128)S(1)}, f32[8,128]{1,0:T(8,128)S(1)}, f32[1,1024]{1,0:T(1,128)S(1)}) custom-call(s32[1]{0:T(128)} %bitcast.me.refs_1_, bf16[512,1024]{1,0:T(8,128)(2,1)S(1)} %get-tuple-element.93.inputs, f32[128,1024]{1,0:T(8,128)S(1)} %get-tuple-element.97.lagged, ...), custom_call_target="tpu_custom_call" | custom-call | flops 7000000000 | bytes 4000000 | tf_op jit(solution)/shard_map/critic_pass/pallas_call | solution.py:547
  68.3 0.2 collective-permute-start.14
  68.5 1.5 %add_core.2 = (bf16[2,10,16,1024]{3,2,1,0:T(8,128)(2,1)S(1)}, bf16[2,10,16,1024]{3,2,1,0:T(8,128)(2,1)S(1)}) custom-call(s32[1]{0:T(128)} %bitcast.me.refs_1_, s32[160]{0:T(256)S(1)} %copy-done.16, bf16[18,16,1024]{2,1,0:T(8,128)(2,1)S(1)} %get-tuple-element.99.refs_0_, bf16[18,16,1024]{2,1,0:T(8,128)(2,1)S(1)} %get-tuple-element.103.refs_1_, ...), custom_call_target="tpu_custom_call" | custom-call | flops 1000000 | bytes 8000000 | tf_op jit(solution)/shard_map/add_core/pallas_call | solution.py:616
  70.0 0.3 collective-permute-start.12
  70.3 7.4 %critic_pass.9 = (bf16[6,16,1024]{2,1,0:T(8,128)(2,1)S(1)}, bf16[6,16,1024]{2,1,0:T(8,128)(2,1)S(1)}, bf16[6,16,1024]{2,1,0:T(8,128)(2,1)S(1)}, bf16[4,16,1024]{...) custom-call(s32[1]{0:T(128)} %bitcast.me.refs_1_, bf16[512,1024]{1,0:T(8,128)(2,1)S(1)} %get-tuple-element.93.inputs, ...), custom_call_target="tpu_custom_call" | custom-call | flops 7000000000 | bytes 4000000 | tf_op jit(solution)/shard_map/critic_pass/pallas_call | solution.py:547
  77.8 0.7 collective-permute-start.15
  78.4 0.1 collective-permute-start.16
  78.5 0.4 collective-permute-start.17
  78.9 0.9 collective-permute-done.12.refs_1_
  79.8 1.2 collective-permute-start.18
  81.1 0.2 add_half.2
  81.2 0.8 collective-permute-done.18.refs_9_
  82.1 1.5 %add_core.3 = (bf16[2,11,16,1024]{3,2,1,0:T(8,128)(2,1)S(1)}, bf16[2,11,16,1024]{3,2,1,0:T(8,128)(2,1)S(1)}) custom-call(s32[1]{0:T(128)} %bitcast.me.refs_1_, s32[160]{0:T(256)S(1)} %copy-done.15, bf16[10,16,1024]{2,1,0:T(8,128)(2,1)S(1)} %get-tuple-element.113.refs_0_.refs_2_, bf16[18,16,1024]{2,1,0:T(8,128)(2,1)S(1)} %get-tuple-element.107.refs_2_.refs_1_, ...), custom_call_target="tpu_custom_call" | custom-call | flops 1000000 | bytes 8000000 | tf_op jit(solution)/shard_map/add_core/pallas_call | solution.py:616
  83.6 0.3 collective-permute-start.19
  83.9 0.2 collective-permute-start.13
  84.1 0.1 collective-permute-start.7
  84.2 7.9 %collective-permute-done.7.b = bf16[352,256]{1,0:T(8,128)(2,1)S(1)} collective-permute-done((bf16[352,256]{1,0:T(8,128)(2,1)S(1)}, bf16[352,256]{1,0:T(8,128)(2,1)S(1)}, u32[]{:S(2)}, u32[]{:S(2)}) %collective-permute-start.7) | collective-permute-done | bytes 180256 | tf_op jit(solution)/shard_map/ppermute | solution.py:804
  92.2 0.9 collective-permute-done.13.refs_1_.refs_3_
  93.1 4.6 %collective-permute-done.19.refs_3_ = bf16[2,11,16,1024]{3,2,1,0:T(8,128)(2,1)S(1)} collective-permute-done((bf16[2,11,16,1024]{3,2,1,0:T(8,128)(2,1)S(1)}, bf16[2,11,16,1024]{3,2,1,0:T(8,128)(2,1)S(1)}, u32[]{:S(2)}, u32[]{:S(2)}) %collective-permute-start.19) | collective-permute-done | bytes 720928 | tf_op jit(solution)/shard_map/ppermute | solution.py:809
  97.6 0.2 add_half.3
  97.9 0.2 collective-permute-start.20
  98.2 1.5 %collective-permute-start.8 = (bf16[352,256]{1,0:T(8,128)(2,1)S(1)}, bf16[352,256]{1,0:T(8,128)(2,1)S(1)}, u32[]{:S(2)}, u32[]{:S(2)}) collective-permute-start(bf16[352,256]{1,0:T(8,128)(2,1)S(1)} %add_actor.9.own.refs_0_), channel_id=1, source_target_pairs={{0,1},{1,0},{2,3},{3,2},{4,5},{5,4},{6,7},{7,6},{8,9},{9,8},{10,11... | collective-permute-start | bytes 540680 | tf_op jit(solution)/shard_map/ppermute | solution.py:804
  100.5 0.1 pad_maximum_fusion.1.factors
  100.6 0.2 collective-permute-done.8.peer
  100.8 2.4 %actor_update.1 = (f32[666,256]{1,0:T(8,128)}, f32[666,256]{1,0:T(8,128)}, f32[666,256]{1,0:T(8,128)}, f32[8,128]{1,0:T(8,128)S(1)}) custom-call(s32[1]{0:T(128)} %bitcast.me.refs_1_, f32[2]{0:T(128)S(1)} %pad_maximum_fusion.1.factors, bf16[352,256]{1,0:T(8,128)(2,1)S(1)} %add_actor.9.own.refs_0_, bf16[352,256]{1,0:T(8,128)(2,1)S(1)} %collective-permute-done.8.peer, ...), custom_call_target="tpu_custom_call" | custom-call | flops 2000000 | bytes 5000000 | tf_op jit(solution)/shard_map/actor_update/pallas_call | solution.py:758
  103.2 1.4 %collective-permute-done.20.refs_5_ = bf16[11,16,1024]{2,1,0:T(8,128)(2,1)S(1)} collective-permute-done((bf16[11,16,1024]{2,1,0:T(8,128)(2,1)S(1)}, bf16[11,16,1024]{2,1,0:T(8,128)(2,1)S(1)}, u32[]{:S(2)}, u32[]{:S(2)}) %collective-permute-start.20) | collective-permute-done | bytes 360480 | tf_op jit(solution)/shard_map/ppermute | solution.py:809
  104.6 0.4 add_line.1
  105.0 0.2 collective-permute-start.21
  105.1 0.1 collective-permute-start.22
  105.2 2.5 %collective-permute-start.23 = (bf16[5,16,1024]{2,1,0:T(8,128)(2,1)S(1)}, bf16[5,16,1024]{2,1,0:T(8,128)(2,1)S(1)}, u32[]{:S(2)}, u32[]{:S(2)}) collective-permute-start(bf16[5,16,1024]{2,1,0:T(8,128)(2,1)S(1)} %get-tuple-element.135), channel_id=1, source_target_pairs={{0,24},{1,25},{2,26},{3,27},{4,28},{5,29},{6,30},{7,31},{8,16},{9,... | collective-permute-start | bytes 491528 | tf_op jit(solution)/shard_map/ppermute | solution.py:804
  107.7 1.5 %collective-permute-done.21.refs_1_ = bf16[5,16,1024]{2,1,0:T(8,128)(2,1)S(1)} collective-permute-done((bf16[5,16,1024]{2,1,0:T(8,128)(2,1)S(1)}, bf16[5,16,1024]{2,1,0:T(8,128)(2,1)S(1)}, u32[]{:S(2)}, u32[]{:S(2)}) %collective-permute-start.21) | collective-permute-done | bytes 163872 | tf_op jit(solution)/shard_map/ppermute | solution.py:804
  109.2 3.1 %collective-permute-done.22.refs_2_ = bf16[5,16,1024]{2,1,0:T(8,128)(2,1)S(1)} collective-permute-done((bf16[5,16,1024]{2,1,0:T(8,128)(2,1)S(1)}, bf16[5,16,1024]{2,1,0:T(8,128)(2,1)S(1)}, u32[]{:S(2)}, u32[]{:S(2)}) %collective-permute-start.22) | collective-permute-done | bytes 163872 | tf_op jit(solution)/shard_map/ppermute | solution.py:804
  112.3 9.4 %collective-permute-done.23.refs_3_ = bf16[5,16,1024]{2,1,0:T(8,128)(2,1)S(1)} collective-permute-done((bf16[5,16,1024]{2,1,0:T(8,128)(2,1)S(1)}, bf16[5,16,1024]{2,1,0:T(8,128)(2,1)S(1)}, u32[]{:S(2)}, u32[]{:S(2)}) %collective-permute-start.23) | collective-permute-done | bytes 163872 | tf_op jit(solution)/shard_map/ppermute | solution.py:804
  121.7 0.1 sum_row.1.row_own
  121.8 1.6 %collective-permute-start.24 = (f32[8,128]{1,0:T(8,128)S(1)}, f32[8,128]{1,0:T(8,128)S(1)}, u32[]{:S(2)}, u32[]{:S(2)}) collective-permute-start(f32[8,128]{1,0:T(8,128)S(1)} %sum_row.1.row_own), channel_id=1, source_target_pairs={{0,1},{1,0},{2,3},{3,2},{4,5},{5,4},{6,7},{7,6},{8,9},{9,8},{10,11... | collective-permute-start | bytes 12296 | tf_op jit(solution)/shard_map/ppermute | solution.py:804
  124.9 1.8 %update.1 = (f32[80,393]{1,0:T(8,128)}, f32[80,393]{1,0:T(8,128)}, f32[80,393]{1,0:T(8,128)}, f32[80,512]{1,0:T(8,128)}, f32[80,512]{1,0:T(8,128)}, /*index=5*/f...) custom-call(f32[2]{0:T(128)S(1)} %pad_maximum_fusion.1.factors, ...), custom_call_target="tpu_custom_call" | custom-call | flops 2000000 | bytes 6000000 | tf_op jit(solution)/shard_map/update/pallas_call | solution.py:735
  126.7 1.2 small_update.1
  (81 shorter events, 0.5 us)
Async XLA Ops:
  1.4 4.6 %collective-permute-start.2 = (bf16[32,1024]{1,0:T(8,128)(2,1)S(1)}, bf16[32,1024]{1,0:T(8,128)(2,1)S(1)}, u32[]{:S(2)}, u32[]{:S(2)}) collective-permute-start(bf16[32,1024]{1,0:T(8,128)(2,1)S(1)} %pad_maximum_fusion.own), channel_id=1, source_target_pairs={{0,3},{1,2},{2,1},{3,0},{4,7},{5,6},{6,5},{7,4},{8,11},{9,10},{10,... | collective-permute-start | bytes 196616 | tf_op jit(solution)/shard_map/ppermute | solution.py:854
  3.2 4.1 %collective-permute-start.1 = (bf16[32,1024]{1,0:T(8,128)(2,1)S(1)}, bf16[32,1024]{1,0:T(8,128)(2,1)S(1)}, u32[]{:S(2)}, u32[]{:S(2)}) collective-permute-start(bf16[32,1024]{1,0:T(8,128)(2,1)S(1)} %pad_maximum_fusion.own), channel_id=1, source_target_pairs={{0,2},{1,3},{2,0},{3,1},{4,6},{5,7},{6,4},{7,5},{8,10},{9,11},{10,... | collective-permute-start | bytes 196616 | tf_op jit(solution)/shard_map/ppermute | solution.py:854
  3.5 3.9 %collective-permute-start = (bf16[32,1024]{1,0:T(8,128)(2,1)S(1)}, bf16[32,1024]{1,0:T(8,128)(2,1)S(1)}, u32[]{:S(2)}, u32[]{:S(2)}) collective-permute-start(bf16[32,1024]{1,0:T(8,128)(2,1)S(1)} %pad_maximum_fusion.own), channel_id=1, source_target_pairs={{0,1},{1,0},{2,3},{3,2},{4,5},{5,4},{6,7},{7,6},{8,9},{9,8},{10,11... | collective-permute-start | bytes 196616 | tf_op jit(solution)/shard_map/ppermute | solution.py:854
  7.4 1.1 copy-start.25
  7.4 1.2 copy-start.26
  7.4 1.3 %copy-start.27 = (bf16[666,256]{1,0:T(8,128)(2,1)S(1)}, bf16[666,256]{1,0:T(8,128)(2,1)}, u32[]{:S(2)}) copy-start(bf16[666,256]{1,0:T(8,128)(2,1)} %actor.1) | copy-start | bytes 1022980
  7.4 1.3 %copy-start.28 = (f32[1024,17]{0,1:T(8,128)S(1)}, f32[1024,17]{0,1:T(8,128)}, u32[]{:S(2)}) copy-start(f32[1024,17]{0,1:T(8,128)} %param.44) | copy-start | bytes 208900
  7.4 1.3 %copy-start.29 = (bf16[1024,17]{0,1:T(8,128)(2,1)S(1)}, bf16[1024,17]{0,1:T(8,128)(2,1)}, u32[]{:S(2)}) copy-start(bf16[1024,17]{0,1:T(8,128)(2,1)} %param.43) | copy-start | bytes 104452
  7.4 1.3 %copy-start.31 = (f32[2,2560]{1,0:T(2,128)S(1)}, f32[2,2560]{1,0:T(2,128)}, u32[]{:S(2)}) copy-start(f32[2,2560]{1,0:T(2,128)} %bias.13) | copy-start | bytes 61444
  7.4 1.3 %copy-start.34 = (f32[128]{0:T(128)S(1)}, f32[128]{0:T(128)}, u32[]{:S(2)}) copy-start(f32[128]{0:T(128)} %param.58) | copy-start | bytes 1540
  8.7 16.9 %copy-start.20 = (bf16[512,2560]{1,0:T(8,128)(2,1)S(1)}, bf16[512,2560]{1,0:T(8,128)(2,1)}, u32[]{:S(2)}) copy-start(bf16[512,2560]{1,0:T(8,128)(2,1)} %second.6) | copy-start | bytes 7864324
  8.7 16.9 %copy-start.22 = (s32[4096,125]{1,0:T(8,128)S(1)}, s32[4096,125]{1,0:T(8,128)}, u32[]{:S(2)}) copy-start(s32[4096,125]{1,0:T(8,128)} %order_in.1) | copy-start | bytes 6144004
  8.7 16.9 %copy-start.23 = (bf16[393,2560]{1,0:T(8,128)(2,1)S(1)}, bf16[393,2560]{1,0:T(8,128)(2,1)}, u32[]{:S(2)}) copy-start(bf16[393,2560]{1,0:T(8,128)(2,1)} %first.6) | copy-start | bytes 6036484
  8.7 16.9 %copy-start.30 = (f32[2,2560]{1,0:T(2,128)S(1)}, f32[2,2560]{1,0:T(2,128)}, u32[]{:S(2)}) copy-start(f32[2,2560]{1,0:T(2,128)} %bias.8) | copy-start | bytes 61444
  8.7 16.9 %copy-start.32 = (f32[4096]{0:T(1024)S(1)}, f32[4096]{0:T(1024)}, u32[]{:S(2)}) copy-start(f32[4096]{0:T(1024)} %param.47) | copy-start | bytes 49156
  8.8 16.9 %copy-start.33 = (s32[4096]{0:T(1024)S(1)}, s32[4096]{0:T(1024)}, u32[]{:S(2)}) copy-start(s32[4096]{0:T(1024)} %param.48) | copy-start | bytes 49156
  25.0 8.9 %collective-permute-start.3 = (bf16[352,256]{1,0:T(8,128)(2,1)S(1)}, bf16[352,256]{1,0:T(8,128)(2,1)S(1)}, u32[]{:S(2)}, u32[]{:S(2)}) collective-permute-start(bf16[352,256]{1,0:T(8,128)(2,1)S(1)} %get-tuple-element.91), channel_id=1, source_target_pairs={{0,1},{1,0},{2,3},{3,2},{4,5},{5,4},{6,7},{7,6},{8,9},{9,8},{10,11... | collective-permute-start | bytes 540680 | tf_op jit(solution)/shard_map/ppermute | solution.py:804
  25.6 9.6 %copy-start.21 = (bf16[512,2560]{1,0:T(8,128)(2,1)S(1)}, bf16[512,2560]{1,0:T(8,128)(2,1)}, u32[]{:S(2)}) copy-start(bf16[512,2560]{1,0:T(8,128)(2,1)} %second.11) | copy-start | bytes 7864324
  25.6 9.6 %copy-start.24 = (bf16[393,2560]{1,0:T(8,128)(2,1)S(1)}, bf16[393,2560]{1,0:T(8,128)(2,1)}, u32[]{:S(2)}) copy-start(bf16[393,2560]{1,0:T(8,128)(2,1)} %first.11) | copy-start | bytes 6036484
  34.0 8.9 %collective-permute-start.4 = (bf16[352,256]{1,0:T(8,128)(2,1)S(1)}, bf16[352,256]{1,0:T(8,128)(2,1)S(1)}, u32[]{:S(2)}, u32[]{:S(2)}) collective-permute-start(bf16[352,256]{1,0:T(8,128)(2,1)S(1)} %add_actor.5.a.refs_0_), channel_id=1, source_target_pairs={{0,2},{1,3},{2,0},{3,1},{4,6},{5,7},{6,4},{7,5},{8,10},{9,11},{10,... | collective-permute-start | bytes 540680 | tf_op jit(solution)/shard_map/ppermute | solution.py:804
  42.4 26.1 %collective-permute-start.9 = (bf16[18,16,1024]{2,1,0:T(8,128)(2,1)S(1)}, bf16[18,16,1024]{2,1,0:T(8,128)(2,1)S(1)}, u32[]{:S(2)}, u32[]{:S(2)}) collective-permute-start(bf16[18,16,1024]{2,1,0:T(8,128)(2,1)S(1)} %get-tuple-element.108), channel_id=1, source_target_pairs={{0,1},{1,0},{2,3},{3,2},{4,5},{5,4},{6,7},{7,6},{8,9},{9,8},{10,11... | collective-permute-start | bytes 1769480 | tf_op jit(solution)/shard_map/ppermute | solution.py:804
  42.9 9.1 %collective-permute-start.5 = (bf16[352,256]{1,0:T(8,128)(2,1)S(1)}, bf16[352,256]{1,0:T(8,128)(2,1)S(1)}, u32[]{:S(2)}, u32[]{:S(2)}) collective-permute-start(bf16[352,256]{1,0:T(8,128)(2,1)S(1)} %add_actor.6.a.refs_0_), channel_id=1, source_target_pairs={{0,4},{1,5},{2,6},{3,7},{4,0},{5,1},{6,2},{7,3},{8,12},{9,13},{10,... | collective-permute-start | bytes 540680 | tf_op jit(solution)/shard_map/ppermute | solution.py:804
  51.5 17.0 %collective-permute-start.10 = (bf16[18,16,1024]{2,1,0:T(8,128)(2,1)S(1)}, bf16[18,16,1024]{2,1,0:T(8,128)(2,1)S(1)}, u32[]{:S(2)}, u32[]{:S(2)}) collective-permute-start(bf16[18,16,1024]{2,1,0:T(8,128)(2,1)S(1)} %get-tuple-element.109), channel_id=1, source_target_pairs={{0,1},{1,0},{2,3},{3,2},{4,5},{5,4},{6,7},{7,6},{8,9},{9,8},{10,11... | collective-permute-start | bytes 1769480 | tf_op jit(solution)/shard_map/ppermute | solution.py:804
  52.0 9.0 %collective-permute-start.6 = (bf16[352,256]{1,0:T(8,128)(2,1)S(1)}, bf16[352,256]{1,0:T(8,128)(2,1)S(1)}, u32[]{:S(2)}, u32[]{:S(2)}) collective-permute-start(bf16[352,256]{1,0:T(8,128)(2,1)S(1)} %add_actor.7.a.refs_0_), channel_id=1, source_target_pairs={{0,8},{1,9},{2,10},{3,11},{4,12},{5,13},{6,14},{7,15},{8,0},{9,1},... | collective-permute-start | bytes 540680 | tf_op jit(solution)/shard_map/ppermute | solution.py:804
  60.6 7.9 %collective-permute-start.11 = (bf16[18,16,1024]{2,1,0:T(8,128)(2,1)S(1)}, bf16[18,16,1024]{2,1,0:T(8,128)(2,1)S(1)}, u32[]{:S(2)}, u32[]{:S(2)}) collective-permute-start(bf16[18,16,1024]{2,1,0:T(8,128)(2,1)S(1)} %get-tuple-element.110), channel_id=1, source_target_pairs={{0,1},{1,0},{2,3},{3,2},{4,5},{5,4},{6,7},{7,6},{8,9},{9,8},{10,11... | collective-permute-start | bytes 1769480 | tf_op jit(solution)/shard_map/ppermute | solution.py:804
  61.1 7.4 %copy-start.16 = (s32[160]{0:T(256)S(1)}, s32[160]{0:T(256)}, u32[]{:S(2)}) copy-start(s32[160]{0:T(256)} %constant.21.clone.places) | copy-start | bytes 1924
  68.3 13.8 %collective-permute-start.14 = (bf16[18,16,1024]{2,1,0:T(8,128)(2,1)S(1)}, bf16[18,16,1024]{2,1,0:T(8,128)(2,1)S(1)}, u32[]{:S(2)}, u32[]{:S(2)}) collective-permute-start(bf16[18,16,1024]{2,1,0:T(8,128)(2,1)S(1)} %get-tuple-element.123), channel_id=1, source_target_pairs={{0,1},{1,0},{2,3},{3,2},{4,5},{5,4},{6,7},{7,6},{8,9},{9,8},{10,11... | collective-permute-start | bytes 1769480 | tf_op jit(solution)/shard_map/ppermute | solution.py:804
  70.0 9.8 %collective-permute-start.12 = (bf16[2,10,16,1024]{3,2,1,0:T(8,128)(2,1)S(1)}, bf16[2,10,16,1024]{3,2,1,0:T(8,128)(2,1)S(1)}, u32[]{:S(2)}, u32[]{:S(2)}) collective-permute-start(bf16[2,10,16,1024]{3,2,1,0:T(8,128)(2,1)S(1)} %get-tuple-element.112), channel_id=1, source_target_pairs={{0,2},{1,5},{2,0},{3,7},{4,6},{5,1},{6,4},{7,3},{8,10},{9,13},{10,... | collective-permute-start | bytes 1966088 | tf_op jit(solution)/shard_map/ppermute | solution.py:809
  70.3 11.8 %copy-start.15 = (s32[160]{0:T(256)S(1)}, s32[160]{0:T(256)}, u32[]{:S(2)}) copy-start(s32[160]{0:T(256)} %constant.22.clone.places) | copy-start | bytes 1924
  77.8 4.3 %collective-permute-start.15 = (bf16[6,16,1024]{2,1,0:T(8,128)(2,1)S(1)}, bf16[6,16,1024]{2,1,0:T(8,128)(2,1)S(1)}, u32[]{:S(2)}, u32[]{:S(2)}) collective-permute-start(bf16[6,16,1024]{2,1,0:T(8,128)(2,1)S(1)} %get-tuple-element.124), channel_id=1, source_target_pairs={{0,1},{1,0},{2,3},{3,2},{4,5},{5,4},{6,7},{7,6},{8,9},{9,8},{10,11... | collective-permute-start | bytes 589832 | tf_op jit(solution)/shard_map/ppermute | solution.py:804
  78.4 3.6 %collective-permute-start.16 = (bf16[6,16,1024]{2,1,0:T(8,128)(2,1)S(1)}, bf16[6,16,1024]{2,1,0:T(8,128)(2,1)S(1)}, u32[]{:S(2)}, u32[]{:S(2)}) collective-permute-start(bf16[6,16,1024]{2,1,0:T(8,128)(2,1)S(1)} %get-tuple-element.125), channel_id=1, source_target_pairs={{0,1},{1,0},{2,3},{3,2},{4,5},{5,4},{6,7},{7,6},{8,9},{9,8},{10,11... | collective-permute-start | bytes 589832 | tf_op jit(solution)/shard_map/ppermute | solution.py:804
  78.5 3.6 %collective-permute-start.17 = (bf16[6,16,1024]{2,1,0:T(8,128)(2,1)S(1)}, bf16[6,16,1024]{2,1,0:T(8,128)(2,1)S(1)}, u32[]{:S(2)}, u32[]{:S(2)}) collective-permute-start(bf16[6,16,1024]{2,1,0:T(8,128)(2,1)S(1)} %get-tuple-element.126), channel_id=1, source_target_pairs={{0,1},{1,0},{2,3},{3,2},{4,5},{5,4},{6,7},{7,6},{8,9},{9,8},{10,11... | collective-permute-start | bytes 589832 | tf_op jit(solution)/shard_map/ppermute | solution.py:804
  79.8 2.2 %collective-permute-start.18 = (bf16[4,16,1024]{2,1,0:T(8,128)(2,1)S(1)}, bf16[4,16,1024]{2,1,0:T(8,128)(2,1)S(1)}, u32[]{:S(2)}, u32[]{:S(2)}) collective-permute-start(bf16[4,16,1024]{2,1,0:T(8,128)(2,1)S(1)} %get-tuple-element.127), channel_id=1, source_target_pairs={{0,1},{1,0},{2,3},{3,2},{4,5},{5,4},{6,7},{7,6},{8,9},{9,8},{10,11... | collective-permute-start | bytes 393224 | tf_op jit(solution)/shard_map/ppermute | solution.py:804
  82.1 18.7 %copy-start = (f32[666,256]{1,0:T(8,128)S(1)}, f32[666,256]{1,0:T(8,128)}, u32[]{:S(2)}) copy-start(f32[666,256]{1,0:T(8,128)} %refs_0_.2) | copy-start | bytes 2045956
  82.1 18.7 %copy-start.1 = (f32[666,256]{1,0:T(8,128)S(1)}, f32[666,256]{1,0:T(8,128)}, u32[]{:S(2)}) copy-start(f32[666,256]{1,0:T(8,128)} %refs_1_.2) | copy-start | bytes 2045956
  82.1 18.7 %copy-start.2 = (f32[666,256]{1,0:T(8,128)S(1)}, f32[666,256]{1,0:T(8,128)}, u32[]{:S(2)}) copy-start(f32[666,256]{1,0:T(8,128)} %refs_2_.2) | copy-start | bytes 2045956
  83.6 14.0 %collective-permute-start.19 = (bf16[2,11,16,1024]{3,2,1,0:T(8,128)(2,1)S(1)}, bf16[2,11,16,1024]{3,2,1,0:T(8,128)(2,1)S(1)}, u32[]{:S(2)}, u32[]{:S(2)}) collective-permute-start(bf16[2,11,16,1024]{3,2,1,0:T(8,128)(2,1)S(1)} %get-tuple-element.129), channel_id=1, source_target_pairs={{0,2},{1,5},{2,0},{3,7},{4,6},{5,1},{6,4},{7,3},{8,10},{9,13},{10,... | collective-permute-start | bytes 2162696 | tf_op jit(solution)/shard_map/ppermute | solution.py:809
  83.9 9.2 %collective-permute-start.13 = (bf16[10,16,1024]{2,1,0:T(8,128)(2,1)S(1)}, bf16[10,16,1024]{2,1,0:T(8,128)(2,1)S(1)}, u32[]{:S(2)}, u32[]{:S(2)}) collective-permute-start(bf16[10,16,1024]{2,1,0:T(8,128)(2,1)S(1)} %get-tuple-element.114), channel_id=1, source_target_pairs={{0,4},{1,3},{2,6},{3,1},{4,0},{5,7},{6,2},{7,5},{8,12},{9,11},{10,... | collective-permute-start | bytes 983048 | tf_op jit(solution)/shard_map/ppermute | solution.py:809
  84.1 8.0 %collective-permute-start.7 = (bf16[352,256]{1,0:T(8,128)(2,1)S(1)}, bf16[352,256]{1,0:T(8,128)(2,1)S(1)}, u32[]{:S(2)}, u32[]{:S(2)}) collective-permute-start(bf16[352,256]{1,0:T(8,128)(2,1)S(1)} %add_actor.8.a.refs_0_), channel_id=1, source_target_pairs={{0,16},{1,17},{2,18},{3,19},{4,20},{5,21},{6,22},{7,23},{8,24},{9,... | collective-permute-start | bytes 540680 | tf_op jit(solution)/shard_map/ppermute | solution.py:804
  97.8 26.9 %copy-start.3 = (f32[393,80]{0,1:T(8,128)S(1)}, f32[393,80]{0,1:T(8,128)}, u32[]{:S(2)}) copy-start(f32[393,80]{0,1:T(8,128)} %param.61) | copy-start | bytes 377284
  97.8 26.9 %copy-start.4 = (f32[393,80]{0,1:T(8,128)S(1)}, f32[393,80]{0,1:T(8,128)}, u32[]{:S(2)}) copy-start(f32[393,80]{0,1:T(8,128)} %param.62) | copy-start | bytes 377284
  97.8 26.9 %copy-start.5 = (f32[393,80]{0,1:T(8,128)S(1)}, f32[393,80]{0,1:T(8,128)}, u32[]{:S(2)}) copy-start(f32[393,80]{0,1:T(8,128)} %param.63) | copy-start | bytes 377284
  97.8 26.9 %copy-start.6 = (f32[512,80]{0,1:T(8,128)S(1)}, f32[512,80]{0,1:T(8,128)}, u32[]{:S(2)}) copy-start(f32[512,80]{0,1:T(8,128)} %param.64) | copy-start | bytes 491524
  97.9 26.9 %copy-start.7 = (f32[512,80]{0,1:T(8,128)S(1)}, f32[512,80]{0,1:T(8,128)}, u32[]{:S(2)}) copy-start(f32[512,80]{0,1:T(8,128)} %param.65) | copy-start | bytes 491524
  97.9 26.9 %copy-start.8 = (f32[512,80]{0,1:T(8,128)S(1)}, f32[512,80]{0,1:T(8,128)}, u32[]{:S(2)}) copy-start(f32[512,80]{0,1:T(8,128)} %param.66) | copy-start | bytes 491524
  97.9 26.9 %copy-start.9 = (f32[64,32]{0,1:T(8,128)S(1)}, f32[64,32]{0,1:T(8,128)}, u32[]{:S(2)}) copy-start(f32[64,32]{0,1:T(8,128)} %param.70) | copy-start | bytes 24580
  97.9 26.9 %copy-start.10 = (f32[64,32]{0,1:T(8,128)S(1)}, f32[64,32]{0,1:T(8,128)}, u32[]{:S(2)}) copy-start(f32[64,32]{0,1:T(8,128)} %param.71) | copy-start | bytes 24580
  97.9 26.9 %copy-start.11 = (f32[64,32]{0,1:T(8,128)S(1)}, f32[64,32]{0,1:T(8,128)}, u32[]{:S(2)}) copy-start(f32[64,32]{0,1:T(8,128)} %param.72) | copy-start | bytes 24580
  97.9 26.9 %copy-start.17 = (f32[2,80]{1,0:T(2,128)S(1)}, f32[2,80]{1,0:T(2,128)}, u32[]{:S(2)}) copy-start(f32[2,80]{1,0:T(2,128)} %refs_10_.1) | copy-start | bytes 1924
  97.9 26.9 %copy-start.18 = (f32[2,80]{1,0:T(2,128)S(1)}, f32[2,80]{1,0:T(2,128)}, u32[]{:S(2)}) copy-start(f32[2,80]{1,0:T(2,128)} %refs_11_.1) | copy-start | bytes 1924
  97.9 26.9 %copy-start.19 = (f32[2,80]{1,0:T(2,128)S(1)}, f32[2,80]{1,0:T(2,128)}, u32[]{:S(2)}) copy-start(f32[2,80]{1,0:T(2,128)} %refs_12_.1) | copy-start | bytes 1924
  97.9 6.6 %collective-permute-start.20 = (bf16[11,16,1024]{2,1,0:T(8,128)(2,1)S(1)}, bf16[11,16,1024]{2,1,0:T(8,128)(2,1)S(1)}, u32[]{:S(2)}, u32[]{:S(2)}) collective-permute-start(bf16[11,16,1024]{2,1,0:T(8,128)(2,1)S(1)} %get-tuple-element.131), channel_id=1, source_target_pairs={{0,4},{1,3},{2,6},{3,1},{4,0},{5,7},{6,2},{7,5},{8,12},{9,11},{10,... | collective-permute-start | bytes 1081352 | tf_op jit(solution)/shard_map/ppermute | solution.py:809
  98.2 2.6 %collective-permute-start.8 = (bf16[352,256]{1,0:T(8,128)(2,1)S(1)}, bf16[352,256]{1,0:T(8,128)(2,1)S(1)}, u32[]{:S(2)}, u32[]{:S(2)}) collective-permute-start(bf16[352,256]{1,0:T(8,128)(2,1)S(1)} %add_actor.9.own.refs_0_), channel_id=1, source_target_pairs={{0,1},{1,0},{2,3},{3,2},{4,5},{5,4},{6,7},{7,6},{8,9},{9,8},{10,11... | collective-permute-start | bytes 540680 | tf_op jit(solution)/shard_map/ppermute | solution.py:804
  100.6 26.0 %copy-start.12 = (f32[674]{0:T(1024)S(1)}, f32[674]{0:T(1024)}, u32[]{:S(2)}) copy-start(f32[674]{0:T(1024)} %refs_0_.3) | copy-start | bytes 8092
  100.6 26.0 %copy-start.13 = (f32[674]{0:T(1024)S(1)}, f32[674]{0:T(1024)}, u32[]{:S(2)}) copy-start(f32[674]{0:T(1024)} %refs_1_.3) | copy-start | bytes 8092
  100.6 26.0 %copy-start.14 = (f32[674]{0:T(1024)S(1)}, f32[674]{0:T(1024)}, u32[]{:S(2)}) copy-start(f32[674]{0:T(1024)} %refs_2_.3) | copy-start | bytes 8092
  105.0 4.2 %collective-permute-start.21 = (bf16[5,16,1024]{2,1,0:T(8,128)(2,1)S(1)}, bf16[5,16,1024]{2,1,0:T(8,128)(2,1)S(1)}, u32[]{:S(2)}, u32[]{:S(2)}) collective-permute-start(bf16[5,16,1024]{2,1,0:T(8,128)(2,1)S(1)} %get-tuple-element.133), channel_id=1, source_target_pairs={{0,8},{1,9},{2,10},{3,11},{4,12},{5,13},{6,14},{7,15},{8,0},{9,1},... | collective-permute-start | bytes 491528 | tf_op jit(solution)/shard_map/ppermute | solution.py:804
  105.1 7.1 %collective-permute-start.22 = (bf16[5,16,1024]{2,1,0:T(8,128)(2,1)S(1)}, bf16[5,16,1024]{2,1,0:T(8,128)(2,1)S(1)}, u32[]{:S(2)}, u32[]{:S(2)}) collective-permute-start(bf16[5,16,1024]{2,1,0:T(8,128)(2,1)S(1)} %get-tuple-element.134), channel_id=1, source_target_pairs={{0,16},{1,17},{2,18},{3,19},{4,20},{5,21},{6,22},{7,23},{8,24},{9,... | collective-permute-start | bytes 491528 | tf_op jit(solution)/shard_map/ppermute | solution.py:804
  105.2 16.5 %collective-permute-start.23 = (bf16[5,16,1024]{2,1,0:T(8,128)(2,1)S(1)}, bf16[5,16,1024]{2,1,0:T(8,128)(2,1)S(1)}, u32[]{:S(2)}, u32[]{:S(2)}) collective-permute-start(bf16[5,16,1024]{2,1,0:T(8,128)(2,1)S(1)} %get-tuple-element.135), channel_id=1, source_target_pairs={{0,24},{1,25},{2,26},{3,27},{4,28},{5,29},{6,30},{7,31},{8,16},{9,... | collective-permute-start | bytes 491528 | tf_op jit(solution)/shard_map/ppermute | solution.py:804
  121.8 4.8 %collective-permute-start.24 = (f32[8,128]{1,0:T(8,128)S(1)}, f32[8,128]{1,0:T(8,128)S(1)}, u32[]{:S(2)}, u32[]{:S(2)}) collective-permute-start(f32[8,128]{1,0:T(8,128)S(1)} %sum_row.1.row_own), channel_id=1, source_target_pairs={{0,1},{1,0},{2,3},{3,2},{4,5},{5,4},{6,7},{7,6},{8,9},{9,8},{10,11... | collective-permute-start | bytes 12296 | tf_op jit(solution)/shard_map/ppermute | solution.py:804

commit v2 on v1

--- a/solution.py
+++ b/solution.py
@@ -59,6 +59,14 @@
     return lax.dot_general(left, right, (((1,), (1,)), ((), ())), preferred_element_type=F32)
 
 
+def relu(value):
+    return jnp.maximum(value.astype(BF), jnp.zeros((), BF))
+
+
+def gate(kept, value):
+    return jnp.where(kept > 0, value.astype(BF), jnp.zeros((), BF))
+
+
 def params(limit=32, steps=0):
     semantics = ("arbitrary",) * steps if steps else None
     return pltpu.CompilerParams(vmem_limit_bytes=limit * MiB, dimension_semantics=semantics)
@@ -88,8 +96,8 @@
     s_one = column(small[:, :ACTOR_HIDDEN])
     s_two = column(small[:, ACTOR_HIDDEN : 2 * ACTOR_HIDDEN])
     s_three = column(small[:, 2 * ACTOR_HIDDEN : 2 * ACTOR_HIDDEN + PADDED])[: 2 * ACT_DIM]
-    g_one = jnp.maximum(dot_tn(actor[:OBS_DIM], inputs) + s_one, 0.0).astype(BF)
-    g_two = jnp.maximum(dot_tn(actor[OBS_DIM : OBS_DIM + ACTOR_HIDDEN], g_one) + s_two, 0.0).astype(BF)
+    g_one = relu(dot_tn(actor[:OBS_DIM], inputs) + s_one)
+    g_two = relu(dot_tn(actor[OBS_DIM : OBS_DIM + ACTOR_HIDDEN], g_one) + s_two)
     out_scratch[: 2 * ACT_DIM] = dot_nn(actor[OBS_DIM + ACTOR_HIDDEN :], g_two) + s_three
     mean = out_scratch[:ACT_DIM]
     log_std = out_scratch[ACT_DIM : 2 * ACT_DIM]
@@ -175,13 +183,13 @@
         b_two = column(bias[1:2, lanes])
         w_two = second[:, lanes]
         for part in tiles(rows):
-            h_one = jnp.maximum(dot_tn(filled[...], inputs[:, part]), 0.0).astype(BF)
-            h_two = jnp.maximum(dot_tn(w_two, h_one) + b_two, 0.0).astype(BF)
+            h_one = relu(dot_tn(filled[...], inputs[:, part]))
+            h_two = relu(dot_tn(w_two, h_one) + b_two)
             value = dot_nn(head[e, :, HIDDEN_SIZE:], h_two) + head_bias[1, e, :, :1]
             slots[pl.ds(pl.multiple_of(e * SLOT, SLOT), SLOT), part] = value
         return carry
 
-    lax.fori_loop(0, CRITICS, one_critic, 0)
+    lax.fori_loop(0, CRITICS, one_critic, 0, unroll=True)
     for e in range(CRITICS):
         packed[e * QUANTS : e * QUANTS + SLOT] = slots[e * SLOT : (e + 1) * SLOT]
     copy.wait()
@@ -266,13 +274,12 @@
         push = column(head_sum * level)
         w_two = second[:, lanes]
         for part in tiles(rows):
-            h_one = jnp.maximum(dot_tn(filled[...], inputs[:, part]), 0.0).astype(BF)
-            h_two = jnp.maximum(dot_tn(w_two, h_one) + b_two, 0.0)
-            weighted = h_two * weight
+            h_one = relu(dot_tn(filled[...], inputs[:, part]))
+            h_two = relu(dot_tn(w_two, h_one) + b_two)
+            weighted = h_two.astype(F32) * weight
             total[:, part] += jnp.sum(weighted.reshape(-1, 8, weighted.shape[1]), axis=0)
-            dz_two = jnp.where(h_two > 0, push, 0.0).astype(BF)
-            grad = dot_nn(w_two, dz_two)
-            dz_one = jnp.where(h_one > 0, grad, 0.0).astype(BF)
+            dz_two = jnp.where(h_two > 0, push.astype(BF), jnp.zeros((), BF))
+            dz_one = gate(h_one, dot_nn(w_two, dz_two))
             dact[:, part] += dot_nn(first[OBS_DIM // 16 * 16 :, lanes], dz_one)
         return tail + head_bias[0, e, :, :1]
 
@@ -286,8 +293,8 @@
     dout = out_scratch[: 2 * ACT_DIM].astype(BF)
     a_two = actor[OBS_DIM : OBS_DIM + ACTOR_HIDDEN]
     a_three = actor[OBS_DIM + ACTOR_HIDDEN :]
-    dz_two = jnp.where(g_two > 0, dot_tn(a_three, dout), 0.0).astype(BF)
-    dz_one = jnp.where(g_one > 0, dot_nn(a_two, dz_two), 0.0).astype(BF)
+    dz_two = gate(g_two, dot_tn(a_three, dout))
+    dz_one = gate(g_one, dot_nn(a_two, dz_two))
     grad_out[OBS_DIM + ACTOR_HIDDEN : OBS_DIM + ACTOR_HIDDEN + 2 * ACT_DIM] = dot_nt(dout, g_two)
     grad_out[OBS_DIM + ACTOR_HIDDEN + 2 * ACT_DIM :] = jnp.zeros((6, ACTOR_HIDDEN), F32)
     grad_out[OBS_DIM : OBS_DIM + ACTOR_HIDDEN] = dot_nt(g_one, dz_two)
@@ -372,7 +379,7 @@
             parts[(QUANTS + j) * 16 : (QUANTS + j) * 16 + 16, part] = h[0] + h[1]
         return carry
 
-    lax.fori_loop(0, rows // PADDED, group, 0)
+    lax.fori_loop(0, rows // PADDED, group, 0, unroll=2)
     shape = (48, 2 * QUANTS * 16)
     row = lax.broadcasted_iota(jnp.int32, shape, 0)
     owner = jnp.minimum(lax.broadcasted_iota(jnp.int32, shape, 1) // 16, SLOT)
@@ -425,9 +432,9 @@
     fill_first(tall_w, filled, first[:, lanes], bias[:1, lanes])
     b_two = column(bias[1:2, lanes])
     for part in tiles(rows, CRITIC_TILE):
-        h_one[:, part] = jnp.maximum(dot_tn(filled[...], inputs[:, part]), 0.0).astype(BF)
+        h_one[:, part] = relu(dot_tn(filled[...], inputs[:, part]))
     for part in tiles(rows, CRITIC_TILE):
-        h_two[:, part] = jnp.maximum(dot_tn(second[...], h_one[:, part]) + b_two, 0.0).astype(BF)
+        h_two[:, part] = relu(dot_tn(second[...], h_one[:, part]) + b_two)
     for part in tiles(rows, CRITIC_TILE):
         q[:, part] = dot_nn(head[0], h_two[:, part]) + head_bias[0, 0, :, :1]
     terms = pair_terms(q, lagged, keep, parts, rows)
@@ -439,14 +446,14 @@
     sums = jnp.zeros((HIDDEN_SIZE, PADDED), F32)
     for part in tiles(rows, CRITIC_TILE):
         two = h_two[:, part]
-        dz_two = jnp.where(two > 0, dot_tn(head[0], low[:, part.start : part.start + part.size]), 0.0)
-        for i in range(part.size // PADDED):
-            sums = sums + dz_two[:, i * PADDED : (i + 1) * PADDED]
-        h_two[:, part] = dz_two.astype(BF)
+        dz_two = gate(two, dot_tn(head[0], low[:, part.start : part.start + part.size]))
+        lanes_of = [dz_two[:, i * PADDED : (i + 1) * PADDED] for i in range(part.size // PADDED)]
+        sums = sums + tree(lanes_of).astype(F32)
+        h_two[:, part] = dz_two
     second_grad = dot_nt(h_two[...], h_one[...])
     for part in tiles(rows, CRITIC_TILE):
         one = h_one[:, part]
-        h_one[:, part] = jnp.where(one > 0, dot_nn(second[...], h_two[:, part]), 0.0).astype(BF)
+        h_one[:, part] = gate(one, dot_nn(second[...], h_two[:, part]))
     grads[:, :, :HIDDEN_SIZE] = second_grad.astype(BF).reshape(-1, 16, HIDDEN_SIZE)
     first_grad = dot_nt(h_one[...], inputs[...])
     grads[:, :, HIDDEN_SIZE : LANES - PADDED] = (
@@ -594,7 +601,7 @@
     for piece in got:
         i, inside = min(first // PARITY, count - 1), first - min(first // PARITY, count - 1) * PARITY
         own = kept[i][inside : inside + piece.shape[0]]
-        sums[first : first + piece.shape[0]] = (own.astype(F32) + piece[...].astype(F32)).astype(BF)
+        sums[first : first + piece.shape[0]] = own + piece[...]
         first += piece.shape[0]
     z_first = chunk[-1] // 3 * depth
     side = me[0] & 1
@@ -633,7 +640,7 @@
 
 def half_kernel(kept, got, own, send):
     for k, out in enumerate((own, send)):
-        out[...] = (kept[k].astype(F32) + got[k].astype(F32)).astype(BF)
+        out[...] = kept[k] + got[k]
 
 
 def add_half(kept, got, after=()):
@@ -652,7 +659,7 @@
 def line_kernel(me, early, early_got, late, late_got, *refs):
     outs, sums = refs[:-1], refs[-1]
     count = early.shape[0]
-    sums[:count] = (early[...].astype(F32) + early_got[...].astype(F32)).astype(BF)
+    sums[:count] = early[...] + early_got[...]
     total = late[...].astype(F32) + late_got[...].astype(F32)
     sums[count:] = total[:count].astype(BF)
     extra = total[count]

time: 128 us -> 123 us (0.961)
  Pallas kernels: 70.2 us -> 65.1 us
    pallas_call x1, Pallas kernels: 16.2 us -> 14.7 us  [pilot_pass(): pl.pallas_call(functools.partial(pilot_kernel, level, share), in_specs=[S...]
    pallas_call x2, Pallas kernels: 3.02 us -> 1.66 us  [add_core(): pl.pallas_call(functools.partial(core_kernel, chunk, depth, len(after)),...]
where the time goes in v2:
time: 123 us
  Pallas kernels  65.1 us (53%)
  waiting for transfers between devices  33.3 us (27%)
  starting transfers between devices  17.7 us (14%)
  between operations  3.94 us (3%)
  local copies, waits for them, and re-layouts  2.06 us (2%)
    pallas_call x5, Pallas kernels, critic_pass(): pl.pallas_call(functools.partial(critic_kernel, e, len(after), rows_scale...  35.2 us
    ppermute x18, waiting for transfers between devices, exchange(): return lax.ppermute(value, AXES, [(i, i ^ flip) for i in range(count)])  23.1 us
    pallas_call x1, Pallas kernels, pilot_pass(): pl.pallas_call(functools.partial(pilot_kernel, level, share), in_specs=[S...  14.7 us
    ppermute x18, starting transfers between devices, exchange(): return lax.ppermute(value, AXES, [(i, i ^ flip) for i in range(count)])  14.5 us
    ppermute x4, waiting for transfers between devices, exchange_sides(): lax.ppermute(value, AXES, [(i, i ^ (odd if i % 2 else even)) for i in ran...  7.93 us
    pallas_call x1, Pallas kernels, target_pass(): pl.pallas_call(target_kernel, in_specs=[SCALAR] * 2 + [WHOLE] * 4 + [pl.B...  7.13 us
  transfers between devices with their start and end apart: 25, of which 12 were waited for; matrix products, arithmetic and copies ran while one was open for 1% of the time, Pallas kernels for 39%

profile of v2, /device:TPU:17, one launch (start us, length us, event | category | flops | bytes accessed | tf_op | source)
XLA Modules:
  0.0 123.0 jit_solution(1678599365401470147)
XLA Ops:
  0.7 0.8 pad_maximum_fusion.own
  1.4 1.8 %collective-permute-start.2 = (bf16[32,1024]{1,0:T(8,128)(2,1)S(1)}, bf16[32,1024]{1,0:T(8,128)(2,1)S(1)}, u32[]{:S(2)}, u32[]{:S(2)}) collective-permute-start(bf16[32,1024]{1,0:T(8,128)(2,1)S(1)} %pad_maximum_fusion.own), channel_id=1, source_target_pairs={{0,3},{1,2},{2,1},{3,0},{4,7},{5,6},{6,5},{7,4},{8,11},{9,10},{10,... | collective-permute-start | bytes 196616 | tf_op jit(solution)/shard_map/ppermute | solution.py:861
  3.2 0.3 collective-permute-start.1
  3.5 0.2 collective-permute-start
  4.3 0.7 reshape.85.small
  5.0 1.1 collective-permute-done.2.got_three
  6.1 1.3 %collective-permute-done.1.got_two = bf16[32,1024]{1,0:T(8,128)(2,1)S(1)} collective-permute-done((bf16[32,1024]{1,0:T(8,128)(2,1)S(1)}, bf16[32,1024]{1,0:T(8,128)(2,1)S(1)}, u32[]{:S(2)}, u32[]{:S(2)}) %collective-permute-start.1) | collective-permute-done | bytes 65568 | tf_op jit(solution)/shard_map/ppermute | solution.py:861
  7.4 0.0 copy-start.29
  7.4 0.0 copy-start.31
  7.4 0.1 heads.1.head
  7.5 1.0 copy-done.25
  8.5 0.1 copy-done.26
  8.6 0.1 copy-done.27
  8.7 0.0 copy-done.28
  8.8 14.7 %pilot_pass.1 = (bf16[352,256]{1,0:T(8,128)(2,1)S(1)}, bf16[352,256]{1,0:T(8,128)(2,1)S(1)}, bf16[512,1024]{1,0:T(8,128)(2,1)S(1)}, bf16[512,1024]{1,0:T(8,128)(...) custom-call(s32[1]{0:T(128)} %bitcast.me.refs_1_, s32[1]{0:T(128)} %bitcast.1.me.index, f32[1]{0:T(128)} %copy.65.heat, ...), custom_call_target="tpu_custom_call" | custom-call | flops 14000000000 | bytes 9000000 | tf_op jit(solution)/shard_map/pilot_pass/pallas_call | solution.py:328
  23.5 0.6 collective-permute-start.3
  24.2 7.1 %target_pass.1 = (f32[128,1024]{1,0:T(8,128)S(1)}, bf16[128,1024]{1,0:T(8,128)(2,1)S(1)}) custom-call(s32[1]{0:T(128)} %bitcast.1.me.index, f32[1]{0:T(128)} %copy.65.heat, bf16[512,1024]{1,0:T(8,128)(2,1)S(1)} %get-tuple-element.94.inputs, f32[1,1024]{1,0:T(1,128)S(1)} %get-tuple-element.95.logp, f32[1,4096]{1,0:T(1,128)S(1)} %bitcast.53, ...), custom_call_target="tpu_custom_call" | custom-call | flops 7000000000 | bytes 7000000 | tf_op jit(solution)/shard_map/target_pass/pallas_call | solution.py:208
  31.4 1.3 %collective-permute-start.4 = (bf16[352,256]{1,0:T(8,128)(2,1)S(1)}, bf16[352,256]{1,0:T(8,128)(2,1)S(1)}, u32[]{:S(2)}, u32[]{:S(2)}) collective-permute-start(bf16[352,256]{1,0:T(8,128)(2,1)S(1)} %add_actor.5.a.refs_0_), channel_id=1, source_target_pairs={{0,2},{1,3},{2,0},{3,1},{4,6},{5,7},{6,4},{7,5},{8,10},{9,11},{10,... | collective-permute-start | bytes 540680 | tf_op jit(solution)/shard_map/ppermute | solution.py:811
  32.7 7.0 %critic_pass.5 = (bf16[18,16,1024]{2,1,0:T(8,128)(2,1)S(1)}, bf16[18,16,1024]{2,1,0:T(8,128)(2,1)S(1)}, f32[160,512]{1,0:T(8,128)S(1)}, f32[8,128]{1,0:T(8,128)S(1)}, f32[1,1024]{1,0:T(1,128)S(1)}) custom-call(s32[1]{0:T(128)} %bitcast.me.refs_1_, bf16[512,1024]{1,0:T(8,128)(2,1)S(1)} %get-tuple-element.93.inputs, f32[128,1024]{1,0:T(8,128)S(1)} %get-tuple-element.97.lagged, ...), custom_call_target="tpu_custom_call" | custom-call | flops 7000000000 | bytes 4000000 | tf_op jit(solution)/shard_map/critic_pass/pallas_call | solution.py:554
  39.7 0.4 collective-permute-start.9
  40.2 1.3 %collective-permute-start.5 = (bf16[352,256]{1,0:T(8,128)(2,1)S(1)}, bf16[352,256]{1,0:T(8,128)(2,1)S(1)}, u32[]{:S(2)}, u32[]{:S(2)}) collective-permute-start(bf16[352,256]{1,0:T(8,128)(2,1)S(1)} %add_actor.6.a.refs_0_), channel_id=1, source_target_pairs={{0,4},{1,5},{2,6},{3,7},{4,0},{5,1},{6,2},{7,3},{8,12},{9,13},{10,... | collective-permute-start | bytes 540680 | tf_op jit(solution)/shard_map/ppermute | solution.py:811
  41.5 6.9 %critic_pass.6 = (bf16[18,16,1024]{2,1,0:T(8,128)(2,1)S(1)}, bf16[18,16,1024]{2,1,0:T(8,128)(2,1)S(1)}, f32[160,512]{1,0:T(8,128)S(1)}, f32[8,128]{1,0:T(8,128)S(1)}, f32[1,1024]{1,0:T(1,128)S(1)}) custom-call(s32[1]{0:T(128)} %bitcast.me.refs_1_, bf16[512,1024]{1,0:T(8,128)(2,1)S(1)} %get-tuple-element.93.inputs, f32[128,1024]{1,0:T(8,128)S(1)} %get-tuple-element.97.lagged, ...), custom_call_target="tpu_custom_call" | custom-call | flops 7000000000 | bytes 4000000 | tf_op jit(solution)/shard_map/critic_pass/pallas_call | solution.py:554
  48.4 0.5 collective-permute-start.10
  49.0 1.4 %collective-permute-start.6 = (bf16[352,256]{1,0:T(8,128)(2,1)S(1)}, bf16[352,256]{1,0:T(8,128)(2,1)S(1)}, u32[]{:S(2)}, u32[]{:S(2)}) collective-permute-start(bf16[352,256]{1,0:T(8,128)(2,1)S(1)} %add_actor.7.a.refs_0_), channel_id=1, source_target_pairs={{0,8},{1,9},{2,10},{3,11},{4,12},{5,13},{6,14},{7,15},{8,0},{9,1},... | collective-permute-start | bytes 540680 | tf_op jit(solution)/shard_map/ppermute | solution.py:811
  50.4 7.1 %critic_pass.7 = (bf16[18,16,1024]{2,1,0:T(8,128)(2,1)S(1)}, bf16[18,16,1024]{2,1,0:T(8,128)(2,1)S(1)}, f32[160,512]{1,0:T(8,128)S(1)}, f32[8,128]{1,0:T(8,128)S(1)}, f32[1,1024]{1,0:T(1,128)S(1)}) custom-call(s32[1]{0:T(128)} %bitcast.me.refs_1_, bf16[512,1024]{1,0:T(8,128)(2,1)S(1)} %get-tuple-element.93.inputs, f32[128,1024]{1,0:T(8,128)S(1)} %get-tuple-element.97.lagged, ...), custom_call_target="tpu_custom_call" | custom-call | flops 7000000000 | bytes 4000000 | tf_op jit(solution)/shard_map/critic_pass/pallas_call | solution.py:554
  57.5 0.4 collective-permute-start.11
  57.9 0.0 copy-start.16
  58.0 6.9 %critic_pass.8 = (bf16[18,16,1024]{2,1,0:T(8,128)(2,1)S(1)}, bf16[18,16,1024]{2,1,0:T(8,128)(2,1)S(1)}, f32[160,512]{1,0:T(8,128)S(1)}, f32[8,128]{1,0:T(8,128)S(1)}, f32[1,1024]{1,0:T(1,128)S(1)}) custom-call(s32[1]{0:T(128)} %bitcast.me.refs_1_, bf16[512,1024]{1,0:T(8,128)(2,1)S(1)} %get-tuple-element.93.inputs, f32[128,1024]{1,0:T(8,128)S(1)} %get-tuple-element.97.lagged, ...), custom_call_target="tpu_custom_call" | custom-call | flops 7000000000 | bytes 4000000 | tf_op jit(solution)/shard_map/critic_pass/pallas_call | solution.py:554
  64.9 0.2 collective-permute-start.14
  65.1 0.8 add_core.2
  66.0 0.3 collective-permute-start.12
  66.2 7.2 %critic_pass.9 = (bf16[6,16,1024]{2,1,0:T(8,128)(2,1)S(1)}, bf16[6,16,1024]{2,1,0:T(8,128)(2,1)S(1)}, bf16[6,16,1024]{2,1,0:T(8,128)(2,1)S(1)}, bf16[4,16,1024]{...) custom-call(s32[1]{0:T(128)} %bitcast.me.refs_1_, bf16[512,1024]{1,0:T(8,128)(2,1)S(1)} %get-tuple-element.93.inputs, ...), custom_call_target="tpu_custom_call" | custom-call | flops 7000000000 | bytes 4000000 | tf_op jit(solution)/shard_map/critic_pass/pallas_call | solution.py:554
  73.5 0.7 collective-permute-start.15
  74.2 0.1 collective-permute-start.16
  74.2 0.4 collective-permute-start.17
  74.7 1.1 collective-permute-done.12.refs_1_
  75.7 1.2 collective-permute-start.18
  77.0 0.1 add_half.2
  77.0 0.9 collective-permute-done.18.refs_9_
  78.0 0.8 add_core.3
  78.9 0.3 collective-permute-start.19
  79.2 0.2 collective-permute-start.13
  79.4 0.1 collective-permute-start.7
  79.4 8.0 %collective-permute-done.7.b = bf16[352,256]{1,0:T(8,128)(2,1)S(1)} collective-permute-done((bf16[352,256]{1,0:T(8,128)(2,1)S(1)}, bf16[352,256]{1,0:T(8,128)(2,1)S(1)}, u32[]{:S(2)}, u32[]{:S(2)}) %collective-permute-start.7) | collective-permute-done | bytes 180256 | tf_op jit(solution)/shard_map/ppermute | solution.py:811
  87.4 0.9 collective-permute-done.13.refs_1_.refs_3_
  88.3 4.5 %collective-permute-done.19.refs_3_ = bf16[2,11,16,1024]{3,2,1,0:T(8,128)(2,1)S(1)} collective-permute-done((bf16[2,11,16,1024]{3,2,1,0:T(8,128)(2,1)S(1)}, bf16[2,11,16,1024]{3,2,1,0:T(8,128)(2,1)S(1)}, u32[]{:S(2)}, u32[]{:S(2)}) %collective-permute-start.19) | collective-permute-done | bytes 720928 | tf_op jit(solution)/shard_map/ppermute | solution.py:816
  92.9 0.1 add_half.3
  93.1 0.3 collective-permute-start.20
  93.4 1.5 %collective-permute-start.8 = (bf16[352,256]{1,0:T(8,128)(2,1)S(1)}, bf16[352,256]{1,0:T(8,128)(2,1)S(1)}, u32[]{:S(2)}, u32[]{:S(2)}) collective-permute-start(bf16[352,256]{1,0:T(8,128)(2,1)S(1)} %add_actor.9.own.refs_0_), channel_id=1, source_target_pairs={{0,1},{1,0},{2,3},{3,2},{4,5},{5,4},{6,7},{7,6},{8,9},{9,8},{10,11... | collective-permute-start | bytes 540680 | tf_op jit(solution)/shard_map/ppermute | solution.py:811
  95.7 0.1 pad_maximum_fusion.1.factors
  95.8 0.2 collective-permute-done.8.peer
  96.0 2.4 %actor_update.1 = (f32[666,256]{1,0:T(8,128)}, f32[666,256]{1,0:T(8,128)}, f32[666,256]{1,0:T(8,128)}, f32[8,128]{1,0:T(8,128)S(1)}) custom-call(s32[1]{0:T(128)} %bitcast.me.refs_1_, f32[2]{0:T(128)S(1)} %pad_maximum_fusion.1.factors, bf16[352,256]{1,0:T(8,128)(2,1)S(1)} %add_actor.9.own.refs_0_, bf16[352,256]{1,0:T(8,128)(2,1)S(1)} %collective-permute-done.8.peer, ...), custom_call_target="tpu_custom_call" | custom-call | flops 2000000 | bytes 5000000 | tf_op jit(solution)/shard_map/actor_update/pallas_call | solution.py:765
  98.4 1.4 %collective-permute-done.20.refs_5_ = bf16[11,16,1024]{2,1,0:T(8,128)(2,1)S(1)} collective-permute-done((bf16[11,16,1024]{2,1,0:T(8,128)(2,1)S(1)}, bf16[11,16,1024]{2,1,0:T(8,128)(2,1)S(1)}, u32[]{:S(2)}, u32[]{:S(2)}) %collective-permute-start.20) | collective-permute-done | bytes 360480 | tf_op jit(solution)/shard_map/ppermute | solution.py:816
  99.8 0.3 add_line.1
  100.0 0.2 collective-permute-start.21
  100.3 0.1 collective-permute-start.22
  100.3 2.4 %collective-permute-start.23 = (bf16[5,16,1024]{2,1,0:T(8,128)(2,1)S(1)}, bf16[5,16,1024]{2,1,0:T(8,128)(2,1)S(1)}, u32[]{:S(2)}, u32[]{:S(2)}) collective-permute-start(bf16[5,16,1024]{2,1,0:T(8,128)(2,1)S(1)} %get-tuple-element.135), channel_id=1, source_target_pairs={{0,24},{1,25},{2,26},{3,27},{4,28},{5,29},{6,30},{7,31},{8,16},{9,... | collective-permute-start | bytes 491528 | tf_op jit(solution)/shard_map/ppermute | solution.py:811
  102.7 1.5 %collective-permute-done.21.refs_1_ = bf16[5,16,1024]{2,1,0:T(8,128)(2,1)S(1)} collective-permute-done((bf16[5,16,1024]{2,1,0:T(8,128)(2,1)S(1)}, bf16[5,16,1024]{2,1,0:T(8,128)(2,1)S(1)}, u32[]{:S(2)}, u32[]{:S(2)}) %collective-permute-start.21) | collective-permute-done | bytes 163872 | tf_op jit(solution)/shard_map/ppermute | solution.py:811
  104.3 3.0 %collective-permute-done.22.refs_2_ = bf16[5,16,1024]{2,1,0:T(8,128)(2,1)S(1)} collective-permute-done((bf16[5,16,1024]{2,1,0:T(8,128)(2,1)S(1)}, bf16[5,16,1024]{2,1,0:T(8,128)(2,1)S(1)}, u32[]{:S(2)}, u32[]{:S(2)}) %collective-permute-start.22) | collective-permute-done | bytes 163872 | tf_op jit(solution)/shard_map/ppermute | solution.py:811
  107.3 9.5 %collective-permute-done.23.refs_3_ = bf16[5,16,1024]{2,1,0:T(8,128)(2,1)S(1)} collective-permute-done((bf16[5,16,1024]{2,1,0:T(8,128)(2,1)S(1)}, bf16[5,16,1024]{2,1,0:T(8,128)(2,1)S(1)}, u32[]{:S(2)}, u32[]{:S(2)}) %collective-permute-start.23) | collective-permute-done | bytes 163872 | tf_op jit(solution)/shard_map/ppermute | solution.py:811
  116.8 0.1 sum_row.1.row_own
  116.9 1.6 %collective-permute-start.24 = (f32[8,128]{1,0:T(8,128)S(1)}, f32[8,128]{1,0:T(8,128)S(1)}, u32[]{:S(2)}, u32[]{:S(2)}) collective-permute-start(f32[8,128]{1,0:T(8,128)S(1)} %sum_row.1.row_own), channel_id=1, source_target_pairs={{0,1},{1,0},{2,3},{3,2},{4,5},{5,4},{6,7},{7,6},{8,9},{9,8},{10,11... | collective-permute-start | bytes 12296 | tf_op jit(solution)/shard_map/ppermute | solution.py:811
  119.9 1.8 %update.1 = (f32[80,393]{1,0:T(8,128)}, f32[80,393]{1,0:T(8,128)}, f32[80,393]{1,0:T(8,128)}, f32[80,512]{1,0:T(8,128)}, f32[80,512]{1,0:T(8,128)}, /*index=5*/f...) custom-call(f32[2]{0:T(128)S(1)} %pad_maximum_fusion.1.factors, ...), custom_call_target="tpu_custom_call" | custom-call | flops 2000000 | bytes 6000000 | tf_op jit(solution)/shard_map/update/pallas_call | solution.py:742
  121.7 1.2 %small_update.1 = (f32[1,1]{1,0:T(1,128)}, f32[674]{0:T(1024)}, f32[674]{0:T(1024)}, f32[674]{0:T(1024)}, f32[1,1]{1,0:T(1,128)}, /*index=5*/f32[1,1]{1,0:T(1,128)}, f32[1,1]{1,0:T(1,128)}) custom-call(s32[1]{0:T(128)} %bitcast.me.refs_1_, f32[2]{0:T(128)S(1)} %pad_maximum_fusion.1.factors, f32[8,128]{1,0:T(8,128)S(1)} %sum_row.1.row_own, ...), custom_call_target="tpu_custom_call" | custom-call | flops 1000000 | bytes 100000 | tf_op jit(solution)/shard_map/small_update/pallas_call | solution.py:797
  (81 shorter events, 0.5 us)
Async XLA Ops:
  1.4 4.6 %collective-permute-start.2 = (bf16[32,1024]{1,0:T(8,128)(2,1)S(1)}, bf16[32,1024]{1,0:T(8,128)(2,1)S(1)}, u32[]{:S(2)}, u32[]{:S(2)}) collective-permute-start(bf16[32,1024]{1,0:T(8,128)(2,1)S(1)} %pad_maximum_fusion.own), channel_id=1, source_target_pairs={{0,3},{1,2},{2,1},{3,0},{4,7},{5,6},{6,5},{7,4},{8,11},{9,10},{10,... | collective-permute-start | bytes 196616 | tf_op jit(solution)/shard_map/ppermute | solution.py:861
  3.2 4.1 %collective-permute-start.1 = (bf16[32,1024]{1,0:T(8,128)(2,1)S(1)}, bf16[32,1024]{1,0:T(8,128)(2,1)S(1)}, u32[]{:S(2)}, u32[]{:S(2)}) collective-permute-start(bf16[32,1024]{1,0:T(8,128)(2,1)S(1)} %pad_maximum_fusion.own), channel_id=1, source_target_pairs={{0,2},{1,3},{2,0},{3,1},{4,6},{5,7},{6,4},{7,5},{8,10},{9,11},{10,... | collective-permute-start | bytes 196616 | tf_op jit(solution)/shard_map/ppermute | solution.py:861
  3.5 3.9 %collective-permute-start = (bf16[32,1024]{1,0:T(8,128)(2,1)S(1)}, bf16[32,1024]{1,0:T(8,128)(2,1)S(1)}, u32[]{:S(2)}, u32[]{:S(2)}) collective-permute-start(bf16[32,1024]{1,0:T(8,128)(2,1)S(1)} %pad_maximum_fusion.own), channel_id=1, source_target_pairs={{0,1},{1,0},{2,3},{3,2},{4,5},{5,4},{6,7},{7,6},{8,9},{9,8},{10,11... | collective-permute-start | bytes 196616 | tf_op jit(solution)/shard_map/ppermute | solution.py:861
  7.4 1.1 copy-start.25
  7.4 1.2 copy-start.26
  7.4 1.3 %copy-start.27 = (bf16[666,256]{1,0:T(8,128)(2,1)S(1)}, bf16[666,256]{1,0:T(8,128)(2,1)}, u32[]{:S(2)}) copy-start(bf16[666,256]{1,0:T(8,128)(2,1)} %actor.1) | copy-start | bytes 1022980
  7.4 1.3 %copy-start.28 = (f32[1024,17]{0,1:T(8,128)S(1)}, f32[1024,17]{0,1:T(8,128)}, u32[]{:S(2)}) copy-start(f32[1024,17]{0,1:T(8,128)} %param.44) | copy-start | bytes 208900
  7.4 1.3 %copy-start.29 = (bf16[1024,17]{0,1:T(8,128)(2,1)S(1)}, bf16[1024,17]{0,1:T(8,128)(2,1)}, u32[]{:S(2)}) copy-start(bf16[1024,17]{0,1:T(8,128)(2,1)} %param.43) | copy-start | bytes 104452
  7.4 1.3 %copy-start.31 = (f32[2,2560]{1,0:T(2,128)S(1)}, f32[2,2560]{1,0:T(2,128)}, u32[]{:S(2)}) copy-start(f32[2,2560]{1,0:T(2,128)} %bias.13) | copy-start | bytes 61444
  7.4 1.3 %copy-start.34 = (f32[128]{0:T(128)S(1)}, f32[128]{0:T(128)}, u32[]{:S(2)}) copy-start(f32[128]{0:T(128)} %param.58) | copy-start | bytes 1540
  8.7 15.4 %copy-start.20 = (bf16[512,2560]{1,0:T(8,128)(2,1)S(1)}, bf16[512,2560]{1,0:T(8,128)(2,1)}, u32[]{:S(2)}) copy-start(bf16[512,2560]{1,0:T(8,128)(2,1)} %second.6) | copy-start | bytes 7864324
  8.7 15.4 %copy-start.22 = (s32[4096,125]{1,0:T(8,128)S(1)}, s32[4096,125]{1,0:T(8,128)}, u32[]{:S(2)}) copy-start(s32[4096,125]{1,0:T(8,128)} %order_in.1) | copy-start | bytes 6144004
  8.7 15.4 %copy-start.23 = (bf16[393,2560]{1,0:T(8,128)(2,1)S(1)}, bf16[393,2560]{1,0:T(8,128)(2,1)}, u32[]{:S(2)}) copy-start(bf16[393,2560]{1,0:T(8,128)(2,1)} %first.6) | copy-start | bytes 6036484
  8.7 15.4 %copy-start.30 = (f32[2,2560]{1,0:T(2,128)S(1)}, f32[2,2560]{1,0:T(2,128)}, u32[]{:S(2)}) copy-start(f32[2,2560]{1,0:T(2,128)} %bias.8) | copy-start | bytes 61444
  8.7 15.4 %copy-start.32 = (f32[4096]{0:T(1024)S(1)}, f32[4096]{0:T(1024)}, u32[]{:S(2)}) copy-start(f32[4096]{0:T(1024)} %param.47) | copy-start | bytes 49156
  8.8 15.4 %copy-start.33 = (s32[4096]{0:T(1024)S(1)}, s32[4096]{0:T(1024)}, u32[]{:S(2)}) copy-start(s32[4096]{0:T(1024)} %param.48) | copy-start | bytes 49156
  23.5 7.8 %collective-permute-start.3 = (bf16[352,256]{1,0:T(8,128)(2,1)S(1)}, bf16[352,256]{1,0:T(8,128)(2,1)S(1)}, u32[]{:S(2)}, u32[]{:S(2)}) collective-permute-start(bf16[352,256]{1,0:T(8,128)(2,1)S(1)} %get-tuple-element.91), channel_id=1, source_target_pairs={{0,1},{1,0},{2,3},{3,2},{4,5},{5,4},{6,7},{7,6},{8,9},{9,8},{10,11... | collective-permute-start | bytes 540680 | tf_op jit(solution)/shard_map/ppermute | solution.py:811
  24.2 8.5 %copy-start.21 = (bf16[512,2560]{1,0:T(8,128)(2,1)S(1)}, bf16[512,2560]{1,0:T(8,128)(2,1)}, u32[]{:S(2)}) copy-start(bf16[512,2560]{1,0:T(8,128)(2,1)} %second.11) | copy-start | bytes 7864324
  24.2 8.5 %copy-start.24 = (bf16[393,2560]{1,0:T(8,128)(2,1)S(1)}, bf16[393,2560]{1,0:T(8,128)(2,1)}, u32[]{:S(2)}) copy-start(bf16[393,2560]{1,0:T(8,128)(2,1)} %first.11) | copy-start | bytes 6036484
  31.4 8.7 %collective-permute-start.4 = (bf16[352,256]{1,0:T(8,128)(2,1)S(1)}, bf16[352,256]{1,0:T(8,128)(2,1)S(1)}, u32[]{:S(2)}, u32[]{:S(2)}) collective-permute-start(bf16[352,256]{1,0:T(8,128)(2,1)S(1)} %add_actor.5.a.refs_0_), channel_id=1, source_target_pairs={{0,2},{1,3},{2,0},{3,1},{4,6},{5,7},{6,4},{7,5},{8,10},{9,11},{10,... | collective-permute-start | bytes 540680 | tf_op jit(solution)/shard_map/ppermute | solution.py:811
  39.7 25.4 %collective-permute-start.9 = (bf16[18,16,1024]{2,1,0:T(8,128)(2,1)S(1)}, bf16[18,16,1024]{2,1,0:T(8,128)(2,1)S(1)}, u32[]{:S(2)}, u32[]{:S(2)}) collective-permute-start(bf16[18,16,1024]{2,1,0:T(8,128)(2,1)S(1)} %get-tuple-element.108), channel_id=1, source_target_pairs={{0,1},{1,0},{2,3},{3,2},{4,5},{5,4},{6,7},{7,6},{8,9},{9,8},{10,11... | collective-permute-start | bytes 1769480 | tf_op jit(solution)/shard_map/ppermute | solution.py:811
  40.2 8.7 %collective-permute-start.5 = (bf16[352,256]{1,0:T(8,128)(2,1)S(1)}, bf16[352,256]{1,0:T(8,128)(2,1)S(1)}, u32[]{:S(2)}, u32[]{:S(2)}) collective-permute-start(bf16[352,256]{1,0:T(8,128)(2,1)S(1)} %add_actor.6.a.refs_0_), channel_id=1, source_target_pairs={{0,4},{1,5},{2,6},{3,7},{4,0},{5,1},{6,2},{7,3},{8,12},{9,13},{10,... | collective-permute-start | bytes 540680 | tf_op jit(solution)/shard_map/ppermute | solution.py:811
  48.4 16.7 %collective-permute-start.10 = (bf16[18,16,1024]{2,1,0:T(8,128)(2,1)S(1)}, bf16[18,16,1024]{2,1,0:T(8,128)(2,1)S(1)}, u32[]{:S(2)}, u32[]{:S(2)}) collective-permute-start(bf16[18,16,1024]{2,1,0:T(8,128)(2,1)S(1)} %get-tuple-element.109), channel_id=1, source_target_pairs={{0,1},{1,0},{2,3},{3,2},{4,5},{5,4},{6,7},{7,6},{8,9},{9,8},{10,11... | collective-permute-start | bytes 1769480 | tf_op jit(solution)/shard_map/ppermute | solution.py:811
  49.0 8.9 %collective-permute-start.6 = (bf16[352,256]{1,0:T(8,128)(2,1)S(1)}, bf16[352,256]{1,0:T(8,128)(2,1)S(1)}, u32[]{:S(2)}, u32[]{:S(2)}) collective-permute-start(bf16[352,256]{1,0:T(8,128)(2,1)S(1)} %add_actor.7.a.refs_0_), channel_id=1, source_target_pairs={{0,8},{1,9},{2,10},{3,11},{4,12},{5,13},{6,14},{7,15},{8,0},{9,1},... | collective-permute-start | bytes 540680 | tf_op jit(solution)/shard_map/ppermute | solution.py:811
  57.5 7.7 %collective-permute-start.11 = (bf16[18,16,1024]{2,1,0:T(8,128)(2,1)S(1)}, bf16[18,16,1024]{2,1,0:T(8,128)(2,1)S(1)}, u32[]{:S(2)}, u32[]{:S(2)}) collective-permute-start(bf16[18,16,1024]{2,1,0:T(8,128)(2,1)S(1)} %get-tuple-element.110), channel_id=1, source_target_pairs={{0,1},{1,0},{2,3},{3,2},{4,5},{5,4},{6,7},{7,6},{8,9},{9,8},{10,11... | collective-permute-start | bytes 1769480 | tf_op jit(solution)/shard_map/ppermute | solution.py:811
  57.9 7.2 %copy-start.16 = (s32[160]{0:T(256)S(1)}, s32[160]{0:T(256)}, u32[]{:S(2)}) copy-start(s32[160]{0:T(256)} %constant.21.clone.places) | copy-start | bytes 1924
  64.9 13.1 %collective-permute-start.14 = (bf16[18,16,1024]{2,1,0:T(8,128)(2,1)S(1)}, bf16[18,16,1024]{2,1,0:T(8,128)(2,1)S(1)}, u32[]{:S(2)}, u32[]{:S(2)}) collective-permute-start(bf16[18,16,1024]{2,1,0:T(8,128)(2,1)S(1)} %get-tuple-element.123), channel_id=1, source_target_pairs={{0,1},{1,0},{2,3},{3,2},{4,5},{5,4},{6,7},{7,6},{8,9},{9,8},{10,11... | collective-permute-start | bytes 1769480 | tf_op jit(solution)/shard_map/ppermute | solution.py:811
  66.0 9.8 %collective-permute-start.12 = (bf16[2,10,16,1024]{3,2,1,0:T(8,128)(2,1)S(1)}, bf16[2,10,16,1024]{3,2,1,0:T(8,128)(2,1)S(1)}, u32[]{:S(2)}, u32[]{:S(2)}) collective-permute-start(bf16[2,10,16,1024]{3,2,1,0:T(8,128)(2,1)S(1)} %get-tuple-element.112), channel_id=1, source_target_pairs={{0,2},{1,5},{2,0},{3,7},{4,6},{5,1},{6,4},{7,3},{8,10},{9,13},{10,... | collective-permute-start | bytes 1966088 | tf_op jit(solution)/shard_map/ppermute | solution.py:816
  66.2 11.7 %copy-start.15 = (s32[160]{0:T(256)S(1)}, s32[160]{0:T(256)}, u32[]{:S(2)}) copy-start(s32[160]{0:T(256)} %constant.22.clone.places) | copy-start | bytes 1924
  73.5 4.5 %collective-permute-start.15 = (bf16[6,16,1024]{2,1,0:T(8,128)(2,1)S(1)}, bf16[6,16,1024]{2,1,0:T(8,128)(2,1)S(1)}, u32[]{:S(2)}, u32[]{:S(2)}) collective-permute-start(bf16[6,16,1024]{2,1,0:T(8,128)(2,1)S(1)} %get-tuple-element.124), channel_id=1, source_target_pairs={{0,1},{1,0},{2,3},{3,2},{4,5},{5,4},{6,7},{7,6},{8,9},{9,8},{10,11... | collective-permute-start | bytes 589832 | tf_op jit(solution)/shard_map/ppermute | solution.py:811
  74.2 3.8 %collective-permute-start.16 = (bf16[6,16,1024]{2,1,0:T(8,128)(2,1)S(1)}, bf16[6,16,1024]{2,1,0:T(8,128)(2,1)S(1)}, u32[]{:S(2)}, u32[]{:S(2)}) collective-permute-start(bf16[6,16,1024]{2,1,0:T(8,128)(2,1)S(1)} %get-tuple-element.125), channel_id=1, source_target_pairs={{0,1},{1,0},{2,3},{3,2},{4,5},{5,4},{6,7},{7,6},{8,9},{9,8},{10,11... | collective-permute-start | bytes 589832 | tf_op jit(solution)/shard_map/ppermute | solution.py:811
  74.2 3.7 %collective-permute-start.17 = (bf16[6,16,1024]{2,1,0:T(8,128)(2,1)S(1)}, bf16[6,16,1024]{2,1,0:T(8,128)(2,1)S(1)}, u32[]{:S(2)}, u32[]{:S(2)}) collective-permute-start(bf16[6,16,1024]{2,1,0:T(8,128)(2,1)S(1)} %get-tuple-element.126), channel_id=1, source_target_pairs={{0,1},{1,0},{2,3},{3,2},{4,5},{5,4},{6,7},{7,6},{8,9},{9,8},{10,11... | collective-permute-start | bytes 589832 | tf_op jit(solution)/shard_map/ppermute | solution.py:811
  75.7 2.2 %collective-permute-start.18 = (bf16[4,16,1024]{2,1,0:T(8,128)(2,1)S(1)}, bf16[4,16,1024]{2,1,0:T(8,128)(2,1)S(1)}, u32[]{:S(2)}, u32[]{:S(2)}) collective-permute-start(bf16[4,16,1024]{2,1,0:T(8,128)(2,1)S(1)} %get-tuple-element.127), channel_id=1, source_target_pairs={{0,1},{1,0},{2,3},{3,2},{4,5},{5,4},{6,7},{7,6},{8,9},{9,8},{10,11... | collective-permute-start | bytes 393224 | tf_op jit(solution)/shard_map/ppermute | solution.py:811
  78.0 18.0 %copy-start = (f32[666,256]{1,0:T(8,128)S(1)}, f32[666,256]{1,0:T(8,128)}, u32[]{:S(2)}) copy-start(f32[666,256]{1,0:T(8,128)} %refs_0_.2) | copy-start | bytes 2045956
  78.0 18.0 %copy-start.1 = (f32[666,256]{1,0:T(8,128)S(1)}, f32[666,256]{1,0:T(8,128)}, u32[]{:S(2)}) copy-start(f32[666,256]{1,0:T(8,128)} %refs_1_.2) | copy-start | bytes 2045956
  78.0 18.0 %copy-start.2 = (f32[666,256]{1,0:T(8,128)S(1)}, f32[666,256]{1,0:T(8,128)}, u32[]{:S(2)}) copy-start(f32[666,256]{1,0:T(8,128)} %refs_2_.2) | copy-start | bytes 2045956
  78.9 14.0 %collective-permute-start.19 = (bf16[2,11,16,1024]{3,2,1,0:T(8,128)(2,1)S(1)}, bf16[2,11,16,1024]{3,2,1,0:T(8,128)(2,1)S(1)}, u32[]{:S(2)}, u32[]{:S(2)}) collective-permute-start(bf16[2,11,16,1024]{3,2,1,0:T(8,128)(2,1)S(1)} %get-tuple-element.129), channel_id=1, source_target_pairs={{0,2},{1,5},{2,0},{3,7},{4,6},{5,1},{6,4},{7,3},{8,10},{9,13},{10,... | collective-permute-start | bytes 2162696 | tf_op jit(solution)/shard_map/ppermute | solution.py:816
  79.2 9.2 %collective-permute-start.13 = (bf16[10,16,1024]{2,1,0:T(8,128)(2,1)S(1)}, bf16[10,16,1024]{2,1,0:T(8,128)(2,1)S(1)}, u32[]{:S(2)}, u32[]{:S(2)}) collective-permute-start(bf16[10,16,1024]{2,1,0:T(8,128)(2,1)S(1)} %get-tuple-element.114), channel_id=1, source_target_pairs={{0,4},{1,3},{2,6},{3,1},{4,0},{5,7},{6,2},{7,5},{8,12},{9,11},{10,... | collective-permute-start | bytes 983048 | tf_op jit(solution)/shard_map/ppermute | solution.py:816
  79.4 8.0 %collective-permute-start.7 = (bf16[352,256]{1,0:T(8,128)(2,1)S(1)}, bf16[352,256]{1,0:T(8,128)(2,1)S(1)}, u32[]{:S(2)}, u32[]{:S(2)}) collective-permute-start(bf16[352,256]{1,0:T(8,128)(2,1)S(1)} %add_actor.8.a.refs_0_), channel_id=1, source_target_pairs={{0,16},{1,17},{2,18},{3,19},{4,20},{5,21},{6,22},{7,23},{8,24},{9,... | collective-permute-start | bytes 540680 | tf_op jit(solution)/shard_map/ppermute | solution.py:811
  93.0 26.8 %copy-start.3 = (f32[393,80]{0,1:T(8,128)S(1)}, f32[393,80]{0,1:T(8,128)}, u32[]{:S(2)}) copy-start(f32[393,80]{0,1:T(8,128)} %param.61) | copy-start | bytes 377284
  93.0 26.8 %copy-start.4 = (f32[393,80]{0,1:T(8,128)S(1)}, f32[393,80]{0,1:T(8,128)}, u32[]{:S(2)}) copy-start(f32[393,80]{0,1:T(8,128)} %param.62) | copy-start | bytes 377284
  93.0 26.8 %copy-start.5 = (f32[393,80]{0,1:T(8,128)S(1)}, f32[393,80]{0,1:T(8,128)}, u32[]{:S(2)}) copy-start(f32[393,80]{0,1:T(8,128)} %param.63) | copy-start | bytes 377284
  93.0 26.8 %copy-start.6 = (f32[512,80]{0,1:T(8,128)S(1)}, f32[512,80]{0,1:T(8,128)}, u32[]{:S(2)}) copy-start(f32[512,80]{0,1:T(8,128)} %param.64) | copy-start | bytes 491524
  93.0 26.8 %copy-start.7 = (f32[512,80]{0,1:T(8,128)S(1)}, f32[512,80]{0,1:T(8,128)}, u32[]{:S(2)}) copy-start(f32[512,80]{0,1:T(8,128)} %param.65) | copy-start | bytes 491524
  93.0 26.8 %copy-start.8 = (f32[512,80]{0,1:T(8,128)S(1)}, f32[512,80]{0,1:T(8,128)}, u32[]{:S(2)}) copy-start(f32[512,80]{0,1:T(8,128)} %param.66) | copy-start | bytes 491524
  93.1 26.8 %copy-start.9 = (f32[64,32]{0,1:T(8,128)S(1)}, f32[64,32]{0,1:T(8,128)}, u32[]{:S(2)}) copy-start(f32[64,32]{0,1:T(8,128)} %param.70) | copy-start | bytes 24580
  93.1 26.8 %copy-start.10 = (f32[64,32]{0,1:T(8,128)S(1)}, f32[64,32]{0,1:T(8,128)}, u32[]{:S(2)}) copy-start(f32[64,32]{0,1:T(8,128)} %param.71) | copy-start | bytes 24580
  93.1 26.8 %copy-start.11 = (f32[64,32]{0,1:T(8,128)S(1)}, f32[64,32]{0,1:T(8,128)}, u32[]{:S(2)}) copy-start(f32[64,32]{0,1:T(8,128)} %param.72) | copy-start | bytes 24580
  93.1 26.8 %copy-start.17 = (f32[2,80]{1,0:T(2,128)S(1)}, f32[2,80]{1,0:T(2,128)}, u32[]{:S(2)}) copy-start(f32[2,80]{1,0:T(2,128)} %refs_10_.1) | copy-start | bytes 1924
  93.1 26.8 %copy-start.18 = (f32[2,80]{1,0:T(2,128)S(1)}, f32[2,80]{1,0:T(2,128)}, u32[]{:S(2)}) copy-start(f32[2,80]{1,0:T(2,128)} %refs_11_.1) | copy-start | bytes 1924
  93.1 26.8 %copy-start.19 = (f32[2,80]{1,0:T(2,128)S(1)}, f32[2,80]{1,0:T(2,128)}, u32[]{:S(2)}) copy-start(f32[2,80]{1,0:T(2,128)} %refs_12_.1) | copy-start | bytes 1924
  93.1 6.6 %collective-permute-start.20 = (bf16[11,16,1024]{2,1,0:T(8,128)(2,1)S(1)}, bf16[11,16,1024]{2,1,0:T(8,128)(2,1)S(1)}, u32[]{:S(2)}, u32[]{:S(2)}) collective-permute-start(bf16[11,16,1024]{2,1,0:T(8,128)(2,1)S(1)} %get-tuple-element.131), channel_id=1, source_target_pairs={{0,4},{1,3},{2,6},{3,1},{4,0},{5,7},{6,2},{7,5},{8,12},{9,11},{10,... | collective-permute-start | bytes 1081352 | tf_op jit(solution)/shard_map/ppermute | solution.py:816
  93.4 2.6 %collective-permute-start.8 = (bf16[352,256]{1,0:T(8,128)(2,1)S(1)}, bf16[352,256]{1,0:T(8,128)(2,1)S(1)}, u32[]{:S(2)}, u32[]{:S(2)}) collective-permute-start(bf16[352,256]{1,0:T(8,128)(2,1)S(1)} %add_actor.9.own.refs_0_), channel_id=1, source_target_pairs={{0,1},{1,0},{2,3},{3,2},{4,5},{5,4},{6,7},{7,6},{8,9},{9,8},{10,11... | collective-permute-start | bytes 540680 | tf_op jit(solution)/shard_map/ppermute | solution.py:811
  95.8 25.9 %copy-start.12 = (f32[674]{0:T(1024)S(1)}, f32[674]{0:T(1024)}, u32[]{:S(2)}) copy-start(f32[674]{0:T(1024)} %refs_0_.3) | copy-start | bytes 8092
  95.8 25.9 %copy-start.13 = (f32[674]{0:T(1024)S(1)}, f32[674]{0:T(1024)}, u32[]{:S(2)}) copy-start(f32[674]{0:T(1024)} %refs_1_.3) | copy-start | bytes 8092
  95.8 25.9 %copy-start.14 = (f32[674]{0:T(1024)S(1)}, f32[674]{0:T(1024)}, u32[]{:S(2)}) copy-start(f32[674]{0:T(1024)} %refs_2_.3) | copy-start | bytes 8092
  100.0 4.2 %collective-permute-start.21 = (bf16[5,16,1024]{2,1,0:T(8,128)(2,1)S(1)}, bf16[5,16,1024]{2,1,0:T(8,128)(2,1)S(1)}, u32[]{:S(2)}, u32[]{:S(2)}) collective-permute-start(bf16[5,16,1024]{2,1,0:T(8,128)(2,1)S(1)} %get-tuple-element.133), channel_id=1, source_target_pairs={{0,8},{1,9},{2,10},{3,11},{4,12},{5,13},{6,14},{7,15},{8,0},{9,1},... | collective-permute-start | bytes 491528 | tf_op jit(solution)/shard_map/ppermute | solution.py:811
  100.3 7.0 %collective-permute-start.22 = (bf16[5,16,1024]{2,1,0:T(8,128)(2,1)S(1)}, bf16[5,16,1024]{2,1,0:T(8,128)(2,1)S(1)}, u32[]{:S(2)}, u32[]{:S(2)}) collective-permute-start(bf16[5,16,1024]{2,1,0:T(8,128)(2,1)S(1)} %get-tuple-element.134), channel_id=1, source_target_pairs={{0,16},{1,17},{2,18},{3,19},{4,20},{5,21},{6,22},{7,23},{8,24},{9,... | collective-permute-start | bytes 491528 | tf_op jit(solution)/shard_map/ppermute | solution.py:811
  100.3 16.4 %collective-permute-start.23 = (bf16[5,16,1024]{2,1,0:T(8,128)(2,1)S(1)}, bf16[5,16,1024]{2,1,0:T(8,128)(2,1)S(1)}, u32[]{:S(2)}, u32[]{:S(2)}) collective-permute-start(bf16[5,16,1024]{2,1,0:T(8,128)(2,1)S(1)} %get-tuple-element.135), channel_id=1, source_target_pairs={{0,24},{1,25},{2,26},{3,27},{4,28},{5,29},{6,30},{7,31},{8,16},{9,... | collective-permute-start | bytes 491528 | tf_op jit(solution)/shard_map/ppermute | solution.py:811
  116.9 4.8 %collective-permute-start.24 = (f32[8,128]{1,0:T(8,128)S(1)}, f32[8,128]{1,0:T(8,128)S(1)}, u32[]{:S(2)}, u32[]{:S(2)}) collective-permute-start(f32[8,128]{1,0:T(8,128)S(1)} %sum_row.1.row_own), channel_id=1, source_target_pairs={{0,1},{1,0},{2,3},{3,2},{4,5},{5,4},{6,7},{7,6},{8,9},{9,8},{10,11... | collective-permute-start | bytes 12296 | tf_op jit(solution)/shard_map/ppermute | solution.py:811

commit v3 on v2

--- a/solution.py
+++ b/solution.py
@@ -276,8 +276,8 @@
         for part in tiles(rows):
             h_one = relu(dot_tn(filled[...], inputs[:, part]))
             h_two = relu(dot_tn(w_two, h_one) + b_two)
-            weighted = h_two.astype(F32) * weight
-            total[:, part] += jnp.sum(weighted.reshape(-1, 8, weighted.shape[1]), axis=0)
+            weighted = (h_two * weight.astype(BF)).reshape(8, -1, 16, h_two.shape[1])
+            total[:, part] += jnp.sum(tree([weighted[i] for i in range(8)]).astype(F32), axis=0)
             dz_two = jnp.where(h_two > 0, push.astype(BF), jnp.zeros((), BF))
             dz_one = gate(h_one, dot_nn(w_two, dz_two))
             dact[:, part] += dot_nn(first[OBS_DIM // 16 * 16 :, lanes], dz_one)
@@ -338,7 +338,7 @@
             pltpu.VMEM((32, rows), F32),
             pltpu.VMEM((32, HIDDEN_SIZE), F32),
             pltpu.VMEM((INPUTS - OBS_DIM // 16 * 16, rows), F32),
-            pltpu.VMEM((8, rows), F32),
+            pltpu.VMEM((16, rows), F32),
             pltpu.VMEM((40, rows), F32),
             pltpu.VMEM((2 * HALF, ACTOR_HIDDEN), F32),
             pltpu.VMEM((8, PADDED), F32),
@@ -356,7 +356,7 @@
 
 
 def pair_terms(q_ref, lagged, keep, parts, rows):
-    def group(i, carry):
+    def group(i, loss):
         part = pl.ds(pl.multiple_of(i * PADDED, PADDED), PADDED)
         q = q_ref[:, part]
         shift = jnp.sum(q, axis=0, keepdims=True) * (1.0 / QUANTS)
@@ -376,15 +376,20 @@
             parts[j * 16 : j * 16 + 16, part] = g[0] + g[1]
             h = h[:4] + h[4:]
             h = h[:2] + h[2:]
-            parts[(QUANTS + j) * 16 : (QUANTS + j) * 16 + 16, part] = h[0] + h[1]
-        return carry
-
-    lax.fori_loop(0, rows // PADDED, group, 0, unroll=2)
-    shape = (48, 2 * QUANTS * 16)
+            h = h[0] + h[1]
+            if j % 2:
+                h = h + waiting
+            if j % 2 or j == QUANTS - 1:
+                h = h.astype(F32)
+                loss = loss + (h[:8] + h[8:])
+            waiting = h
+        return loss
+
+    loss = lax.fori_loop(0, rows // PADDED, group, jnp.zeros((8, PADDED), F32), unroll=2)
+    shape = (SLOT, QUANTS * 16)
     row = lax.broadcasted_iota(jnp.int32, shape, 0)
-    owner = jnp.minimum(lax.broadcasted_iota(jnp.int32, shape, 1) // 16, SLOT)
-    owner = jnp.where(owner >= QUANTS, SLOT, owner)
-    return dot_nn((row == owner).astype(F32).astype(BF), parts[...])
+    owner = lax.broadcasted_iota(jnp.int32, shape, 1) // 16
+    return dot_nn((row == owner).astype(F32).astype(BF), parts[...]), loss
 
 
 PARITY = 18
@@ -404,7 +409,7 @@
     return places
 
 
-SENT = (6, 6, 6, 4)
+SENT = (11, 11)
 
 
 def store_piece(outs, t, value):
@@ -437,9 +442,8 @@
         h_two[:, part] = relu(dot_tn(second[...], h_one[:, part]) + b_two)
     for part in tiles(rows, CRITIC_TILE):
         q[:, part] = dot_nn(head[0], h_two[:, part]) + head_bias[0, 0, :, :1]
-    terms = pair_terms(q, lagged, keep, parts, rows)
-    low = (terms[:SLOT] * -rows_scale).astype(BF)
-    loss = terms[SLOT : SLOT + 1]
+    terms, loss = pair_terms(q, lagged, keep, parts, rows)
+    low = (terms * -rows_scale).astype(BF)
     head_grad = dot_nt(low, h_two[...])
     count = jnp.ones((8, rows), BF)
     bias_grad = dot_nt(count, low)[:1]
@@ -494,7 +498,8 @@
             piece = pltpu.roll(jnp.broadcast_to(piece, (8, PADDED)), i * QUANTS, 1)[:1]
             inside = (lane >= i * QUANTS) & (lane < (i + 1) * QUANTS)
             bias_row = jnp.where(inside, piece, bias_row)
-        value = jnp.sum(before[2][...] + loss, axis=1, keepdims=True) * rows_scale
+        value = jnp.sum(before[2][...] + loss, axis=0, keepdims=True)
+        value = jnp.sum(value, axis=1, keepdims=True) * rows_scale
         value = jnp.broadcast_to(value, (1, PADDED))
         if direct:
             width = HIDDEN_SIZE // n_rows
@@ -544,7 +549,7 @@
         out_shape += [
             jax.ShapeDtypeStruct((CRITICS * SLOT, HIDDEN_SIZE), F32),
             jax.ShapeDtypeStruct((8, PADDED), F32),
-            jax.ShapeDtypeStruct((1, rows), F32),
+            jax.ShapeDtypeStruct((8, PADDED), F32),
         ]
     elif not split[0]:
         out_shape += [
@@ -562,7 +567,7 @@
             pltpu.VMEM((HIDDEN_SIZE, rows), BF),
             pltpu.VMEM((HIDDEN_SIZE, rows), BF),
             pltpu.VMEM((SLOT, rows), F32),
-            pltpu.VMEM((2 * QUANTS * 16, rows), BF),
+            pltpu.VMEM((QUANTS * 16, rows), BF),
             pltpu.VMEM((HIDDEN_SIZE // 16, 16, LANES), BF),
             pltpu.VMEM((136, HIDDEN_SIZE), F32),
             pltpu.VMEM((8, 16, LANES), BF),

time: 123 us -> 121 us (0.984)
  waiting for transfers between devices: 33.3 us -> 31.2 us
    ppermute x4, starting transfers between devices: 1.03 us -> 3.2 us  [exchange_sides(): lax.ppermute(value, AXES, [(i, i ^ (odd if i % 2 else even)) for i in ran...]
    ppermute x18 -> x16, starting transfers between devices: 14.5 us -> 12.4 us  [exchange(): return lax.ppermute(value, AXES, [(i, i ^ flip) for i in range(count)])]
    ppermute x18 -> x16, waiting for transfers between devices: 23.1 us -> 22 us  [exchange(): return lax.ppermute(value, AXES, [(i, i ^ flip) for i in range(count)])]
  transfers between devices with their start and end apart: 25 -> 23, of which waited for: 12 -> 12; matrix products, arithmetic and copies ran while one was open for 1% -> 1% of each run, Pallas kernels for 39% -> 39%
where the time goes in v3:
time: 121 us
  Pallas kernels  64.8 us (54%)
  waiting for transfers between devices  31.2 us (26%)
  starting transfers between devices  17.9 us (15%)
  between operations  3.91 us (3%)
  local copies, waits for them, and re-layouts  2.05 us (2%)
    pallas_call x5, Pallas kernels, critic_pass(): pl.pallas_call(functools.partial(critic_kernel, e, len(after), rows_scale...  35 us
    ppermute x16, waiting for transfers between devices, exchange(): return lax.ppermute(value, AXES, [(i, i ^ flip) for i in range(count)])  22 us
    pallas_call x1, Pallas kernels, pilot_pass(): pl.pallas_call(functools.partial(pilot_kernel, level, share), in_specs=[S...  14.7 us
    ppermute x16, starting transfers between devices, exchange(): return lax.ppermute(value, AXES, [(i, i ^ flip) for i in range(count)])  12.4 us
    pallas_call x1, Pallas kernels, target_pass(): pl.pallas_call(target_kernel, in_specs=[SCALAR] * 2 + [WHOLE] * 4 + [pl.B...  7.13 us
    ppermute x4, waiting for transfers between devices, exchange_sides(): lax.ppermute(value, AXES, [(i, i ^ (odd if i % 2 else even)) for i in ran...  6.89 us
    ppermute x4, starting transfers between devices, exchange_sides(): lax.ppermute(value, AXES, [(i, i ^ (odd if i % 2 else even)) for i in ran...  3.2 us
  transfers between devices with their start and end apart: 23, of which 12 were waited for; matrix products, arithmetic and copies ran while one was open for 1% of the time, Pallas kernels for 39%

profile of v3, /device:TPU:17, one launch (start us, length us, event | category | flops | bytes accessed | tf_op | source)
XLA Modules:
  0.0 120.6 jit_solution(88279352686653261)
XLA Ops:
  0.7 0.8 pad_maximum_fusion.own
  1.4 1.8 %collective-permute-start.2 = (bf16[32,1024]{1,0:T(8,128)(2,1)S(1)}, bf16[32,1024]{1,0:T(8,128)(2,1)S(1)}, u32[]{:S(2)}, u32[]{:S(2)}) collective-permute-start(bf16[32,1024]{1,0:T(8,128)(2,1)S(1)} %pad_maximum_fusion.own), channel_id=1, source_target_pairs={{0,3},{1,2},{2,1},{3,0},{4,7},{5,6},{6,5},{7,4},{8,11},{9,10},{10,... | collective-permute-start | bytes 196616 | tf_op jit(solution)/shard_map/ppermute | solution.py:866
  3.2 0.3 collective-permute-start.1
  3.5 0.2 collective-permute-start
  4.3 0.7 reshape.85.small
  5.0 1.1 collective-permute-done.2.got_three
  6.1 1.3 %collective-permute-done.1.got_two = bf16[32,1024]{1,0:T(8,128)(2,1)S(1)} collective-permute-done((bf16[32,1024]{1,0:T(8,128)(2,1)S(1)}, bf16[32,1024]{1,0:T(8,128)(2,1)S(1)}, u32[]{:S(2)}, u32[]{:S(2)}) %collective-permute-start.1) | collective-permute-done | bytes 65568 | tf_op jit(solution)/shard_map/ppermute | solution.py:866
  7.4 0.0 copy-start.28
  7.4 0.0 copy-start.29
  7.4 0.1 heads.1.head
  7.5 1.0 copy-done.25
  8.5 0.1 copy-done.26
  8.6 0.1 copy-done.27
  8.7 0.0 copy-done.28
  8.7 0.0 copy-start.30
  8.7 0.0 copy-start.32
  8.8 14.7 %pilot_pass.1 = (bf16[352,256]{1,0:T(8,128)(2,1)S(1)}, bf16[352,256]{1,0:T(8,128)(2,1)S(1)}, bf16[512,1024]{1,0:T(8,128)(2,1)S(1)}, bf16[512,1024]{1,0:T(8,128)(...) custom-call(s32[1]{0:T(128)} %bitcast.me.refs_1_, s32[1]{0:T(128)} %bitcast.1.me.index, f32[1]{0:T(128)} %copy.65.heat, ...), custom_call_target="tpu_custom_call" | custom-call | flops 14000000000 | bytes 9000000 | tf_op jit(solution)/shard_map/pilot_pass/pallas_call | solution.py:328
  23.4 0.6 collective-permute-start.3
  24.1 7.1 %target_pass.1 = (f32[128,1024]{1,0:T(8,128)S(1)}, bf16[128,1024]{1,0:T(8,128)(2,1)S(1)}) custom-call(s32[1]{0:T(128)} %bitcast.1.me.index, f32[1]{0:T(128)} %copy.65.heat, bf16[512,1024]{1,0:T(8,128)(2,1)S(1)} %get-tuple-element.92.inputs, f32[1,1024]{1,0:T(1,128)S(1)} %get-tuple-element.93.logp, f32[1,4096]{1,0:T(1,128)S(1)} %bitcast.53, ...), custom_call_target="tpu_custom_call" | custom-call | flops 7000000000 | bytes 7000000 | tf_op jit(solution)/shard_map/target_pass/pallas_call | solution.py:208
  31.3 1.3 %collective-permute-start.4 = (bf16[352,256]{1,0:T(8,128)(2,1)S(1)}, bf16[352,256]{1,0:T(8,128)(2,1)S(1)}, u32[]{:S(2)}, u32[]{:S(2)}) collective-permute-start(bf16[352,256]{1,0:T(8,128)(2,1)S(1)} %add_actor.5.a.refs_0_), channel_id=1, source_target_pairs={{0,2},{1,3},{2,0},{3,1},{4,6},{5,7},{6,4},{7,5},{8,10},{9,11},{10,... | collective-permute-start | bytes 540680 | tf_op jit(solution)/shard_map/ppermute | solution.py:816
  32.6 6.9 %critic_pass.5 = (bf16[18,16,1024]{2,1,0:T(8,128)(2,1)S(1)}, bf16[18,16,1024]{2,1,0:T(8,128)(2,1)S(1)}, f32[160,512]{1,0:T(8,128)S(1)}, f32[8,128]{1,0:T(8,128)S(1)}, f32[8,128]{1,0:T(8,128)S(1)}) custom-call(s32[1]{0:T(128)} %bitcast.me.refs_1_, bf16[512,1024]{1,0:T(8,128)(2,1)S(1)} %get-tuple-element.91.inputs, f32[128,1024]{1,0:T(8,128)S(1)} %get-tuple-element.95.lagged, ...), custom_call_target="tpu_custom_call" | custom-call | flops 7000000000 | bytes 4000000 | tf_op jit(solution)/shard_map/critic_pass/pallas_call | solution.py:559
  39.6 0.4 collective-permute-start.9
  40.0 1.3 %collective-permute-start.5 = (bf16[352,256]{1,0:T(8,128)(2,1)S(1)}, bf16[352,256]{1,0:T(8,128)(2,1)S(1)}, u32[]{:S(2)}, u32[]{:S(2)}) collective-permute-start(bf16[352,256]{1,0:T(8,128)(2,1)S(1)} %add_actor.6.a.refs_0_), channel_id=1, source_target_pairs={{0,4},{1,5},{2,6},{3,7},{4,0},{5,1},{6,2},{7,3},{8,12},{9,13},{10,... | collective-permute-start | bytes 540680 | tf_op jit(solution)/shard_map/ppermute | solution.py:816
  41.3 6.9 %critic_pass.6 = (bf16[18,16,1024]{2,1,0:T(8,128)(2,1)S(1)}, bf16[18,16,1024]{2,1,0:T(8,128)(2,1)S(1)}, f32[160,512]{1,0:T(8,128)S(1)}, f32[8,128]{1,0:T(8,128)S(1)}, f32[8,128]{1,0:T(8,128)S(1)}) custom-call(s32[1]{0:T(128)} %bitcast.me.refs_1_, bf16[512,1024]{1,0:T(8,128)(2,1)S(1)} %get-tuple-element.91.inputs, f32[128,1024]{1,0:T(8,128)S(1)} %get-tuple-element.95.lagged, ...), custom_call_target="tpu_custom_call" | custom-call | flops 7000000000 | bytes 4000000 | tf_op jit(solution)/shard_map/critic_pass/pallas_call | solution.py:559
  48.2 0.5 collective-permute-start.10
  48.8 1.4 %collective-permute-start.6 = (bf16[352,256]{1,0:T(8,128)(2,1)S(1)}, bf16[352,256]{1,0:T(8,128)(2,1)S(1)}, u32[]{:S(2)}, u32[]{:S(2)}) collective-permute-start(bf16[352,256]{1,0:T(8,128)(2,1)S(1)} %add_actor.7.a.refs_0_), channel_id=1, source_target_pairs={{0,8},{1,9},{2,10},{3,11},{4,12},{5,13},{6,14},{7,15},{8,0},{9,1},... | collective-permute-start | bytes 540680 | tf_op jit(solution)/shard_map/ppermute | solution.py:816
  50.2 7.1 %critic_pass.7 = (bf16[18,16,1024]{2,1,0:T(8,128)(2,1)S(1)}, bf16[18,16,1024]{2,1,0:T(8,128)(2,1)S(1)}, f32[160,512]{1,0:T(8,128)S(1)}, f32[8,128]{1,0:T(8,128)S(1)}, f32[8,128]{1,0:T(8,128)S(1)}) custom-call(s32[1]{0:T(128)} %bitcast.me.refs_1_, bf16[512,1024]{1,0:T(8,128)(2,1)S(1)} %get-tuple-element.91.inputs, f32[128,1024]{1,0:T(8,128)S(1)} %get-tuple-element.95.lagged, ...), custom_call_target="tpu_custom_call" | custom-call | flops 7000000000 | bytes 4000000 | tf_op jit(solution)/shard_map/critic_pass/pallas_call | solution.py:559
  57.3 0.4 collective-permute-start.11
  57.7 0.0 copy-start.16
  57.7 6.9 %critic_pass.8 = (bf16[18,16,1024]{2,1,0:T(8,128)(2,1)S(1)}, bf16[18,16,1024]{2,1,0:T(8,128)(2,1)S(1)}, f32[160,512]{1,0:T(8,128)S(1)}, f32[8,128]{1,0:T(8,128)S(1)}, f32[8,128]{1,0:T(8,128)S(1)}) custom-call(s32[1]{0:T(128)} %bitcast.me.refs_1_, bf16[512,1024]{1,0:T(8,128)(2,1)S(1)} %get-tuple-element.91.inputs, f32[128,1024]{1,0:T(8,128)S(1)} %get-tuple-element.95.lagged, ...), custom_call_target="tpu_custom_call" | custom-call | flops 7000000000 | bytes 4000000 | tf_op jit(solution)/shard_map/critic_pass/pallas_call | solution.py:559
  64.6 0.2 collective-permute-start.14
  64.9 0.8 add_core.2
  65.7 0.3 collective-permute-start.12
  66.0 7.2 %critic_pass.9 = (bf16[11,16,1024]{2,1,0:T(8,128)(2,1)S(1)}, bf16[11,16,1024]{2,1,0:T(8,128)(2,1)S(1)}, bf16[22,16,1024]{2,1,0:T(8,128)(2,1)S(1)}) custom-call(s32[1]{0:T(128)} %bitcast.me.refs_1_, bf16[512,1024]{1,0:T(8,128)(2,1)S(1)} %get-tuple-element.91.inputs, f32[128,1024]{1,0:T(8,128)S(1)} %get-tuple-element.95.lagged, ...), custom_call_target="tpu_custom_call" | custom-call | flops 7000000000 | bytes 4000000 | tf_op jit(solution)/shard_map/critic_pass/pallas_call | solution.py:559
  73.2 0.6 collective-permute-start.15
  73.9 0.1 collective-permute-start.16
  73.9 1.6 %collective-permute-done.12.refs_1_ = bf16[2,10,16,1024]{3,2,1,0:T(8,128)(2,1)S(1)} collective-permute-done((bf16[2,10,16,1024]{3,2,1,0:T(8,128)(2,1)S(1)}, bf16[2,10,16,1024]{3,2,1,0:T(8,128)(2,1)S(1)}, u32[]{:S(2)}, u32[]{:S(2)}) %collective-permute-start.12) | collective-permute-done | bytes 655392 | tf_op jit(solution)/shard_map/ppermute | solution.py:821
  75.5 0.1 add_half.2
  75.6 0.1 collective-permute-done.16.refs_7_
  75.7 0.9 add_core.3
  76.5 1.1 collective-permute-start.17
  77.6 0.5 collective-permute-start.13
  78.1 0.1 collective-permute-start.7
  78.2 8.0 %collective-permute-done.7.b = bf16[352,256]{1,0:T(8,128)(2,1)S(1)} collective-permute-done((bf16[352,256]{1,0:T(8,128)(2,1)S(1)}, bf16[352,256]{1,0:T(8,128)(2,1)S(1)}, u32[]{:S(2)}, u32[]{:S(2)}) %collective-permute-start.7) | collective-permute-done | bytes 180256 | tf_op jit(solution)/shard_map/ppermute | solution.py:816
  86.2 0.6 collective-permute-done.13.refs_1_.refs_3_
  86.8 3.7 %collective-permute-done.17.refs_3_ = bf16[2,11,16,1024]{3,2,1,0:T(8,128)(2,1)S(1)} collective-permute-done((bf16[2,11,16,1024]{3,2,1,0:T(8,128)(2,1)S(1)}, bf16[2,11,16,1024]{3,2,1,0:T(8,128)(2,1)S(1)}, u32[]{:S(2)}, u32[]{:S(2)}) %collective-permute-start.17) | collective-permute-done | bytes 720928 | tf_op jit(solution)/shard_map/ppermute | solution.py:821
  90.6 0.1 add_half.3
  90.8 1.3 %collective-permute-start.18 = (bf16[11,16,1024]{2,1,0:T(8,128)(2,1)S(1)}, bf16[11,16,1024]{2,1,0:T(8,128)(2,1)S(1)}, u32[]{:S(2)}, u32[]{:S(2)}) collective-permute-start(bf16[11,16,1024]{2,1,0:T(8,128)(2,1)S(1)} %get-tuple-element.127), channel_id=1, source_target_pairs={{0,4},{1,3},{2,6},{3,1},{4,0},{5,7},{6,2},{7,5},{8,12},{9,11},{10,... | collective-permute-start | bytes 1081352 | tf_op jit(solution)/shard_map/ppermute | solution.py:821
  92.1 0.9 collective-permute-start.8
  93.8 0.1 pad_maximum_fusion.1.factors
  93.9 0.2 collective-permute-done.8.peer
  94.1 2.4 %actor_update.1 = (f32[666,256]{1,0:T(8,128)}, f32[666,256]{1,0:T(8,128)}, f32[666,256]{1,0:T(8,128)}, f32[8,128]{1,0:T(8,128)S(1)}) custom-call(s32[1]{0:T(128)} %bitcast.me.refs_1_, f32[2]{0:T(128)S(1)} %pad_maximum_fusion.1.factors, bf16[352,256]{1,0:T(8,128)(2,1)S(1)} %add_actor.9.own.refs_0_, bf16[352,256]{1,0:T(8,128)(2,1)S(1)} %collective-permute-done.8.peer, ...), custom_call_target="tpu_custom_call" | custom-call | flops 2000000 | bytes 5000000 | tf_op jit(solution)/shard_map/actor_update/pallas_call | solution.py:770
  96.4 1.0 collective-permute-done.18.refs_5_
  97.4 0.3 add_line.1
  97.7 0.2 collective-permute-start.19
  97.9 0.1 collective-permute-start.20
  98.0 2.4 %collective-permute-start.21 = (bf16[5,16,1024]{2,1,0:T(8,128)(2,1)S(1)}, bf16[5,16,1024]{2,1,0:T(8,128)(2,1)S(1)}, u32[]{:S(2)}, u32[]{:S(2)}) collective-permute-start(bf16[5,16,1024]{2,1,0:T(8,128)(2,1)S(1)} %get-tuple-element.131), channel_id=1, source_target_pairs={{0,24},{1,25},{2,26},{3,27},{4,28},{5,29},{6,30},{7,31},{8,16},{9,... | collective-permute-start | bytes 491528 | tf_op jit(solution)/shard_map/ppermute | solution.py:816
  100.4 1.5 %collective-permute-done.19.refs_1_ = bf16[5,16,1024]{2,1,0:T(8,128)(2,1)S(1)} collective-permute-done((bf16[5,16,1024]{2,1,0:T(8,128)(2,1)S(1)}, bf16[5,16,1024]{2,1,0:T(8,128)(2,1)S(1)}, u32[]{:S(2)}, u32[]{:S(2)}) %collective-permute-start.19) | collective-permute-done | bytes 163872 | tf_op jit(solution)/shard_map/ppermute | solution.py:816
  101.9 2.5 %collective-permute-done.20.refs_2_ = bf16[5,16,1024]{2,1,0:T(8,128)(2,1)S(1)} collective-permute-done((bf16[5,16,1024]{2,1,0:T(8,128)(2,1)S(1)}, bf16[5,16,1024]{2,1,0:T(8,128)(2,1)S(1)}, u32[]{:S(2)}, u32[]{:S(2)}) %collective-permute-start.20) | collective-permute-done | bytes 163872 | tf_op jit(solution)/shard_map/ppermute | solution.py:816
  104.4 9.7 %collective-permute-done.21.refs_3_ = bf16[5,16,1024]{2,1,0:T(8,128)(2,1)S(1)} collective-permute-done((bf16[5,16,1024]{2,1,0:T(8,128)(2,1)S(1)}, bf16[5,16,1024]{2,1,0:T(8,128)(2,1)S(1)}, u32[]{:S(2)}, u32[]{:S(2)}) %collective-permute-start.21) | collective-permute-done | bytes 163872 | tf_op jit(solution)/shard_map/ppermute | solution.py:816
  114.1 0.1 sum_row.1.row_own
  114.3 1.9 %collective-permute-start.22 = (f32[8,128]{1,0:T(8,128)S(1)}, f32[8,128]{1,0:T(8,128)S(1)}, u32[]{:S(2)}, u32[]{:S(2)}) collective-permute-start(f32[8,128]{1,0:T(8,128)S(1)} %sum_row.1.row_own), channel_id=1, source_target_pairs={{0,1},{1,0},{2,3},{3,2},{4,5},{5,4},{6,7},{7,6},{8,9},{9,8},{10,11... | collective-permute-start | bytes 12296 | tf_op jit(solution)/shard_map/ppermute | solution.py:816
  117.6 1.8 %update.1 = (f32[80,393]{1,0:T(8,128)}, f32[80,393]{1,0:T(8,128)}, f32[80,393]{1,0:T(8,128)}, f32[80,512]{1,0:T(8,128)}, f32[80,512]{1,0:T(8,128)}, /*index=5*/f...) custom-call(f32[2]{0:T(128)S(1)} %pad_maximum_fusion.1.factors, ...), custom_call_target="tpu_custom_call" | custom-call | flops 2000000 | bytes 6000000 | tf_op jit(solution)/shard_map/update/pallas_call | solution.py:747
  119.4 1.2 %small_update.1 = (f32[1,1]{1,0:T(1,128)}, f32[674]{0:T(1024)}, f32[674]{0:T(1024)}, f32[674]{0:T(1024)}, f32[1,1]{1,0:T(1,128)}, /*index=5*/f32[1,1]{1,0:T(1,128)}, f32[1,1]{1,0:T(1,128)}) custom-call(s32[1]{0:T(128)} %bitcast.me.refs_1_, f32[2]{0:T(128)S(1)} %pad_maximum_fusion.1.factors, f32[8,128]{1,0:T(8,128)S(1)} %sum_row.1.row_own, ...), custom_call_target="tpu_custom_call" | custom-call | flops 1000000 | bytes 100000 | tf_op jit(solution)/shard_map/small_update/pallas_call | solution.py:802
  (77 shorter events, 0.4 us)
Async XLA Ops:
  1.4 4.6 %collective-permute-start.2 = (bf16[32,1024]{1,0:T(8,128)(2,1)S(1)}, bf16[32,1024]{1,0:T(8,128)(2,1)S(1)}, u32[]{:S(2)}, u32[]{:S(2)}) collective-permute-start(bf16[32,1024]{1,0:T(8,128)(2,1)S(1)} %pad_maximum_fusion.own), channel_id=1, source_target_pairs={{0,3},{1,2},{2,1},{3,0},{4,7},{5,6},{6,5},{7,4},{8,11},{9,10},{10,... | collective-permute-start | bytes 196616 | tf_op jit(solution)/shard_map/ppermute | solution.py:866
  3.2 4.1 %collective-permute-start.1 = (bf16[32,1024]{1,0:T(8,128)(2,1)S(1)}, bf16[32,1024]{1,0:T(8,128)(2,1)S(1)}, u32[]{:S(2)}, u32[]{:S(2)}) collective-permute-start(bf16[32,1024]{1,0:T(8,128)(2,1)S(1)} %pad_maximum_fusion.own), channel_id=1, source_target_pairs={{0,2},{1,3},{2,0},{3,1},{4,6},{5,7},{6,4},{7,5},{8,10},{9,11},{10,... | collective-permute-start | bytes 196616 | tf_op jit(solution)/shard_map/ppermute | solution.py:866
  3.5 3.9 %collective-permute-start = (bf16[32,1024]{1,0:T(8,128)(2,1)S(1)}, bf16[32,1024]{1,0:T(8,128)(2,1)S(1)}, u32[]{:S(2)}, u32[]{:S(2)}) collective-permute-start(bf16[32,1024]{1,0:T(8,128)(2,1)S(1)} %pad_maximum_fusion.own), channel_id=1, source_target_pairs={{0,1},{1,0},{2,3},{3,2},{4,5},{5,4},{6,7},{7,6},{8,9},{9,8},{10,11... | collective-permute-start | bytes 196616 | tf_op jit(solution)/shard_map/ppermute | solution.py:866
  7.4 1.1 copy-start.25
  7.4 1.2 %copy-start.26 = (f32[4096,17]{0,1:T(8,128)S(1)}, f32[4096,17]{0,1:T(8,128)}, u32[]{:S(2)}) copy-start(f32[4096,17]{0,1:T(8,128)} %param.46) | copy-start | bytes 835588
  7.4 1.3 %copy-start.27 = (bf16[666,256]{1,0:T(8,128)(2,1)S(1)}, bf16[666,256]{1,0:T(8,128)(2,1)}, u32[]{:S(2)}) copy-start(bf16[666,256]{1,0:T(8,128)(2,1)} %actor.1) | copy-start | bytes 1022980
  7.4 1.3 %copy-start.28 = (f32[1024,17]{0,1:T(8,128)S(1)}, f32[1024,17]{0,1:T(8,128)}, u32[]{:S(2)}) copy-start(f32[1024,17]{0,1:T(8,128)} %param.44) | copy-start | bytes 208900
  7.4 1.3 %copy-start.29 = (bf16[1024,17]{0,1:T(8,128)(2,1)S(1)}, bf16[1024,17]{0,1:T(8,128)(2,1)}, u32[]{:S(2)}) copy-start(bf16[1024,17]{0,1:T(8,128)(2,1)} %param.43) | copy-start | bytes 104452
  7.4 1.3 %copy-start.31 = (f32[2,2560]{1,0:T(2,128)S(1)}, f32[2,2560]{1,0:T(2,128)}, u32[]{:S(2)}) copy-start(f32[2,2560]{1,0:T(2,128)} %bias.13) | copy-start | bytes 61444
  7.4 1.3 %copy-start.34 = (f32[128]{0:T(128)S(1)}, f32[128]{0:T(128)}, u32[]{:S(2)}) copy-start(f32[128]{0:T(128)} %param.58) | copy-start | bytes 1540
  8.7 15.4 %copy-start.20 = (bf16[512,2560]{1,0:T(8,128)(2,1)S(1)}, bf16[512,2560]{1,0:T(8,128)(2,1)}, u32[]{:S(2)}) copy-start(bf16[512,2560]{1,0:T(8,128)(2,1)} %second.6) | copy-start | bytes 7864324
  8.7 15.4 %copy-start.22 = (s32[4096,125]{1,0:T(8,128)S(1)}, s32[4096,125]{1,0:T(8,128)}, u32[]{:S(2)}) copy-start(s32[4096,125]{1,0:T(8,128)} %order_in.1) | copy-start | bytes 6144004
  8.7 15.4 %copy-start.23 = (bf16[393,2560]{1,0:T(8,128)(2,1)S(1)}, bf16[393,2560]{1,0:T(8,128)(2,1)}, u32[]{:S(2)}) copy-start(bf16[393,2560]{1,0:T(8,128)(2,1)} %first.6) | copy-start | bytes 6036484
  8.7 15.4 %copy-start.30 = (f32[2,2560]{1,0:T(2,128)S(1)}, f32[2,2560]{1,0:T(2,128)}, u32[]{:S(2)}) copy-start(f32[2,2560]{1,0:T(2,128)} %bias.8) | copy-start | bytes 61444
  8.7 15.3 %copy-start.32 = (f32[4096]{0:T(1024)S(1)}, f32[4096]{0:T(1024)}, u32[]{:S(2)}) copy-start(f32[4096]{0:T(1024)} %param.47) | copy-start | bytes 49156
  8.8 15.3 %copy-start.33 = (s32[4096]{0:T(1024)S(1)}, s32[4096]{0:T(1024)}, u32[]{:S(2)}) copy-start(s32[4096]{0:T(1024)} %param.48) | copy-start | bytes 49156
  23.4 7.8 %collective-permute-start.3 = (bf16[352,256]{1,0:T(8,128)(2,1)S(1)}, bf16[352,256]{1,0:T(8,128)(2,1)S(1)}, u32[]{:S(2)}, u32[]{:S(2)}) collective-permute-start(bf16[352,256]{1,0:T(8,128)(2,1)S(1)} %get-tuple-element.89), channel_id=1, source_target_pairs={{0,1},{1,0},{2,3},{3,2},{4,5},{5,4},{6,7},{7,6},{8,9},{9,8},{10,11... | collective-permute-start | bytes 540680 | tf_op jit(solution)/shard_map/ppermute | solution.py:816
  24.1 8.5 %copy-start.21 = (bf16[512,2560]{1,0:T(8,128)(2,1)S(1)}, bf16[512,2560]{1,0:T(8,128)(2,1)}, u32[]{:S(2)}) copy-start(bf16[512,2560]{1,0:T(8,128)(2,1)} %second.11) | copy-start | bytes 7864324
  24.1 8.5 %copy-start.24 = (bf16[393,2560]{1,0:T(8,128)(2,1)S(1)}, bf16[393,2560]{1,0:T(8,128)(2,1)}, u32[]{:S(2)}) copy-start(bf16[393,2560]{1,0:T(8,128)(2,1)} %first.11) | copy-start | bytes 6036484
  31.3 8.7 %collective-permute-start.4 = (bf16[352,256]{1,0:T(8,128)(2,1)S(1)}, bf16[352,256]{1,0:T(8,128)(2,1)S(1)}, u32[]{:S(2)}, u32[]{:S(2)}) collective-permute-start(bf16[352,256]{1,0:T(8,128)(2,1)S(1)} %add_actor.5.a.refs_0_), channel_id=1, source_target_pairs={{0,2},{1,3},{2,0},{3,1},{4,6},{5,7},{6,4},{7,5},{8,10},{9,11},{10,... | collective-permute-start | bytes 540680 | tf_op jit(solution)/shard_map/ppermute | solution.py:816
  39.6 25.3 %collective-permute-start.9 = (bf16[18,16,1024]{2,1,0:T(8,128)(2,1)S(1)}, bf16[18,16,1024]{2,1,0:T(8,128)(2,1)S(1)}, u32[]{:S(2)}, u32[]{:S(2)}) collective-permute-start(bf16[18,16,1024]{2,1,0:T(8,128)(2,1)S(1)} %get-tuple-element.106), channel_id=1, source_target_pairs={{0,1},{1,0},{2,3},{3,2},{4,5},{5,4},{6,7},{7,6},{8,9},{9,8},{10,11... | collective-permute-start | bytes 1769480 | tf_op jit(solution)/shard_map/ppermute | solution.py:816
  40.0 8.7 %collective-permute-start.5 = (bf16[352,256]{1,0:T(8,128)(2,1)S(1)}, bf16[352,256]{1,0:T(8,128)(2,1)S(1)}, u32[]{:S(2)}, u32[]{:S(2)}) collective-permute-start(bf16[352,256]{1,0:T(8,128)(2,1)S(1)} %add_actor.6.a.refs_0_), channel_id=1, source_target_pairs={{0,4},{1,5},{2,6},{3,7},{4,0},{5,1},{6,2},{7,3},{8,12},{9,13},{10,... | collective-permute-start | bytes 540680 | tf_op jit(solution)/shard_map/ppermute | solution.py:816
  48.2 16.7 %collective-permute-start.10 = (bf16[18,16,1024]{2,1,0:T(8,128)(2,1)S(1)}, bf16[18,16,1024]{2,1,0:T(8,128)(2,1)S(1)}, u32[]{:S(2)}, u32[]{:S(2)}) collective-permute-start(bf16[18,16,1024]{2,1,0:T(8,128)(2,1)S(1)} %get-tuple-element.107), channel_id=1, source_target_pairs={{0,1},{1,0},{2,3},{3,2},{4,5},{5,4},{6,7},{7,6},{8,9},{9,8},{10,11... | collective-permute-start | bytes 1769480 | tf_op jit(solution)/shard_map/ppermute | solution.py:816
  48.8 8.9 %collective-permute-start.6 = (bf16[352,256]{1,0:T(8,128)(2,1)S(1)}, bf16[352,256]{1,0:T(8,128)(2,1)S(1)}, u32[]{:S(2)}, u32[]{:S(2)}) collective-permute-start(bf16[352,256]{1,0:T(8,128)(2,1)S(1)} %add_actor.7.a.refs_0_), channel_id=1, source_target_pairs={{0,8},{1,9},{2,10},{3,11},{4,12},{5,13},{6,14},{7,15},{8,0},{9,1},... | collective-permute-start | bytes 540680 | tf_op jit(solution)/shard_map/ppermute | solution.py:816
  57.3 7.6 %collective-permute-start.11 = (bf16[18,16,1024]{2,1,0:T(8,128)(2,1)S(1)}, bf16[18,16,1024]{2,1,0:T(8,128)(2,1)S(1)}, u32[]{:S(2)}, u32[]{:S(2)}) collective-permute-start(bf16[18,16,1024]{2,1,0:T(8,128)(2,1)S(1)} %get-tuple-element.108), channel_id=1, source_target_pairs={{0,1},{1,0},{2,3},{3,2},{4,5},{5,4},{6,7},{7,6},{8,9},{9,8},{10,11... | collective-permute-start | bytes 1769480 | tf_op jit(solution)/shard_map/ppermute | solution.py:816
  57.7 7.2 %copy-start.16 = (s32[160]{0:T(256)S(1)}, s32[160]{0:T(256)}, u32[]{:S(2)}) copy-start(s32[160]{0:T(256)} %constant.21.clone.places) | copy-start | bytes 1924
  64.6 11.0 %collective-permute-start.14 = (bf16[18,16,1024]{2,1,0:T(8,128)(2,1)S(1)}, bf16[18,16,1024]{2,1,0:T(8,128)(2,1)S(1)}, u32[]{:S(2)}, u32[]{:S(2)}) collective-permute-start(bf16[18,16,1024]{2,1,0:T(8,128)(2,1)S(1)} %get-tuple-element.121), channel_id=1, source_target_pairs={{0,1},{1,0},{2,3},{3,2},{4,5},{5,4},{6,7},{7,6},{8,9},{9,8},{10,11... | collective-permute-start | bytes 1769480 | tf_op jit(solution)/shard_map/ppermute | solution.py:816
  65.7 9.8 %collective-permute-start.12 = (bf16[2,10,16,1024]{3,2,1,0:T(8,128)(2,1)S(1)}, bf16[2,10,16,1024]{3,2,1,0:T(8,128)(2,1)S(1)}, u32[]{:S(2)}, u32[]{:S(2)}) collective-permute-start(bf16[2,10,16,1024]{3,2,1,0:T(8,128)(2,1)S(1)} %get-tuple-element.110), channel_id=1, source_target_pairs={{0,2},{1,5},{2,0},{3,7},{4,6},{5,1},{6,4},{7,3},{8,10},{9,13},{10,... | collective-permute-start | bytes 1966088 | tf_op jit(solution)/shard_map/ppermute | solution.py:821
  66.0 9.7 %copy-start.15 = (s32[160]{0:T(256)S(1)}, s32[160]{0:T(256)}, u32[]{:S(2)}) copy-start(s32[160]{0:T(256)} %constant.22.clone.places) | copy-start | bytes 1924
  73.2 2.4 %collective-permute-start.15 = (bf16[11,16,1024]{2,1,0:T(8,128)(2,1)S(1)}, bf16[11,16,1024]{2,1,0:T(8,128)(2,1)S(1)}, u32[]{:S(2)}, u32[]{:S(2)}) collective-permute-start(bf16[11,16,1024]{2,1,0:T(8,128)(2,1)S(1)} %get-tuple-element.122), channel_id=1, source_target_pairs={{0,1},{1,0},{2,3},{3,2},{4,5},{5,4},{6,7},{7,6},{8,9},{9,8},{10,11... | collective-permute-start | bytes 1081352 | tf_op jit(solution)/shard_map/ppermute | solution.py:816
  73.9 1.8 %collective-permute-start.16 = (bf16[11,16,1024]{2,1,0:T(8,128)(2,1)S(1)}, bf16[11,16,1024]{2,1,0:T(8,128)(2,1)S(1)}, u32[]{:S(2)}, u32[]{:S(2)}) collective-permute-start(bf16[11,16,1024]{2,1,0:T(8,128)(2,1)S(1)} %get-tuple-element.123), channel_id=1, source_target_pairs={{0,1},{1,0},{2,3},{3,2},{4,5},{5,4},{6,7},{7,6},{8,9},{9,8},{10,11... | collective-permute-start | bytes 1081352 | tf_op jit(solution)/shard_map/ppermute | solution.py:816
  75.7 18.4 %copy-start = (f32[666,256]{1,0:T(8,128)S(1)}, f32[666,256]{1,0:T(8,128)}, u32[]{:S(2)}) copy-start(f32[666,256]{1,0:T(8,128)} %refs_0_.2) | copy-start | bytes 2045956
  75.7 18.4 %copy-start.1 = (f32[666,256]{1,0:T(8,128)S(1)}, f32[666,256]{1,0:T(8,128)}, u32[]{:S(2)}) copy-start(f32[666,256]{1,0:T(8,128)} %refs_1_.2) | copy-start | bytes 2045956
  75.7 18.4 %copy-start.2 = (f32[666,256]{1,0:T(8,128)S(1)}, f32[666,256]{1,0:T(8,128)}, u32[]{:S(2)}) copy-start(f32[666,256]{1,0:T(8,128)} %refs_2_.2) | copy-start | bytes 2045956
  76.5 14.0 %collective-permute-start.17 = (bf16[2,11,16,1024]{3,2,1,0:T(8,128)(2,1)S(1)}, bf16[2,11,16,1024]{3,2,1,0:T(8,128)(2,1)S(1)}, u32[]{:S(2)}, u32[]{:S(2)}) collective-permute-start(bf16[2,11,16,1024]{3,2,1,0:T(8,128)(2,1)S(1)} %get-tuple-element.125), channel_id=1, source_target_pairs={{0,2},{1,5},{2,0},{3,7},{4,6},{5,1},{6,4},{7,3},{8,10},{9,13},{10,... | collective-permute-start | bytes 2162696 | tf_op jit(solution)/shard_map/ppermute | solution.py:821
  77.6 9.2 %collective-permute-start.13 = (bf16[10,16,1024]{2,1,0:T(8,128)(2,1)S(1)}, bf16[10,16,1024]{2,1,0:T(8,128)(2,1)S(1)}, u32[]{:S(2)}, u32[]{:S(2)}) collective-permute-start(bf16[10,16,1024]{2,1,0:T(8,128)(2,1)S(1)} %get-tuple-element.112), channel_id=1, source_target_pairs={{0,4},{1,3},{2,6},{3,1},{4,0},{5,7},{6,2},{7,5},{8,12},{9,11},{10,... | collective-permute-start | bytes 983048 | tf_op jit(solution)/shard_map/ppermute | solution.py:821
  78.1 8.1 %collective-permute-start.7 = (bf16[352,256]{1,0:T(8,128)(2,1)S(1)}, bf16[352,256]{1,0:T(8,128)(2,1)S(1)}, u32[]{:S(2)}, u32[]{:S(2)}) collective-permute-start(bf16[352,256]{1,0:T(8,128)(2,1)S(1)} %add_actor.8.a.refs_0_), channel_id=1, source_target_pairs={{0,16},{1,17},{2,18},{3,19},{4,20},{5,21},{6,22},{7,23},{8,24},{9,... | collective-permute-start | bytes 540680 | tf_op jit(solution)/shard_map/ppermute | solution.py:816
  90.6 26.8 %copy-start.3 = (f32[393,80]{0,1:T(8,128)S(1)}, f32[393,80]{0,1:T(8,128)}, u32[]{:S(2)}) copy-start(f32[393,80]{0,1:T(8,128)} %param.61) | copy-start | bytes 377284
  90.7 26.8 %copy-start.4 = (f32[393,80]{0,1:T(8,128)S(1)}, f32[393,80]{0,1:T(8,128)}, u32[]{:S(2)}) copy-start(f32[393,80]{0,1:T(8,128)} %param.62) | copy-start | bytes 377284
  90.7 26.8 %copy-start.5 = (f32[393,80]{0,1:T(8,128)S(1)}, f32[393,80]{0,1:T(8,128)}, u32[]{:S(2)}) copy-start(f32[393,80]{0,1:T(8,128)} %param.63) | copy-start | bytes 377284
  90.7 26.8 %copy-start.6 = (f32[512,80]{0,1:T(8,128)S(1)}, f32[512,80]{0,1:T(8,128)}, u32[]{:S(2)}) copy-start(f32[512,80]{0,1:T(8,128)} %param.64) | copy-start | bytes 491524
  90.7 26.8 %copy-start.7 = (f32[512,80]{0,1:T(8,128)S(1)}, f32[512,80]{0,1:T(8,128)}, u32[]{:S(2)}) copy-start(f32[512,80]{0,1:T(8,128)} %param.65) | copy-start | bytes 491524
  90.7 26.8 %copy-start.8 = (f32[512,80]{0,1:T(8,128)S(1)}, f32[512,80]{0,1:T(8,128)}, u32[]{:S(2)}) copy-start(f32[512,80]{0,1:T(8,128)} %param.66) | copy-start | bytes 491524
  90.7 26.8 %copy-start.9 = (f32[64,32]{0,1:T(8,128)S(1)}, f32[64,32]{0,1:T(8,128)}, u32[]{:S(2)}) copy-start(f32[64,32]{0,1:T(8,128)} %param.70) | copy-start | bytes 24580
  90.7 26.8 %copy-start.10 = (f32[64,32]{0,1:T(8,128)S(1)}, f32[64,32]{0,1:T(8,128)}, u32[]{:S(2)}) copy-start(f32[64,32]{0,1:T(8,128)} %param.71) | copy-start | bytes 24580
  90.7 26.8 %copy-start.11 = (f32[64,32]{0,1:T(8,128)S(1)}, f32[64,32]{0,1:T(8,128)}, u32[]{:S(2)}) copy-start(f32[64,32]{0,1:T(8,128)} %param.72) | copy-start | bytes 24580
  90.8 26.8 %copy-start.17 = (f32[2,80]{1,0:T(2,128)S(1)}, f32[2,80]{1,0:T(2,128)}, u32[]{:S(2)}) copy-start(f32[2,80]{1,0:T(2,128)} %refs_10_.1) | copy-start | bytes 1924
  90.8 26.8 %copy-start.18 = (f32[2,80]{1,0:T(2,128)S(1)}, f32[2,80]{1,0:T(2,128)}, u32[]{:S(2)}) copy-start(f32[2,80]{1,0:T(2,128)} %refs_11_.1) | copy-start | bytes 1924
  90.8 26.8 %copy-start.19 = (f32[2,80]{1,0:T(2,128)S(1)}, f32[2,80]{1,0:T(2,128)}, u32[]{:S(2)}) copy-start(f32[2,80]{1,0:T(2,128)} %refs_12_.1) | copy-start | bytes 1924
  90.8 6.6 %collective-permute-start.18 = (bf16[11,16,1024]{2,1,0:T(8,128)(2,1)S(1)}, bf16[11,16,1024]{2,1,0:T(8,128)(2,1)S(1)}, u32[]{:S(2)}, u32[]{:S(2)}) collective-permute-start(bf16[11,16,1024]{2,1,0:T(8,128)(2,1)S(1)} %get-tuple-element.127), channel_id=1, source_target_pairs={{0,4},{1,3},{2,6},{3,1},{4,0},{5,7},{6,2},{7,5},{8,12},{9,11},{10,... | collective-permute-start | bytes 1081352 | tf_op jit(solution)/shard_map/ppermute | solution.py:821
  92.1 1.9 %collective-permute-start.8 = (bf16[352,256]{1,0:T(8,128)(2,1)S(1)}, bf16[352,256]{1,0:T(8,128)(2,1)S(1)}, u32[]{:S(2)}, u32[]{:S(2)}) collective-permute-start(bf16[352,256]{1,0:T(8,128)(2,1)S(1)} %add_actor.9.own.refs_0_), channel_id=1, source_target_pairs={{0,1},{1,0},{2,3},{3,2},{4,5},{5,4},{6,7},{7,6},{8,9},{9,8},{10,11... | collective-permute-start | bytes 540680 | tf_op jit(solution)/shard_map/ppermute | solution.py:816
  93.9 25.5 %copy-start.12 = (f32[674]{0:T(1024)S(1)}, f32[674]{0:T(1024)}, u32[]{:S(2)}) copy-start(f32[674]{0:T(1024)} %refs_0_.3) | copy-start | bytes 8092
  93.9 25.5 %copy-start.13 = (f32[674]{0:T(1024)S(1)}, f32[674]{0:T(1024)}, u32[]{:S(2)}) copy-start(f32[674]{0:T(1024)} %refs_1_.3) | copy-start | bytes 8092
  93.9 25.5 %copy-start.14 = (f32[674]{0:T(1024)S(1)}, f32[674]{0:T(1024)}, u32[]{:S(2)}) copy-start(f32[674]{0:T(1024)} %refs_2_.3) | copy-start | bytes 8092
  97.7 4.2 %collective-permute-start.19 = (bf16[5,16,1024]{2,1,0:T(8,128)(2,1)S(1)}, bf16[5,16,1024]{2,1,0:T(8,128)(2,1)S(1)}, u32[]{:S(2)}, u32[]{:S(2)}) collective-permute-start(bf16[5,16,1024]{2,1,0:T(8,128)(2,1)S(1)} %get-tuple-element.129), channel_id=1, source_target_pairs={{0,8},{1,9},{2,10},{3,11},{4,12},{5,13},{6,14},{7,15},{8,0},{9,1},... | collective-permute-start | bytes 491528 | tf_op jit(solution)/shard_map/ppermute | solution.py:816
  97.9 6.5 %collective-permute-start.20 = (bf16[5,16,1024]{2,1,0:T(8,128)(2,1)S(1)}, bf16[5,16,1024]{2,1,0:T(8,128)(2,1)S(1)}, u32[]{:S(2)}, u32[]{:S(2)}) collective-permute-start(bf16[5,16,1024]{2,1,0:T(8,128)(2,1)S(1)} %get-tuple-element.130), channel_id=1, source_target_pairs={{0,16},{1,17},{2,18},{3,19},{4,20},{5,21},{6,22},{7,23},{8,24},{9,... | collective-permute-start | bytes 491528 | tf_op jit(solution)/shard_map/ppermute | solution.py:816
  98.0 16.1 %collective-permute-start.21 = (bf16[5,16,1024]{2,1,0:T(8,128)(2,1)S(1)}, bf16[5,16,1024]{2,1,0:T(8,128)(2,1)S(1)}, u32[]{:S(2)}, u32[]{:S(2)}) collective-permute-start(bf16[5,16,1024]{2,1,0:T(8,128)(2,1)S(1)} %get-tuple-element.131), channel_id=1, source_target_pairs={{0,24},{1,25},{2,26},{3,27},{4,28},{5,29},{6,30},{7,31},{8,16},{9,... | collective-permute-start | bytes 491528 | tf_op jit(solution)/shard_map/ppermute | solution.py:816
  114.3 5.1 %collective-permute-start.22 = (f32[8,128]{1,0:T(8,128)S(1)}, f32[8,128]{1,0:T(8,128)S(1)}, u32[]{:S(2)}, u32[]{:S(2)}) collective-permute-start(f32[8,128]{1,0:T(8,128)S(1)} %sum_row.1.row_own), channel_id=1, source_target_pairs={{0,1},{1,0},{2,3},{3,2},{4,5},{5,4},{6,7},{7,6},{8,9},{9,8},{10,11... | collective-permute-start | bytes 12296 | tf_op jit(solution)/shard_map/ppermute | solution.py:816
